TPU v7x, 256 devices: a whole 4x4x8 slice. The times are simulated.
256 devices in a mesh: dp: 32 (over z, y), tp: 8 (over x, core).
Axes of the slice: x: 4, y: 4, z: 8, core: 2. Of those that a mesh axis runs over, the one named last changes fastest.
Arguments:
- prefill_latent: bfloat16 [16384, 576], P('dp'), may hold values from -5 to 5
- request_slot: int32 [128], replicated, may hold values from 0 to 127, each once
- new_lengths: int32 [32, 4], replicated, may hold values from 1 to 8, 16 in all within a row
- ctx_lengths: int32 [128], P('dp'), may hold values from 1 to 1024, 65536 in all
- kv_cache: bfloat16 [128, 1024, 576], P('dp'), may hold values from -5 to 5
- queries: bfloat16 [2, 128, 128, 576], P(None, 'dp', 'tp'), may hold values from -48 to 48
- step_latents: bfloat16 [2, 128, 576], P(None, 'dp'), may hold values from -5 to 5
- w_uv: bfloat16 [128, 512, 128], P('tp'), may hold values from -0.25 to 0.25
- w_out: bfloat16 [128, 128, 7168], P('tp', None, 'dp'), may hold values from -0.09375 to 0.09375
- hidden: bfloat16 [2, 128, 7168], P(None, None, ('dp', 'tp')), may hold values from -2 to 2
- ffn_gain: float32 [7168], replicated, may hold values from 0.5 to 1.5
- w_gate: bfloat16 [7168, 18432], P(None, ('dp', 'tp')), may hold values from -0.0625 to 0.0625
- w_up: bfloat16 [7168, 18432], P(None, ('dp', 'tp')), may hold values from -0.0625 to 0.0625
- w_down: bfloat16 [18432, 7168], P(('dp', 'tp')), may hold values from -0.1875 to 0.1875
Outputs:
- layer_out: bfloat16 [2, 128, 7168], P(None, None, ('dp', 'tp'))
Inputs may be any that keep to these rules, and one draw needn't show every extreme that they name: A permutation of the 128 requests; the owner of request r is request_slot[r] // 4. `new_lengths`: row j lists the 4 requests of owner j; each row sums to 16, and its largest entry is 8. `ctx_lengths`: sums to 65536; the largest is 1024.
All inputs are finite; a program needn't handle non-finite values. No bound on the sum of `ctx_lengths` on one device may be relied on, other than what follows from the above.
Results may differ from a plain program's by a relative error of at most 0.02.
Values may be sent and summed in bfloat16 or wider, within the bound.
No kernel may reach another device: no remote copies, remote signals or barrier semaphores. Data moves between devices by JAX's collectives and lax.ppermute only.
A program may use at most 128 MiB of HBM per device.

v0:
```python
import jax
import jax.numpy as jnp
from jax import lax
from jax.sharding import PartitionSpec as P

LAT = 512
QKD = 192
OWN_TOK = 16


masked_score = -1e30
norm_eps = 1e-06


def attend(query, step_ids, kv_cache, cache_mask, new_rows, new_mask, step_latents, w_uv):
    score_scale = QKD ** (-0.5)
    cache_scores = (
        jnp.einsum("sqhc,qkc->sqhk", query, kv_cache, preferred_element_type=jnp.float32)
        * score_scale
    )
    cache_scores = jnp.where(cache_mask[None, :, None, :], cache_scores, masked_score)
    fresh_scores = (
        jnp.einsum("sqhc,kc->sqhk", query, new_rows, preferred_element_type=jnp.float32)
        * score_scale
    )
    fresh_scores = jnp.where(new_mask[None, :, None, :], fresh_scores, masked_score)
    token_scores = (
        jnp.einsum("sqhc,tqc->sqht", query, step_latents, preferred_element_type=jnp.float32)
        * score_scale
    )
    token_valid = jnp.arange(step_latents.shape[0], dtype=jnp.int32)[None, :] <= step_ids[:, None]
    token_scores = jnp.where(token_valid[:, None, None, :], token_scores, masked_score)
    highest = jnp.maximum(
        jnp.maximum(jnp.max(cache_scores, axis=-1), jnp.max(fresh_scores, axis=-1)),
        jnp.max(token_scores, axis=-1),
    )[..., None]
    cache_exp = jnp.exp(cache_scores - highest)
    fresh_exp = jnp.exp(fresh_scores - highest)
    token_exp = jnp.exp(token_scores - highest)
    totals = (
        jnp.sum(cache_exp, axis=-1, keepdims=True)
        + jnp.sum(fresh_exp, axis=-1, keepdims=True)
        + jnp.sum(token_exp, axis=-1, keepdims=True)
    )
    cache_probs = (cache_exp / totals).astype(jnp.bfloat16)
    fresh_probs = (fresh_exp / totals).astype(jnp.bfloat16)
    token_probs = (token_exp / totals).astype(jnp.bfloat16)
    latent_out = jnp.einsum(
        "sqhk,qkc->sqhc", cache_probs, kv_cache[:, :, :LAT], preferred_element_type=jnp.float32
    )
    latent_out = latent_out + jnp.einsum(
        "sqhk,kc->sqhc", fresh_probs, new_rows[:, :LAT], preferred_element_type=jnp.float32
    )
    latent_out = latent_out + jnp.einsum(
        "sqht,tqc->sqhc", token_probs, step_latents[:, :, :LAT], preferred_element_type=jnp.float32
    )
    latent_out = latent_out.astype(jnp.bfloat16)
    return jnp.einsum(
        "sqhc,hcv->sqhv", latent_out, w_uv, preferred_element_type=jnp.float32
    ).astype(jnp.bfloat16)


def shards(
    prefill_latent,
    request_slot,
    new_lengths,
    ctx_lengths,
    kv_cache,
    queries,
    step_latents,
    w_uv,
    w_out,
    hidden,
    ffn_gain,
    w_gate,
    w_up,
    w_down,
):
    dp_count = lax.axis_size("dp")
    dp_rank = lax.axis_index("dp")
    tp_rank = lax.axis_index("tp")
    per_owner = new_lengths.shape[1]
    total_requests = request_slot.shape[0]
    latent_width = kv_cache.shape[2]
    share_width = hidden.shape[2]
    block_width = w_out.shape[2]
    model_width = block_width * dp_count
    numbers = jnp.arange(total_requests, dtype=jnp.int32)
    one_hot = request_slot[:, None] == numbers[None, :]
    lengths_flat = new_lengths.reshape(-1)
    request_rows = jnp.sum(jnp.where(one_hot, lengths_flat[None, :], 0), axis=1)
    offsets = jnp.cumsum(request_rows) - request_rows
    inverse = jnp.sum(jnp.where(one_hot, numbers[:, None], 0), axis=0)
    slot_start = jnp.cumsum(new_lengths, axis=1) - new_lengths
    positions = jnp.arange(OWN_TOK, dtype=jnp.int32)
    slot_of_place = (
        jnp.sum((slot_start[:, :, None] <= positions[None, None, :]).astype(jnp.int32), axis=1) - 1
    )
    owner_ids = jnp.arange(dp_count, dtype=jnp.int32)[:, None]
    owner_rows = owner_ids * per_owner + slot_of_place
    start_in_slot = jnp.take_along_axis(slot_start, slot_of_place, axis=1)
    source_rows = (
        jnp.take(offsets, jnp.take(inverse, owner_rows)) + positions[None, :] - start_in_slot
    )
    outgoing = jnp.take(prefill_latent, source_rows.reshape(-1), axis=0).reshape(
        dp_count, OWN_TOK, latent_width
    )
    incoming = lax.all_to_all(outgoing, "dp", split_axis=0, concat_axis=0, tiled=True)
    new_rows = incoming.reshape(dp_count * OWN_TOK, latent_width)
    my_lengths = lax.dynamic_index_in_dim(new_lengths, dp_rank, 0, keepdims=False)
    my_start = jnp.cumsum(my_lengths) - my_lengths
    in_slot = (positions[None, :] >= my_start[:, None]) & (
        positions[None, :] < (my_start + my_lengths)[:, None]
    )
    new_mask = jnp.tile(in_slot, (1, dp_count))
    cache_mask = jnp.arange(kv_cache.shape[1], dtype=jnp.int32)[None, :] < ctx_lengths[:, None]
    share_first = tp_rank * share_width

    def finish(first, last):
        step_ids = jnp.arange(first, last, dtype=jnp.int32)
        steps_here = last - first
        head_out = attend(
            queries[first:last],
            step_ids,
            kv_cache,
            cache_mask,
            new_rows,
            new_mask,
            step_latents,
            w_uv,
        )
        every_row = lax.all_gather(head_out, "dp", axis=1, tiled=True)
        partial_value = jnp.dot(
            every_row.reshape(steps_here * total_requests, -1),
            w_out.reshape(-1, block_width),
            preferred_element_type=jnp.float32,
        )
        partial_value = partial_value.reshape(steps_here, total_requests, block_width)
        own_cols = lax.dynamic_slice_in_dim(partial_value, share_first, share_width, 2) + hidden[
            first:last
        ].astype(jnp.float32)
        partial_value = lax.dynamic_update_slice_in_dim(partial_value, own_cols, share_first, 2)
        mixed = lax.psum_scatter(partial_value, "tp", scatter_dimension=2, tiled=True)
        squares = lax.psum(jnp.sum(mixed * mixed, axis=-1), ("dp", "tp"))
        gain_part = lax.dynamic_slice_in_dim(
            ffn_gain, dp_rank * block_width + share_first, share_width
        )
        normed_part = (
            mixed * lax.rsqrt(squares / model_width + norm_eps)[..., None] * gain_part
        ).astype(jnp.bfloat16)
        normed = lax.all_gather(normed_part, ("dp", "tp"), axis=2, tiled=True)
        flat_input = normed.reshape(steps_here * total_requests, model_width)
        gate_out = jnp.dot(flat_input, w_gate, preferred_element_type=jnp.float32)
        up_out = jnp.dot(flat_input, w_up, preferred_element_type=jnp.float32)
        activated = (jax.nn.silu(gate_out) * up_out).astype(jnp.bfloat16)
        down_out = jnp.dot(activated, w_down, preferred_element_type=jnp.float32).reshape(
            steps_here, total_requests, model_width
        )
        ffn_part = lax.psum_scatter(down_out, ("dp", "tp"), scatter_dimension=2, tiled=True)
        return (mixed + ffn_part).astype(jnp.bfloat16)

    step_total = queries.shape[0]
    result = jnp.concatenate([finish(index, index + 1) for index in range(step_total)], axis=0)
    return result


def solution(mesh):
    return jax.shard_map(
        shards,
        mesh=mesh,
        in_specs=(
            P("dp", None),
            P(),
            P(),
            P("dp"),
            P("dp", None, None),
            P(None, "dp", "tp", None),
            P(None, "dp", None),
            P("tp", None, None),
            P("tp", None, "dp"),
            P(None, None, ("dp", "tp")),
            P(),
            P(None, ("dp", "tp")),
            P(None, ("dp", "tp")),
            P(("dp", "tp"), None),
        ),
        out_specs=P(None, None, ("dp", "tp")),
        check_vma=False,
    )
```

profile of v0, /device:TPU:1, one launch (start us, length us, event | category | flops | bytes accessed | tf_op | source)
XLA Modules:
  0.0 847.0 jit_solution(17273692832596488517)
XLA Ops:
  6.5 0.9 copy.119
  7.5 0.7 reduce_window_sum.25
  8.2 0.7 sub.74
  9.0 4.7 gather_fusion.1
  14.1 0.1 broadcast_in_dim.128
  14.2 0.2 select_reduce_fusion
  14.4 3.3 gather_fusion.2
  18.2 0.2 reduce-window.17
  18.5 3.3 gather_fusion.3
  22.3 0.3 copy.127
  22.6 2.0 gather_fusion
  24.7 1.0 broadcast_select_fusion
  25.7 12.3 %all-to-all-start = ((bf16[32,16,576]{2,1,0:T(8,128)(2,1)}), bf16[32,16,576]{2,1,0:T(8,128)(2,1)}, u32[]{:S(2)}, u32[]{:S(2)}) async-start(bf16[32,16,576]{2,1,0:T(8,128)(2,1)} %broadcast_select_fusion), calls=%async_computation | async-start | bytes 1310720 | tf_op jit(solution)/shard_map/all_to_all | solution.py:108
  38.1 0.2 dynamic-slice_reduce_fusion
  38.3 0.2 reduce-window.16
  38.7 1.0 fusion.127
  39.8 1.0 fusion.130
  40.9 4.0 fusion.128
  45.0 0.9 fusion.131
  45.8 10.8 %all-to-all-done = bf16[32,16,576]{2,1,0:T(8,128)(2,1)} async-done(((bf16[32,16,576]{2,1,0:T(8,128)(2,1)}), bf16[32,16,576]{2,1,0:T(8,128)(2,1)}, u32[]{:S(2)}, u32[]{:S(2)}) %all-to-all-start) | async-done | bytes 589856 | tf_op jit(solution)/shard_map/all_to_all | solution.py:108
  56.7 1.6 fusion.129
  58.3 1.5 fusion.132
  59.9 0.2 fusion.75
  60.0 1.1 fusion.69
  61.2 3.5 fusion.18
  64.7 0.2 convolution_bitcast_fusion
  64.9 0.2 fusion.74
  65.1 0.2 fusion.68
  65.4 1.2 fusion.21
  66.5 0.2 convolution_bitcast_fusion.2
  66.8 1.3 fusion.35
  68.1 0.4 fusion.55
  68.5 1.3 fusion.34
  69.8 0.4 fusion.54
  70.2 37.1 %all_gather.12 = bf16[1,128,16,128]{3,2,0,1:T(8,128)(2,1)S(1)} all-gather(bf16[1,4,16,128]{3,2,0,1:T(8,128)(2,1)S(1)} %copy.135), channel_id=1, replica_groups=mesh['dp'=32,'tp'=8] {'dp'}, dimensions={1}, use_global_device_ids=true | all-gather | bytes 540672 | tf_op jit(solution)/shard_map/all_gather | solution.py:132
  107.4 0.5 copy.136
  107.8 34.9 %all_gather.14 = bf16[1,128,16,128]{3,2,0,1:T(8,128)(2,1)S(1)} all-gather(bf16[1,4,16,128]{3,2,0,1:T(8,128)(2,1)S(1)} %copy.147), channel_id=1, replica_groups=mesh['dp'=32,'tp'=8] {'dp'}, dimensions={1}, use_global_device_ids=true | all-gather | bytes 540672 | tf_op jit(solution)/shard_map/all_gather | solution.py:132
  142.7 1.2 copy.148
  143.9 1.6 fusion.62
  145.5 1.8 fusion.64
  147.3 0.2 dynamic_update_slice.7
  147.6 0.2 dynamic_update_slice.6
  147.9 0.4 copy-done.6
  148.2 0.3 copy-done.5
  148.6 0.6 dynamic-slice.8
  149.8 0.8 dynamic_slice.16
  150.6 83.8 %all-reduce.12.cloned.1.call-done = (f32[1,128,224]{1,0,2:T(1,128)}, f32[1,128,224]{1,0,2:T(1,128)}) async-done(((f32[1,128,224]{1,0,2:T(1,128)}, f32[1,128,224]{1,0,2:T(1,128)}), (f32[1,128,224]{1,0,2:T(1,128)}, f32[1,128,224]{1,0,2:T(1,128)})) %all-reduce.12.cloned.1.call-update) | async-done | bytes 229392
  234.4 0.8 multiply_reduce_fusion
  235.1 0.8 multiply_reduce_fusion.1
  235.9 78.4 %all-reduce.4 = (f32[1,128]{1,0:T(1,128)S(1)}, f32[1,128]{1,0:T(1,128)S(1)}) all-reduce(f32[1,128]{1,0:T(1,128)S(1)} %bitcast.242, f32[1,128]{1,0:T(1,128)S(1)} %bitcast.243), channel_id=1, replica_groups=mesh['dp'=32,'tp'=8] {'dp','tp'}, use_global_device_ids=true, to_apply=%region_24.26 | all-reduce | flops 256 | bytes 2048 | tf_op jit(solution)/shard_map/psum | solution.py:144
  314.3 1.4 multiply_convert_fusion.1
  315.8 0.7 all-gather.3.cloned.1.call-update
  316.5 110.4 %all-gather.5.cloned.1.call-done = bf16[1,128,7168]{1,0,2:T(2,128)(2,1)} async-done(((bf16[1,128,28]{1,0,2:T(2,128)(2,1)}), bf16[1,128,7168]{1,0,2:T(2,128)(2,1)}) %all-gather.5.cloned.1.call-update) | async-done | bytes 1835024 | tf_op jit(solution)/shard_map/all_gather | solution.py:151
  427.0 8.5 copy.151
  435.4 2.2 fusion.6
  437.7 105.6 %all-gather.3.cloned.1.call-done = bf16[1,128,7168]{1,0,2:T(2,128)(2,1)} async-done(((bf16[1,128,28]{1,0,2:T(2,128)(2,1)}), bf16[1,128,7168]{1,0,2:T(2,128)(2,1)}) %all-gather.3.cloned.1.call-update) | async-done | bytes 1835024 | tf_op jit(solution)/shard_map/all_gather | solution.py:151
  543.3 8.4 copy.140
  551.7 2.5 fusion.10
  554.3 5.8 fusion.49
  560.0 5.8 fusion.52
  565.9 272.4 %all-reduce.10.cloned.1.call-done = (f32[1,128,7168]{1,0,2:T(1,128)}, f32[1,128,7168]{1,0,2:T(1,128)}) async-done(((f32[1,128,7168]{1,0,2:T(1,128)}, f32[1,128,7168]{1,0,2:T(1,128)}), (f32[1,128,7168]{1,0,2:T(1,128)}, f32[1,128,7168]{1,0,2:T(1,128)})) %all-reduce.10.cloned.1.call-update) | async-done | bytes 7340048
  838.3 0.7 fusion.107
  839.1 0.8 fusion.106
  839.8 0.6 pad_maximum_fusion
  (89 shorter events, 2.2 us)
Async XLA Ops:
  6.5 61.6 %copy-start = (bf16[16,512,128]{2,1,0:T(8,128)(2,1)S(1)}, bf16[16,512,128]{2,1,0:T(8,128)(2,1)}, u32[]{:S(2)}) copy-start(bf16[16,512,128]{2,1,0:T(8,128)(2,1)} %param.23) | copy-start | bytes 6291460
  9.0 5.1 copy-start.11
  18.5 3.8 copy-start.4
  22.6 15.5 %copy-start.8 = (s32[32,4]{0,1:T(4,128)S(1)}, s32[32,4]{0,1:T(4,128)}, u32[]{:S(2)}) copy-start(s32[32,4]{0,1:T(4,128)} %param.18) | copy-start | bytes 1540
  22.6 15.8 %copy-start.9 = (bf16[2,4,576]{2,1,0:T(4,128)(2,1)S(1)}, bf16[2,4,576]{2,1,0:T(4,128)(2,1)}, u32[]{:S(2)}) copy-start(bf16[2,4,576]{2,1,0:T(4,128)(2,1)} %param.22) | copy-start | bytes 27652
  22.6 16.0 %copy-start.7 = (bf16[2,128,28]{1,0,2:T(2,128)(2,1)S(1)}, bf16[2,128,28]{1,0,2:T(2,128)(2,1)}, u32[]{:S(2)}) copy-start(bf16[2,128,28]{1,0,2:T(2,128)(2,1)} %param.25) | copy-start | bytes 43012
  22.6 17.1 %copy-start.10 = (s32[4]{0:T(128)S(1)}, s32[4]{0:T(128)}, u32[]{:S(2)}) copy-start(s32[4]{0:T(128)} %param.19) | copy-start | bytes 52
  25.7 19.2 %slice-start = ((s8[4718592]{0:T(1024)(128)(4,1)}), s8[524288]{0:T(1024)(128)(4,1)S(1)}, s32[]{:S(2)}) async-start(s8[4718592]{0:T(1024)(128)(4,1)} %bitcast.227), calls=%async_computation.5 | async-start | bytes 1048576
  25.7 31.0 %all-to-all-start = ((bf16[32,16,576]{2,1,0:T(8,128)(2,1)}), bf16[32,16,576]{2,1,0:T(8,128)(2,1)}, u32[]{:S(2)}, u32[]{:S(2)}) async-start(bf16[32,16,576]{2,1,0:T(8,128)(2,1)} %broadcast_select_fusion), calls=%async_computation | async-start | bytes 1310720 | tf_op jit(solution)/shard_map/all_to_all | solution.py:108
  38.0 196.4 %all-reduce.12.cloned.1.call-start = ((), (), s32[]{:S(2)}) async-start(), calls=%async_computation.4 | async-start | bytes 458752
  40.9 4.1 slice-start.1
  40.9 4.1 copy-start.3
  45.0 20.4 %slice-start.2 = ((s8[4718592]{0:T(1024)(128)(4,1)}), s8[524288]{0:T(1024)(128)(4,1)S(1)}, s32[]{:S(2)}) async-start(s8[4718592]{0:T(1024)(128)(4,1)} %bitcast.229), calls=%async_computation.7 | async-start | bytes 1048576
  56.7 8.7 %slice-start.3 = ((s8[4718592]{0:T(1024)(128)(4,1)}), s8[4194304]{0:T(1024)(128)(4,1)S(1)}, s32[]{:S(2)}) async-start(s8[4718592]{0:T(1024)(128)(4,1)} %bitcast.229), calls=%async_computation.8 | async-start | bytes 8388608
  70.2 78.4 %copy-start.12 = (u32[256]{0:T(256)S(1)}, u32[256]{0:T(256)}, u32[]{:S(2)}) copy-start(u32[256]{0:T(256)} %constant.123) | copy-start | bytes 3076
  145.5 289.9 %copy-start.2 = (bf16[7168,72]{0,1:T(8,128)(2,1)S(1)}, bf16[7168,72]{0,1:T(8,128)(2,1)}, u32[]{:S(2)}) copy-start(bf16[7168,72]{0,1:T(8,128)(2,1)} %param.27) | copy-start | bytes 3096580
  147.6 0.6 copy-start.6
  147.8 0.6 copy-start.5
  148.5 278.5 %all-gather.5.cloned.1.call-start = ((), (), s32[]{:S(2)}) async-start(), calls=%async_computation.2 | async-start | bytes 3684352 | tf_op jit(solution)/shard_map/all_gather | solution.py:151
  315.7 227.6 %all-gather.3.cloned.1.call-start = ((), (), s32[]{:S(2)}) async-start(), calls=%async_computation.1 | async-start | bytes 3684352 | tf_op jit(solution)/shard_map/all_gather | solution.py:151
  316.5 521.8 %all-reduce.10.cloned.1.call-start = ((), (), s32[]{:S(2)}) async-start(), calls=%async_computation.3 | async-start | bytes 14680064
  437.7 116.6 %copy-start.1 = (bf16[72,7168]{1,0:T(8,128)(2,1)S(1)}, bf16[72,7168]{1,0:T(8,128)(2,1)}, u32[]{:S(2)}) copy-start(bf16[72,7168]{1,0:T(8,128)(2,1)} %param.29) | copy-start | bytes 3096580
Sparse Core Ops, SparseCore 0:
  148.6 85.7 all-reduce.11
  315.9 111.0 all-gather.4
  431.4 111.8 all-gather.2
  566.0 272.2 all-reduce.9
where the time goes:
time: 849 us; the launch traced here: 847 us
  waiting for transfers between devices  584 us (69%)
  blocking collectives  150 us (18%)
  matrix products  38.4 us (5%)
  local copies, waits for them, and re-layouts  37.5 us (4%)
  between operations  14.3 us (2%)
  starting transfers between devices  12.4 us (1%)
  other arithmetic  10.2 us (1%)
    unnamed x6, waiting for transfers between devices  357 us
    all_gather x2, waiting for transfers between devices, finish(): normed = lax.all_gather(normed_part, ('dp', 'tp'), axis=2, tiled=True)  216 us
    psum x1, blocking collectives, finish(): squares = lax.psum(jnp.sum(mixed * mixed, axis=-1), ('dp', 'tp'))  78.4 us
    all_gather x2, blocking collectives, finish(): every_row = lax.all_gather(head_out, 'dp', axis=1, tiled=True)  72 us
  transfers between devices with their start and end apart: 5, of which 5 were waited for; matrix products, arithmetic and copies ran while one was open for 2% of the time, Pallas kernels for 0%

commit v1 on v0

v1 whole, which is shorter than its diff:
```python
import functools

import jax
import jax.numpy as jnp
from jax import lax
from jax.experimental import pallas as pl
from jax.experimental.pallas import tpu as pltpu
from jax.sharding import PartitionSpec as P

LAT = 512
QKD = 192
OWN_TOK = 16
PAD = 32
GROUP = 4

masked_score = -1e30
norm_eps = 1e-06
bf16, f32, i32 = jnp.bfloat16, jnp.float32, jnp.int32

NT = (((1,), (1,)), ((), ()))
NN = (((1,), (0,)), ((), ()))


def dot(a, b, dims=NN):
    return lax.dot_general(a, b, dims, preferred_element_type=f32)


def iota(shape, dim):
    return lax.broadcasted_iota(i32, shape, dim)


def call(body, out_shape, cost=(0, 0), **kwargs):
    return pl.pallas_call(
        body,
        out_shape=out_shape,
        compiler_params=pltpu.CompilerParams(vmem_limit_bytes=40 * 1024 * 1024),
        cost_estimate=pl.CostEstimate(flops=cost[0], bytes_accessed=cost[1], transcendentals=0),
        **kwargs,
    )


def share_picker(tp, width):
    shape = (tp * PAD, tp * width)
    row = iota(shape, 0)
    place = row % PAD
    wanted = (row // PAD) * width + place
    return jnp.where((iota(shape, 1) == wanted) & (place < width), 1.0, 0.0).astype(bf16)


def token_picker(dp, per_owner, steps):
    total = dp * per_owner * steps
    shape = (total, total)
    row = iota(shape, 0)
    step, request = row // (dp * per_owner), row % (dp * per_owner)
    wanted = request * steps + step
    return jnp.where(iota(shape, 1) == wanted, 1.0, 0.0).astype(bf16)


def route_kernel(slot_col, slot_row, len_col, len_row, rows_ref, out_ref):
    count = slot_col.shape[0]
    total = rows_ref.shape[0]
    square = (count, count)
    sub, lane = iota(square, 0), iota(square, 1)
    hot = slot_col[...] == lane
    hot_t = sub == slot_row[...]
    rows_col = jnp.sum(jnp.where(hot, len_row[...], 0), axis=1, keepdims=True)
    rows_row = jnp.sum(jnp.where(hot_t, len_col[...], 0), axis=0, keepdims=True)
    owner_start = jnp.sum(jnp.where(sub < lane, len_col[...], 0), axis=0, keepdims=True)
    start_col = jnp.sum(jnp.where(lane < sub, rows_row, 0), axis=1, keepdims=True)
    target_col = jnp.sum(jnp.where(hot, owner_start, 0), axis=1, keepdims=True)
    at = iota((count, total), 1)
    inside = (at >= start_col) & (at < start_col + rows_col)
    shift = jnp.sum(jnp.where(inside, target_col - start_col, 0), axis=0, keepdims=True)
    target = iota((1, total), 1) + shift
    pick = jnp.where(iota((total, total), 0) == target, 1.0, 0.0).astype(bf16)
    out_ref[...] = dot(pick, rows_ref[...]).astype(bf16)


def route(request_slot, new_lengths, prefill_latent):
    count = request_slot.shape[0]
    flat = new_lengths.reshape(-1)
    total, width = prefill_latent.shape
    return call(
        route_kernel,
        jax.ShapeDtypeStruct((total, width), bf16),
        (2 * total * total * width, 4 * total * width),
        name="route",
    )(
        request_slot.reshape(count, 1),
        request_slot.reshape(1, count),
        flat.reshape(count, 1),
        flat.reshape(1, count),
        prefill_latent,
    )


def reshard_kernel(tp, width, wg_ref, wu_ref, wd_ref, gu_ref, dn_ref, g_scr, u_scr, d_scr):
    block = tp * width
    units = wg_ref.shape[1]
    picker = share_picker(tp, width)
    for i in range(GROUP):
        rows = slice(i * block, (i + 1) * block)
        parts = (
            (dot(picker, wg_ref[rows, :]), g_scr),
            (dot(picker, wu_ref[rows, :]), u_scr),
            (dot(picker, wd_ref[:, rows], NT), d_scr),
        )
        for value, scratch in parts:
            value = value.astype(bf16)
            for j in range(tp):
                scratch[pl.ds((j * GROUP + i) * PAD, PAD), :] = value[j * PAD : (j + 1) * PAD, :]
    two = (2 * units, units)
    eye_g = jnp.where(iota(two, 0) == iota(two, 1), 1.0, 0.0).astype(bf16)
    eye_u = jnp.where(iota(two, 0) == iota(two, 1) + units, 1.0, 0.0).astype(bf16)
    gu = (dot(eye_g, g_scr[...], NT) + dot(eye_u, u_scr[...], NT)).astype(bf16)
    padded = (dn_ref.shape[1], units)
    eye_d = jnp.where(iota(padded, 0) == iota(padded, 1), 1.0, 0.0).astype(bf16)
    dn = dot(eye_d, d_scr[...], NT).astype(bf16)
    lanes = GROUP * PAD
    for j in range(tp):
        gu_ref[j] = gu[:, j * lanes : (j + 1) * lanes]
        dn_ref[j] = dn[:, j * lanes : (j + 1) * lanes]


def reshard(w_gate, w_up, w_down, dp, tp, width, unit_pad):
    units = w_gate.shape[1]
    block = tp * width * GROUP
    lanes = GROUP * PAD
    scratch = pltpu.VMEM((tp * lanes, units), bf16)
    return call(
        functools.partial(reshard_kernel, tp, width),
        (
            jax.ShapeDtypeStruct((tp, 2 * units, dp * PAD), bf16),
            jax.ShapeDtypeStruct((tp, unit_pad, dp * PAD), bf16),
        ),
        (2 * 3 * dp * tp * PAD * tp * width * units, 14 * w_gate.size),
        grid=(dp // GROUP,),
        in_specs=[
            pl.BlockSpec((block, units), lambda c: (c, 0)),
            pl.BlockSpec((block, units), lambda c: (c, 0)),
            pl.BlockSpec((units, block), lambda c: (0, c)),
        ],
        out_specs=(
            pl.BlockSpec((tp, 2 * units, lanes), lambda c: (0, 0, c)),
            pl.BlockSpec((tp, unit_pad, lanes), lambda c: (0, 0, c)),
        ),
        scratch_shapes=[scratch, scratch, scratch],
        name="reshard",
    )(w_gate, w_up, w_down)


def turn_kernel(x_ref, out_ref):
    lanes = x_ref.shape[1]
    eye = jnp.where(iota((lanes, lanes), 0) == iota((lanes, lanes), 1), 1.0, 0.0).astype(bf16)
    out_ref[...] = dot(eye, x_ref[...], NT).astype(bf16)


def turn(x):
    rows, columns = x.shape
    lanes = 256 if columns % 256 == 0 else 128
    return call(
        turn_kernel,
        jax.ShapeDtypeStruct((columns, rows), bf16),
        (2 * lanes * rows * columns, 4 * rows * columns),
        grid=(columns // lanes,),
        in_specs=[pl.BlockSpec((rows, lanes), lambda c: (0, c))],
        out_specs=pl.BlockSpec((lanes, rows), lambda c: (c, 0)),
        name="turn",
    )(x)


def wout_kernel(tp, width, w_ref, out_ref):
    out_ref[...] = dot(share_picker(tp, width), w_ref[0], NT).astype(bf16)


def turn_wout(w_out, tp, width):
    heads, values, columns = w_out.shape
    return call(
        functools.partial(wout_kernel, tp, width),
        jax.ShapeDtypeStruct((tp * PAD, heads * values), bf16),
        (2 * tp * PAD * columns * heads * values, 4 * w_out.size),
        grid=(heads,),
        in_specs=[pl.BlockSpec((1, values, columns), lambda h: (h, 0, 0))],
        out_specs=pl.BlockSpec((tp * PAD, values), lambda h: (0, h)),
        name="turn_wout",
    )(w_out)


def hidden_kernel(dp, per_owner, steps, h_ref, out_ref):
    total, width = h_ref.shape
    eye = jnp.where(iota((PAD, width), 0) == iota((PAD, width), 1), 1.0, 0.0).astype(bf16)
    turned = dot(eye, h_ref[...], NT).astype(bf16)
    out_ref[...] = dot(turned, token_picker(dp, per_owner, steps))


def cache_kernel(ctx_ref, q_ref, kv_ref, tok_ref, acc_ref, top_ref, sum_ref):
    at = pl.program_id(0)
    scale = QKD ** (-0.5)
    steps, _, heads, width = q_ref.shape
    rows = steps * heads
    query = q_ref[...].reshape(rows, width)
    keys = kv_ref[0]
    toks = tok_ref[0]
    scores = dot(query, keys, NT) * scale
    scores = jnp.where(iota(scores.shape, 1) < ctx_ref[at], scores, masked_score)
    fresh = dot(query, toks, NT) * scale
    step = iota(fresh.shape, 0) // heads
    fresh = jnp.where(iota(fresh.shape, 1) <= step, fresh, masked_score)
    top = jnp.maximum(
        jnp.max(scores, axis=1, keepdims=True), jnp.max(fresh, axis=1, keepdims=True)
    )
    scores = jnp.exp(scores - top)
    fresh = jnp.exp(fresh - top)
    total = jnp.sum(scores, axis=1, keepdims=True) + jnp.sum(fresh, axis=1, keepdims=True)
    acc_ref[0] = dot(scores.astype(bf16), keys[:, :LAT]) + dot(fresh.astype(bf16), toks[:, :LAT])
    top_ref[0] = jnp.broadcast_to(top, top_ref.shape[1:])
    sum_ref[0] = jnp.broadcast_to(total, sum_ref.shape[1:])


def attend_cache(ctx_lengths, queries, kv_cache, tokens):
    steps, per_owner, heads, width = queries.shape
    keys = kv_cache.shape[1]
    rows = steps * heads
    side = jax.ShapeDtypeStruct((per_owner, rows, 128), f32)
    side_spec = pl.BlockSpec((1, rows, 128), lambda q: (q, 0, 0))
    return call(
        cache_kernel,
        (jax.ShapeDtypeStruct((per_owner, rows, LAT), f32), side, side),
        (2 * per_owner * rows * keys * (width + LAT), 2 * kv_cache.size),
        grid=(per_owner,),
        in_specs=[
            pl.BlockSpec(memory_space=pltpu.SMEM),
            pl.BlockSpec((steps, 1, heads, width), lambda q: (0, q, 0, 0)),
            pl.BlockSpec((1, keys, width), lambda q: (q, 0, 0)),
            pl.BlockSpec((1, tokens.shape[1], width), lambda q: (q, 0, 0)),
        ],
        out_specs=(pl.BlockSpec((1, rows, LAT), lambda q: (q, 0, 0)), side_spec, side_spec),
        name="attend_cache",
    )(ctx_lengths, queries, kv_cache, tokens)


def merge_kernel(len_ref, q_ref, new_ref, acc_ref, top_ref, sum_ref, uv_ref, out_ref):
    scale = QKD ** (-0.5)
    steps, per_owner, heads, width = q_ref.shape
    rows = steps * heads
    new = new_ref[...]
    query = jnp.concatenate([q_ref[:, q].reshape(rows, width) for q in range(per_owner)], axis=0)
    scores = dot(query, new, NT) * scale
    place = iota(scores.shape, 1) % OWN_TOK
    owner_row = iota(scores.shape, 0) // rows
    first = jnp.zeros(scores.shape, i32)
    last = jnp.zeros(scores.shape, i32)
    start = jnp.int32(0)
    for q in range(per_owner):
        end = start + len_ref[q]
        first = jnp.where(owner_row == q, start, first)
        last = jnp.where(owner_row == q, end, last)
        start = end
    scores = jnp.where((place >= first) & (place < last), scores, masked_score)
    total_rows = per_owner * rows
    old_top = top_ref[...].reshape(total_rows, 128)[:, :1]
    old_sum = sum_ref[...].reshape(total_rows, 128)[:, :1]
    top = jnp.maximum(jnp.max(scores, axis=1, keepdims=True), old_top)
    scores = jnp.exp(scores - top)
    weight = jnp.exp(old_top - top)
    total = jnp.sum(scores, axis=1, keepdims=True) + old_sum * weight
    acc = acc_ref[...].reshape(total_rows, LAT) * weight + dot(scores.astype(bf16), new[:, :LAT])
    latent = (acc / total).astype(bf16)
    values = uv_ref.shape[2]
    groups = per_owner * steps
    head_of = iota((groups, heads, values), 1)
    for h in range(heads):
        full = dot(latent, uv_ref[h]).reshape(groups, heads, values)
        mine = jnp.sum(jnp.where(head_of == h, full, 0.0), axis=1).astype(bf16)
        out_ref[:, :, h * values : (h + 1) * values] = jnp.broadcast_to(
            mine[None], (out_ref.shape[0], groups, values)
        )


def attend_new(my_lengths, queries, new_rows, acc, top, total, w_uv, dp):
    steps, per_owner, heads, _ = queries.shape
    whole = pl.BlockSpec(memory_space=pltpu.VMEM)
    return call(
        merge_kernel,
        jax.ShapeDtypeStruct((dp, per_owner * steps, heads * w_uv.shape[2]), bf16),
        (4 * new_rows.size * per_owner * steps * heads, 2 * w_uv.size),
        in_specs=[pl.BlockSpec(memory_space=pltpu.SMEM)] + [whole] * 6,
        out_specs=whole,
        name="attend_new",
    )(my_lengths, queries, new_rows, acc, top, total, w_uv)


def project_kernel(w_ref, x_ref, out_ref):
    out_ref[...] = dot(w_ref[...], x_ref[...], NT).astype(bf16).reshape(out_ref.shape)


def project(turned, every, tp):
    rows, depth = turned.shape
    return call(
        project_kernel,
        jax.ShapeDtypeStruct((tp, PAD, every.shape[0]), bf16),
        (2 * rows * depth * every.shape[0], 2 * (turned.size + every.size)),
        name="project",
    )(turned, every)


def split_sum(value):
    high = value.astype(bf16).astype(f32)
    return high, value - high


def mixed_kernel(width, part_ref, hidden_ref, gain_ref, mixed_ref, out_ref):
    mixed = jnp.sum(part_ref[...].astype(f32), axis=0) + hidden_ref[...]
    mixed_ref[...] = mixed
    high, low = split_sum(jnp.sum(mixed * mixed, axis=0, keepdims=True))
    row = iota(mixed.shape, 0)
    sent = jnp.where(row == width, high, jnp.where(row == width + 1, low, mixed * gain_ref[...]))
    out_ref[...] = jnp.broadcast_to(sent.astype(bf16)[None], out_ref.shape)


def make_mixed(parts, hidden_t, gain, dp, width):
    _, rows, columns = parts.shape
    return call(
        functools.partial(mixed_kernel, width),
        (
            jax.ShapeDtypeStruct((rows, columns), f32),
            jax.ShapeDtypeStruct((dp, rows, columns), bf16),
        ),
        (parts.size, 4 * parts.size),
        name="make_mixed",
    )(parts, hidden_t, gain)


def gate_kernel(width, w_ref, x_ref, out_ref):
    units = w_ref.shape[1]
    x = x_ref[...]
    depth = x.shape[0]
    extra = out_ref.shape[1] - units
    place = iota((extra, depth), 1) % PAD
    pick = jnp.where((place == width) | (place == width + 1), 1.0, 0.0).astype(bf16)
    squares = dot(pick, x)
    high, low = split_sum(squares)
    row = iota(squares.shape, 0)
    tail = jnp.where(row == 0, high, jnp.where(row == 1, low, 0.0))
    out_ref[0, :units, :] = dot(w_ref[0], x).astype(bf16)
    out_ref[0, units:, :] = tail.astype(bf16)


def gate_up(weights, x, width):
    tp, units, depth = weights.shape
    columns = x.shape[1]
    return call(
        functools.partial(gate_kernel, width),
        jax.ShapeDtypeStruct((tp, units + 16, columns), bf16),
        (2 * weights.size * columns, 2 * weights.size + 2 * x.size),
        grid=(tp,),
        in_specs=[
            pl.BlockSpec((1, units, depth), lambda j: (j, 0, 0)),
            pl.BlockSpec((depth, columns), lambda j: (0, 0)),
        ],
        out_specs=pl.BlockSpec((1, units + 16, columns), lambda j: (j, 0, 0)),
        name="gate_up",
    )(weights, x)


def activate_kernel(model_width, units, part_ref, out_ref):
    sums = jnp.sum(part_ref[...].astype(f32), axis=0)
    squares = sums[2 * units : 2 * units + 1] + sums[2 * units + 1 : 2 * units + 2]
    factor = lax.rsqrt(squares / model_width + norm_eps)
    gate = sums[:units] * factor
    up = sums[units : 2 * units] * factor
    value = gate / (1.0 + jnp.exp(-gate)) * up
    spare = out_ref.shape[1] - units
    if spare:
        value = jnp.concatenate([value, jnp.zeros((spare, value.shape[1]), f32)], axis=0)
    out_ref[...] = jnp.broadcast_to(value.astype(bf16)[None], out_ref.shape)


def activate(parts, model_width, units, unit_pad):
    tp, _, columns = parts.shape
    return call(
        functools.partial(activate_kernel, model_width, units),
        jax.ShapeDtypeStruct((tp, unit_pad, columns), bf16),
        (10 * parts.size, 4 * parts.size),
        name="activate",
    )(parts)


def down_kernel(w_ref, x_ref, out_ref):
    out_ref[...] = dot(w_ref[...], x_ref[...]).astype(bf16).reshape(out_ref.shape)


def down(turned, x, dp):
    rows, depth = turned.shape
    columns = x.shape[1]
    block = 256 if rows % 256 == 0 else 128
    return call(
        down_kernel,
        jax.ShapeDtypeStruct((dp, PAD, columns), bf16),
        (2 * turned.size * columns, 2 * turned.size + 2 * x.size),
        grid=(rows // block,),
        in_specs=[
            pl.BlockSpec((block, depth), lambda c: (c, 0)),
            pl.BlockSpec((depth, columns), lambda c: (0, 0)),
        ],
        out_specs=pl.BlockSpec((block // PAD, PAD, columns), lambda c: (c, 0, 0)),
        name="down",
    )(turned, x)


def finish_kernel(dp, per_owner, steps, part_ref, mixed_ref, out_ref):
    value = jnp.sum(part_ref[...].astype(f32), axis=0) + mixed_ref[...]
    picked = dot(token_picker(dp, per_owner, steps), value.astype(bf16), NT)
    out_ref[...] = picked[:, : out_ref.shape[1]].astype(bf16)


def exchange(x, axis):
    return lax.all_to_all(x, axis, split_axis=0, concat_axis=0, tiled=True)


def shards(
    prefill_latent,
    request_slot,
    new_lengths,
    ctx_lengths,
    kv_cache,
    queries,
    step_latents,
    w_uv,
    w_out,
    hidden,
    ffn_gain,
    w_gate,
    w_up,
    w_down,
):
    dp, tp = lax.axis_size("dp"), lax.axis_size("tp")
    dp_rank, tp_rank = lax.axis_index("dp"), lax.axis_index("tp")
    steps, per_owner = queries.shape[:2]
    width = hidden.shape[2]
    model_width = width * dp * tp
    units = w_gate.shape[1]
    unit_pad = -(-units // 16) * 16
    total = hidden.shape[0] * hidden.shape[1]

    routed = route(request_slot, new_lengths, prefill_latent)
    incoming = exchange(routed.reshape(dp, OWN_TOK, -1), "dp").reshape(dp * OWN_TOK, -1)

    tokens = jnp.pad(step_latents.transpose(1, 0, 2), ((0, 0), (0, 16 - steps), (0, 0)))
    acc, top, sums = attend_cache(ctx_lengths, queries, kv_cache, tokens)

    gate_up_w, down_w = reshard(w_gate, w_up, w_down, dp, tp, width, unit_pad)
    gate_up_w = exchange(gate_up_w, "tp")
    down_w = exchange(down_w, "tp")
    turned_out = turn_wout(w_out, tp, width)
    hidden_t = call(
        functools.partial(hidden_kernel, dp, per_owner, steps),
        jax.ShapeDtypeStruct((PAD, total), f32),
        name="turn_hidden",
    )(hidden.reshape(total, width))
    gain = lax.dynamic_slice_in_dim(ffn_gain, (dp_rank * tp + tp_rank) * width, width)
    gain = jnp.pad(gain, (0, PAD - width)).reshape(PAD, 1)

    my_lengths = lax.dynamic_index_in_dim(new_lengths, dp_rank, 0, keepdims=False)
    heads_out = attend_new(my_lengths, queries, incoming, acc, top, sums, w_uv, dp)
    every = exchange(heads_out, "dp").reshape(total, -1)
    parts = exchange(project(turned_out, every, tp), "tp")
    mixed, sent = make_mixed(parts, hidden_t, gain, dp, width)
    x = exchange(sent, "dp").reshape(dp * PAD, total)
    parts = exchange(gate_up(gate_up_w, x, width), "tp")
    act = exchange(activate(parts, model_width, units, unit_pad), "tp").reshape(-1, total)
    turned_down = turn(down_w.reshape(tp * unit_pad, dp * PAD))
    parts = exchange(down(turned_down, act, dp), "dp")
    out = call(
        functools.partial(finish_kernel, dp, per_owner, steps),
        jax.ShapeDtypeStruct((total, width), bf16),
        name="finish",
    )(parts, mixed)
    return out.reshape(steps, -1, width)


def solution(mesh):
    return jax.shard_map(
        shards,
        mesh=mesh,
        in_specs=(
            P("dp", None),
            P(),
            P(),
            P("dp"),
            P("dp", None, None),
            P(None, "dp", "tp", None),
            P(None, "dp", None),
            P("tp", None, None),
            P("tp", None, "dp"),
            P(None, None, ("dp", "tp")),
            P(),
            P(None, ("dp", "tp")),
            P(None, ("dp", "tp")),
            P(("dp", "tp"), None),
        ),
        out_specs=P(None, None, ("dp", "tp")),
        check_vma=False,
    )
```

time: 849 us -> 227 us (0.27)
  waiting for transfers between devices: 584 us -> 75.4 us
  blocking collectives: 150 us -> 56.6 us
  matrix products: 38.4 us -> 0 us
  Pallas kernels: 0 us -> 28.8 us
  starting transfers between devices: 12.4 us -> 39.3 us
  between operations: 14.3 us -> 0.22 us
  local copies, waits for them, and re-layouts: 37.5 us -> 24.2 us
  other arithmetic: 10.2 us -> 0 us
    unnamed x6 -> x0, waiting for transfers between devices: 357 us -> none
    all_gather x2 -> x0, waiting for transfers between devices: 216 us -> none  [finish(): normed = lax.all_gather(normed_part, ('dp', 'tp'), axis=2, tiled=True)]
    psum x1 -> x0, blocking collectives: 78.4 us -> none  [finish(): squares = lax.psum(jnp.sum(mixed * mixed, axis=-1), ('dp', 'tp'))]
    all_gather x2 -> x0, blocking collectives: 72 us -> none  [finish(): every_row = lax.all_gather(head_out, 'dp', axis=1, tiled=True)]
    all_to_all x1 -> x6, waiting for transfers between devices: 10.8 us -> 75.4 us  [exchange(): return lax.all_to_all(x, axis, split_axis=0, concat_axis=0, tiled=True)]
    all_to_all x0 -> x3, blocking collectives: none -> 56.6 us  [exchange(): return lax.all_to_all(x, axis, split_axis=0, concat_axis=0, tiled=True)]
    dot_general x20 -> x0, matrix products: 38.4 us -> none  [the longest x2 11.6 us: finish(): jnp.dot(activated, w_down, preferred_element_type=jnp.float32)]
    pallas_call x0 -> x13, Pallas kernels: none -> 28.8 us  [the longest x1 8.11 us: reshard(): call(functools.partial(reshard_kernel, tp, width), (jax.ShapeDtypeStruct(...]
  transfers between devices with their start and end apart: 5 -> 6, of which waited for: 5 -> 5; matrix products, arithmetic and copies ran while one was open for 2% -> 6% of each run, Pallas kernels for 0% -> 9%
where the time goes in v1:
time: 227 us; the launch traced here: 225 us
  waiting for transfers between devices  75.4 us (33%)
  blocking collectives  56.6 us (25%)
  starting transfers between devices  39.3 us (17%)
  Pallas kernels  28.8 us (13%)
  local copies, waits for them, and re-layouts  24.2 us (11%)
    all_to_all x6, waiting for transfers between devices, exchange(): return lax.all_to_all(x, axis, split_axis=0, concat_axis=0, tiled=True)  75.4 us
    all_to_all x3, blocking collectives, exchange(): return lax.all_to_all(x, axis, split_axis=0, concat_axis=0, tiled=True)  56.6 us
    all_to_all x6, starting transfers between devices, exchange(): return lax.all_to_all(x, axis, split_axis=0, concat_axis=0, tiled=True)  39.3 us
    unnamed x36, local copies, waits for them, and re-layouts  21.5 us
    pallas_call x1, Pallas kernels, reshard(): call(functools.partial(reshard_kernel, tp, width), (jax.ShapeDtypeStruct(...  8.11 us
    pallas_call x1, Pallas kernels, attend_cache(): call(cache_kernel, (jax.ShapeDtypeStruct((per_owner, rows, LAT), f32), si...  4.99 us
  transfers between devices with their start and end apart: 6, of which 5 were waited for; matrix products, arithmetic and copies ran while one was open for 6% of the time, Pallas kernels for 9%

profile of v1, /device:TPU:1, one launch (start us, length us, event | category | flops | bytes accessed | tf_op | source)
XLA Modules:
  0.0 224.6 jit_solution(8846747029755897828)
XLA Ops:
  0.0 0.0 copy-start.13
  0.0 0.8 copy.31
  0.8 0.1 reshape_reshape.8.len_col
  0.9 0.1 reshape_reshape.7.len_row
  1.0 1.4 copy.35.rows_ref
  2.4 0.8 copy.33.slot_col
  3.2 0.0 copy-start.7
  3.2 0.6 copy-done.7
  3.8 1.7 route.1
  5.5 12.0 %all-to-all-start.2 = ((bf16[32,16,576]{2,1,0:T(8,128)(2,1)}), bf16[32,16,576]{2,1,0:T(8,128)(2,1)S(1)}, u32[]{:S(2)}, u32[]{:S(2)}) async-start(bf16[32,16,576]{2,1,0:T(8,128)(2,1)} %bitcast.3), calls=%async_computation.2 | async-start | bytes 1310720 | tf_op jit(solution)/shard_map/all_to_all | solution.py:418
  17.5 0.0 copy-done.13
  17.6 0.2 dynamic-slice_reduce_fusion.len_ref
  17.7 0.0 copy-start.6
  17.8 0.0 copy-start.8
  17.8 7.7 %copy.37.kv_ref = bf16[4,1024,576]{2,1,0:T(8,128)(2,1)} copy(bf16[4,1024,576]{1,2,0:T(8,128)(2,1)} %param.18) | data formatting | bytes 9437184 | tf_op args[4]
  25.5 0.0 copy-done.12
  25.6 0.0 copy-done.6
  25.6 0.0 copy-done.8
  25.6 0.0 copy-start
  25.6 2.5 %copy-done = bf16[4,1024,576]{2,1,0:T(8,128)(2,1)S(1)} copy-done((bf16[4,1024,576]{2,1,0:T(8,128)(2,1)S(1)}, bf16[4,1024,576]{2,1,0:T(8,128)(2,1)}, u32[]{:S(2)}) %copy-start) | copy-done | bytes 4718616
  28.1 5.0 %attend_cache.1 = (f32[4,32,512]{2,1,0:T(8,128)S(1)}, f32[4,32,128]{2,1,0:T(8,128)S(1)}, f32[4,32,128]{2,1,0:T(8,128)S(1)}) custom-call(s32[4]{0:T(128)S(1)} %copy-done.8, bf16[2,4,16,576]{3,2,1,0:T(8,128)(2,1)S(1)} %copy-done.6, bf16[4,1024,576]{2,1,0:T(8,128)(2,1)S(1)} %copy-done, bf16[4,16,576]{2,1,0:T(8,128)(2,1)S(1)} %pad.8.tok_ref), custom_call_target="tpu_custom_call" | custom-call | flops 285212672 | bytes 4718592 | tf_op jit(solution)/shard_map/attend_cache/pallas_call | solution.py:226
  33.0 3.2 %all-to-all-done.2 = bf16[32,16,576]{2,1,0:T(8,128)(2,1)S(1)} async-done(((bf16[32,16,576]{2,1,0:T(8,128)(2,1)}), bf16[32,16,576]{2,1,0:T(8,128)(2,1)S(1)}, u32[]{:S(2)}, u32[]{:S(2)}) %all-to-all-start.2) | async-done | bytes 589856 | tf_op jit(solution)/shard_map/all_to_all | solution.py:418
  36.2 0.0 copy-done.3
  36.2 3.1 %attend_new.1 = bf16[32,8,2048]{2,1,0:T(8,128)(2,1)} custom-call(s32[4]{0:T(128)S(1)} %dynamic-slice_reduce_fusion.len_ref, bf16[2,4,16,576]{3,2,1,0:T(8,128)(2,1)S(1)} %copy-done.6, bf16[512,576]{1,0:T(8,128)(2,1)S(1)} %bitcast.17, f32[4,32,512]{2,1,0:T(8,128)S(1)} %get-tuple-element.14.acc_ref, f32[4,32,128]{2,1,0:T(8,128)S(1)} %get-tuple-element.15.top_ref, ...), custom_call_target="tpu_custom_call" | custom-call | flops 150994944 | bytes 2097152 | tf_op jit(solution)/shard_map/attend_new/pallas_call | solution.py:283
  39.4 6.2 %all-to-all-start.3 = ((bf16[32,8,2048]{2,1,0:T(8,128)(2,1)}), bf16[32,8,2048]{2,1,0:T(8,128)(2,1)S(1)}, u32[]{:S(2)}, u32[]{:S(2)}) async-start(bf16[32,8,2048]{2,1,0:T(8,128)(2,1)} %attend_new.1), calls=%async_computation.3 | async-start | bytes 2097152 | tf_op jit(solution)/shard_map/all_to_all | solution.py:418
  45.5 0.0 copy-done.10
  45.6 0.5 copy.30.w_ref
  46.1 3.4 %turn_wout.1.w_ref = bf16[256,2048]{1,0:T(8,128)(2,1)S(1)} custom-call(bf16[16,128,224]{2,1,0:T(8,128)(2,1)S(1)} %copy.30.w_ref), custom_call_target="tpu_custom_call" | custom-call | flops 234881024 | bytes 1835008 | tf_op jit(solution)/shard_map/turn_wout/pallas_call | solution.py:178
  49.5 0.0 copy-start.9
  49.5 21.7 %all-to-all-done.3 = bf16[32,8,2048]{2,1,0:T(8,128)(2,1)S(1)} async-done(((bf16[32,8,2048]{2,1,0:T(8,128)(2,1)}), bf16[32,8,2048]{2,1,0:T(8,128)(2,1)S(1)}, u32[]{:S(2)}, u32[]{:S(2)}) %all-to-all-start.3) | async-done | bytes 1048608 | tf_op jit(solution)/shard_map/all_to_all | solution.py:418
  71.2 1.1 project.1
  72.3 7.6 %all-to-all-start.4 = ((bf16[8,32,256]{2,1,0:T(8,128)(2,1)}), bf16[8,32,256]{2,1,0:T(8,128)(2,1)S(1)}, u32[]{:S(2)}, u32[]{:S(2)}) async-start(bf16[8,32,256]{2,1,0:T(8,128)(2,1)} %project.1), calls=%async_computation.4 | async-start | bytes 262144 | tf_op jit(solution)/shard_map/all_to_all | solution.py:418
  80.0 0.0 copy-done.9
  80.0 1.0 copy.28.wg_ref
  81.0 0.0 copy-start.5
  81.0 2.7 %copy.29.wu_ref = bf16[7168,72]{1,0:T(8,128)(2,1)} copy(bf16[7168,72]{0,1:T(8,128)(2,1)} %param.26) | data formatting | bytes 2064384 | tf_op args[12]
  83.7 0.0 copy-done.5
  83.7 1.5 copy-done.1
  85.2 8.1 %reshard.1 = (bf16[8,144,1024]{2,1,0:T(8,128)(2,1)S(1)}, bf16[8,80,1024]{2,1,0:T(8,128)(2,1)S(1)}) custom-call(bf16[7168,72]{1,0:T(8,128)(2,1)S(1)} %copy.28.wg_ref, bf16[7168,72]{1,0:T(8,128)(2,1)S(1)} %copy-done.1, bf16[72,7168]{1,0:T(8,128)(2,1)S(1)} %copy-done.5), custom_call_target="tpu_custom_call" | custom-call | flops 792723456 | bytes 7225344 | tf_op jit(solution)/shard_map/reshard/pallas_call | solution.py:130
  93.3 0.0 copy-start.2
  93.3 1.4 copy-done.2
  94.8 1.1 copy-done.4
  95.8 0.0 all-to-all-done.4.part_ref
  95.8 5.0 %all-to-all-start.1 = ((bf16[8,144,1024]{2,1,0:T(8,128)(2,1)}), bf16[8,144,1024]{2,1,0:T(8,128)(2,1)S(1)}, u32[]{:S(2)}, u32[]{:S(2)}) async-start(bf16[8,144,1024]{2,1,0:T(8,128)(2,1)} %copy-done.2), calls=%async_computation.1 | async-start | bytes 4718592 | tf_op jit(solution)/shard_map/all_to_all | solution.py:418
  100.8 0.8 dynamic_slice.8
  101.5 0.1 copy.39.gain_ref
  101.6 0.0 copy-done.11
  101.6 0.1 copy.38
  101.8 0.3 turn_hidden.1.hidden_ref
  102.1 0.1 make_mixed.1
  102.2 27.7 %all-to-all-done.1.w_ref = bf16[8,144,1024]{2,1,0:T(8,128)(2,1)S(1)} async-done(((bf16[8,144,1024]{2,1,0:T(8,128)(2,1)}), bf16[8,144,1024]{2,1,0:T(8,128)(2,1)S(1)}, u32[]{:S(2)}, u32[]{:S(2)}) %all-to-all-start.1) | async-done | bytes 2359328 | tf_op jit(solution)/shard_map/all_to_all | solution.py:418
  129.9 20.5 %all_to_all.45 = bf16[32,32,256]{2,1,0:T(8,128)(2,1)S(1)} all-to-all(bf16[32,32,256]{2,1,0:T(8,128)(2,1)S(1)} %get-tuple-element.17), channel_id=1, replica_groups=mesh['dp'=32,'tp'=8] {'dp'}, dimensions={0} | all-to-all | bytes 1048576 | tf_op jit(solution)/shard_map/all_to_all | solution.py:418
  150.5 2.4 %gate_up.1 = bf16[8,160,256]{2,1,0:T(8,128)(2,1)S(1)} custom-call(bf16[8,144,1024]{2,1,0:T(8,128)(2,1)S(1)} %all-to-all-done.1.w_ref, bf16[1024,256]{1,0:T(8,128)(2,1)S(1)} %bitcast.18), custom_call_target="tpu_custom_call" | custom-call | flops 603979776 | bytes 2883584 | tf_op jit(solution)/shard_map/gate_up/pallas_call | solution.py:352
  152.9 16.6 %all_to_all.46.part_ref = bf16[8,160,256]{2,1,0:T(8,128)(2,1)S(1)} all-to-all(bf16[8,160,256]{2,1,0:T(8,128)(2,1)S(1)} %gate_up.1), channel_id=1, replica_groups=mesh['dp'=32,'tp'=8] {'tp'}, dimensions={0} | all-to-all | bytes 1310720 | tf_op jit(solution)/shard_map/all_to_all | solution.py:418
  169.5 4.3 %all-to-all-start = ((bf16[8,80,1024]{2,1,0:T(8,128)(2,1)}), bf16[8,80,1024]{2,1,0:T(8,128)(2,1)S(1)}, u32[]{:S(2)}, u32[]{:S(2)}) async-start(bf16[8,80,1024]{2,1,0:T(8,128)(2,1)} %copy-done.4), calls=%async_computation | async-start | bytes 2621440 | tf_op jit(solution)/shard_map/all_to_all | solution.py:418
  173.8 0.8 activate.1
  174.7 17.1 %all-to-all-done = bf16[8,80,1024]{2,1,0:T(8,128)(2,1)S(1)} async-done(((bf16[8,80,1024]{2,1,0:T(8,128)(2,1)}), bf16[8,80,1024]{2,1,0:T(8,128)(2,1)S(1)}, u32[]{:S(2)}, u32[]{:S(2)}) %all-to-all-start) | async-done | bytes 1310752 | tf_op jit(solution)/shard_map/all_to_all | solution.py:418
  191.8 4.2 %all-to-all-start.7 = ((bf16[8,80,256]{2,1,0:T(8,128)(2,1)}), bf16[8,80,256]{2,1,0:T(8,128)(2,1)S(1)}, u32[]{:S(2)}, u32[]{:S(2)}) async-start(bf16[8,80,256]{2,1,0:T(8,128)(2,1)} %activate.1), calls=%async_computation.7 | async-start | bytes 655360 | tf_op jit(solution)/shard_map/all_to_all | solution.py:418
  196.0 1.4 turn.1.w_ref
  197.4 5.7 %all-to-all-done.7 = bf16[8,80,256]{2,1,0:T(8,128)(2,1)S(1)} async-done(((bf16[8,80,256]{2,1,0:T(8,128)(2,1)}), bf16[8,80,256]{2,1,0:T(8,128)(2,1)S(1)}, u32[]{:S(2)}, u32[]{:S(2)}) %all-to-all-start.7) | async-done | bytes 327712 | tf_op jit(solution)/shard_map/all_to_all | solution.py:418
  203.1 1.1 down.1
  204.2 19.4 %all_to_all.47.part_ref = bf16[32,32,256]{2,1,0:T(8,128)(2,1)S(1)} all-to-all(bf16[32,32,256]{2,1,0:T(8,128)(2,1)S(1)} %down.1), channel_id=1, replica_groups=mesh['dp'=32,'tp'=8] {'dp'}, dimensions={0} | all-to-all | bytes 1048576 | tf_op jit(solution)/shard_map/all_to_all | solution.py:418
  223.6 0.2 finish.1
  223.9 0.7 copy.40
  (9 shorter events, 0.0 us)
Async XLA Ops:
  0.0 17.5 %copy-start.13 = (s32[32,4]{0,1:T(4,128)S(1)}, s32[32,4]{0,1:T(4,128)}, u32[]{:S(2)}) copy-start(s32[32,4]{0,1:T(4,128)} %param.16) | copy-start | bytes 1540
  3.2 0.7 copy-start.7
  5.5 30.7 %all-to-all-start.2 = ((bf16[32,16,576]{2,1,0:T(8,128)(2,1)}), bf16[32,16,576]{2,1,0:T(8,128)(2,1)S(1)}, u32[]{:S(2)}, u32[]{:S(2)}) async-start(bf16[32,16,576]{2,1,0:T(8,128)(2,1)} %bitcast.3), calls=%async_computation.2 | async-start | bytes 1310720 | tf_op jit(solution)/shard_map/all_to_all | solution.py:418
  17.7 7.8 %copy-start.12 = (bf16[2,4,576]{2,1,0:T(4,128)(2,1)S(1)}, bf16[2,4,576]{2,1,0:T(4,128)(2,1)}, u32[]{:S(2)}) copy-start(bf16[2,4,576]{2,1,0:T(4,128)(2,1)} %param.20) | copy-start | bytes 27652
  17.7 7.8 %copy-start.6 = (bf16[2,4,16,576]{3,2,1,0:T(8,128)(2,1)S(1)}, bf16[2,4,16,576]{3,2,1,0:T(8,128)(2,1)}, u32[]{:S(2)}) copy-start(bf16[2,4,16,576]{3,2,1,0:T(8,128)(2,1)} %q_ref.3) | copy-start | bytes 442372
  17.8 7.8 %copy-start.8 = (s32[4]{0:T(128)S(1)}, s32[4]{0:T(128)}, u32[]{:S(2)}) copy-start(s32[4]{0:T(128)} %ctx_ref.1) | copy-start | bytes 52
  25.6 2.5 %copy-start = (bf16[4,1024,576]{2,1,0:T(8,128)(2,1)S(1)}, bf16[4,1024,576]{2,1,0:T(8,128)(2,1)}, u32[]{:S(2)}) copy-start(bf16[4,1024,576]{2,1,0:T(8,128)(2,1)} %copy.37.kv_ref) | copy-start | bytes 14155780
  28.1 8.2 %copy-start.3 = (bf16[16,512,128]{2,1,0:T(8,128)(2,1)S(1)}, bf16[16,512,128]{2,1,0:T(8,128)(2,1)}, u32[]{:S(2)}) copy-start(bf16[16,512,128]{2,1,0:T(8,128)(2,1)} %uv_ref.1) | copy-start | bytes 6291460
  39.4 6.2 %copy-start.10 = (bf16[16,128,224]{1,2,0:T(8,128)(2,1)S(1)}, bf16[16,128,224]{1,2,0:T(8,128)(2,1)}, u32[]{:S(2)}) copy-start(bf16[16,128,224]{1,2,0:T(8,128)(2,1)} %param.22) | copy-start | bytes 2752516
  39.4 31.9 %all-to-all-start.3 = ((bf16[32,8,2048]{2,1,0:T(8,128)(2,1)}), bf16[32,8,2048]{2,1,0:T(8,128)(2,1)S(1)}, u32[]{:S(2)}, u32[]{:S(2)}) async-start(bf16[32,8,2048]{2,1,0:T(8,128)(2,1)} %attend_new.1), calls=%async_computation.3 | async-start | bytes 2097152 | tf_op jit(solution)/shard_map/all_to_all | solution.py:418
  49.5 30.5 %copy-start.9 = (bf16[7168,72]{0,1:T(8,128)(2,1)S(1)}, bf16[7168,72]{0,1:T(8,128)(2,1)}, u32[]{:S(2)}) copy-start(bf16[7168,72]{0,1:T(8,128)(2,1)} %param.25) | copy-start | bytes 3096580
  72.3 23.5 %all-to-all-start.4 = ((bf16[8,32,256]{2,1,0:T(8,128)(2,1)}), bf16[8,32,256]{2,1,0:T(8,128)(2,1)S(1)}, u32[]{:S(2)}, u32[]{:S(2)}) async-start(bf16[8,32,256]{2,1,0:T(8,128)(2,1)} %project.1), calls=%async_computation.4 | async-start | bytes 262144 | tf_op jit(solution)/shard_map/all_to_all | solution.py:418
  81.0 2.7 %copy-start.5 = (bf16[72,7168]{1,0:T(8,128)(2,1)S(1)}, bf16[72,7168]{1,0:T(8,128)(2,1)}, u32[]{:S(2)}) copy-start(bf16[72,7168]{1,0:T(8,128)(2,1)} %wd_ref.1) | copy-start | bytes 3096580
  83.7 1.5 copy-start.1
  93.3 1.4 copy-start.2
  94.8 1.1 copy-start.4
  95.8 5.8 %copy-start.11 = (bf16[2,128,28]{1,0,2:T(2,128)(2,1)S(1)}, bf16[2,128,28]{1,0,2:T(2,128)(2,1)}, u32[]{:S(2)}) copy-start(bf16[2,128,28]{1,0,2:T(2,128)(2,1)} %param.23) | copy-start | bytes 43012
  95.8 34.1 %all-to-all-start.1 = ((bf16[8,144,1024]{2,1,0:T(8,128)(2,1)}), bf16[8,144,1024]{2,1,0:T(8,128)(2,1)S(1)}, u32[]{:S(2)}, u32[]{:S(2)}) async-start(bf16[8,144,1024]{2,1,0:T(8,128)(2,1)} %copy-done.2), calls=%async_computation.1 | async-start | bytes 4718592 | tf_op jit(solution)/shard_map/all_to_all | solution.py:418
  169.5 22.3 %all-to-all-start = ((bf16[8,80,1024]{2,1,0:T(8,128)(2,1)}), bf16[8,80,1024]{2,1,0:T(8,128)(2,1)S(1)}, u32[]{:S(2)}, u32[]{:S(2)}) async-start(bf16[8,80,1024]{2,1,0:T(8,128)(2,1)} %copy-done.4), calls=%async_computation | async-start | bytes 2621440 | tf_op jit(solution)/shard_map/all_to_all | solution.py:418
  191.8 11.3 %all-to-all-start.7 = ((bf16[8,80,256]{2,1,0:T(8,128)(2,1)}), bf16[8,80,256]{2,1,0:T(8,128)(2,1)S(1)}, u32[]{:S(2)}, u32[]{:S(2)}) async-start(bf16[8,80,256]{2,1,0:T(8,128)(2,1)} %activate.1), calls=%async_computation.7 | async-start | bytes 655360 | tf_op jit(solution)/shard_map/all_to_all | solution.py:418

commit v2 on v1

v2 whole, which is shorter than its diff:
```python
import functools

import jax
import jax.numpy as jnp
from jax import lax
from jax.experimental import pallas as pl
from jax.experimental.pallas import tpu as pltpu
from jax.sharding import PartitionSpec as P

LAT = 512
QKD = 192
OWN_TOK = 16
PAD = 32
GROUP = 4

masked_score = -1e30
norm_eps = 1e-06
bf16, f32, i32 = jnp.bfloat16, jnp.float32, jnp.int32

NT = (((1,), (1,)), ((), ()))
NN = (((1,), (0,)), ((), ()))


def dot(a, b, dims=NN):
    return lax.dot_general(a, b, dims, preferred_element_type=f32)


def iota(shape, dim):
    return lax.broadcasted_iota(i32, shape, dim)


def call(body, out_shape, cost=(0, 0), mib=16, **kwargs):
    return pl.pallas_call(
        body,
        out_shape=out_shape,
        compiler_params=pltpu.CompilerParams(vmem_limit_bytes=mib * 1024 * 1024),
        cost_estimate=pl.CostEstimate(flops=cost[0], bytes_accessed=cost[1], transcendentals=0),
        **kwargs,
    )


def in_hbm(x):
    return pltpu.with_memory_space_constraint(x, pltpu.HBM)


def share_picker(tp, width):
    shape = (tp * PAD, tp * width)
    row = iota(shape, 0)
    place = row % PAD
    wanted = (row // PAD) * width + place
    return jnp.where((iota(shape, 1) == wanted) & (place < width), 1.0, 0.0).astype(bf16)


def partner(rank, tp, k, sign):
    x = (rank // 2 + sign * (k // 2) + tp // 2) % (tp // 2)
    return 2 * x + ((rank % 2) ^ (k % 2))


def token_picker(dp, per_owner, steps):
    total = dp * per_owner * steps
    shape = (total, total)
    row = iota(shape, 0)
    step, request = row // (dp * per_owner), row % (dp * per_owner)
    wanted = request * steps + step
    return jnp.where(iota(shape, 1) == wanted, 1.0, 0.0).astype(bf16)


def route_kernel(slot_ref, len_ref, rows_ref, out_ref):
    count = slot_ref.shape[1]
    per_owner, owners = len_ref.shape
    total = rows_ref.shape[1]
    square = (count, count)
    sub, lane = iota(square, 0), iota(square, 1)
    slot_row = slot_ref[...]
    spread = jnp.where(iota((owners, count), 1) // per_owner == iota((owners, count), 0), 1.0, 0.0)
    wide = dot(len_ref[...].astype(f32).astype(bf16), spread.astype(bf16))
    own = iota(wide.shape, 1) % per_owner == iota(wide.shape, 0)
    len_row = jnp.sum(jnp.where(own, wide, 0.0), axis=0, keepdims=True).astype(i32)
    len_col = jnp.sum(jnp.where(sub == lane, len_row, 0), axis=1, keepdims=True)
    slot_col = jnp.sum(jnp.where(sub == lane, slot_row, 0), axis=1, keepdims=True)
    hot = slot_col == lane
    hot_t = sub == slot_row
    rows_col = jnp.sum(jnp.where(hot, len_row, 0), axis=1, keepdims=True)
    rows_row = jnp.sum(jnp.where(hot_t, len_col, 0), axis=0, keepdims=True)
    owner_start = jnp.sum(jnp.where(sub < lane, len_col, 0), axis=0, keepdims=True)
    start_col = jnp.sum(jnp.where(lane < sub, rows_row, 0), axis=1, keepdims=True)
    target_col = jnp.sum(jnp.where(hot, owner_start, 0), axis=1, keepdims=True)
    at = iota((count, total), 1)
    inside = (at >= start_col) & (at < start_col + rows_col)
    shift = jnp.sum(jnp.where(inside, target_col - start_col, 0), axis=0, keepdims=True)
    target = iota((1, total), 1) + shift
    pick = jnp.where(iota((total, total), 0) == target, 1.0, 0.0).astype(bf16)
    out_ref[...] = dot(pick, rows_ref[...], NT).astype(bf16)


def route(request_slot, new_lengths, prefill_latent):
    total, width = prefill_latent.shape
    return call(
        route_kernel,
        jax.ShapeDtypeStruct((total, width), bf16),
        (2 * total * total * width, 4 * total * width),
        grid=(1,),
        in_specs=[
            pl.BlockSpec((1, request_slot.size), lambda c: (0, 0)),
            pl.BlockSpec(new_lengths.shape[::-1], lambda c: (0, 0)),
            pl.BlockSpec((width, total), lambda c: (0, 0)),
        ],
        out_specs=pl.BlockSpec((total, width), lambda c: (0, 0)),
        name="route",
    )(in_hbm(request_slot.reshape(1, -1)), in_hbm(new_lengths.T), in_hbm(prefill_latent.T))


def piece_places(tp):
    arrays = [(0,), (1,), (2, 3), (6, 7), (4,), (5,)]
    arrays = [[k for k in ks if k < tp] for ks in arrays]
    arrays = [ks for ks in arrays if ks]
    return {k: (n, at) for n, ks in enumerate(arrays) for at, k in enumerate(ks)}


def reshard_kernel(tp, width, rank_ref, wg_ref, wu_ref, wd_ref, *refs):
    *outs, all_scr, sorted_scr = refs
    block = tp * width
    units = wg_ref.shape[0]
    picker = share_picker(tp, width)
    lanes = GROUP * PAD
    all_scr[3 * units :, :] = jnp.zeros((all_scr.shape[0] - 3 * units, all_scr.shape[1]), bf16)
    for n, w_ref in enumerate((wg_ref, wu_ref, wd_ref)):
        all_scr[n * units : (n + 1) * units, :] = w_ref[...]
    places = piece_places(tp)
    for u in range(outs[0].shape[1]):
        picked = [
            dot(all_scr[:, i * block : (i + 1) * block], picker, NT).astype(bf16)
            for i in range(u * GROUP, (u + 1) * GROUP)
        ]
        for j in range(tp):
            part = [value[:, j * PAD : (j + 1) * PAD] for value in picked]
            sorted_scr[u, :, j * lanes : (j + 1) * lanes] = jnp.concatenate(part, axis=1)
        for k in range(tp):
            first = pl.multiple_of(partner(rank_ref[0], tp, k, 1) * lanes, lanes)
            array, at = places[k]
            outs[array][at, u] = sorted_scr[u, :, pl.ds(first, lanes)]


def reshard(rank, w_gate, w_up, w_down, dp, tp, width, unit_pad):
    units = w_gate.shape[1]
    count = dp // GROUP
    each = count // 2 if count % 2 == 0 else count
    block = tp * width * GROUP * each
    lanes = GROUP * PAD
    rows = 2 * units + unit_pad
    w_spec = pl.BlockSpec((units, block), lambda c: (0, c))
    places = piece_places(tp)
    owners = [n for n, _ in places.values()]
    sizes = [owners.count(n) for n in range(max(owners) + 1)]
    return call(
        functools.partial(reshard_kernel, tp, width),
        tuple(pltpu.HBM((size, count, rows, lanes), bf16) for size in sizes),
        (2 * 3 * dp * tp * PAD * tp * width * units, 14 * w_gate.size),
        grid=(count // each,),
        in_specs=[pl.BlockSpec(memory_space=pltpu.SMEM), w_spec, w_spec, w_spec],
        out_specs=tuple(
            pl.BlockSpec((size, each, rows, lanes), lambda c: (0, c, 0, 0)) for size in sizes
        ),
        scratch_shapes=[
            pltpu.VMEM((rows, block), bf16),
            pltpu.VMEM((each, rows, tp * lanes), bf16),
        ],
        name="reshard",
        mib=24,
    )(rank, in_hbm(w_gate.T), in_hbm(w_up.T), in_hbm(w_down))


def turn_kernel(first, *refs):
    _, count, _, lanes = refs[0].shape
    eye = jnp.where(iota((lanes, lanes), 0) == iota((lanes, lanes), 1), 1.0, 0.0).astype(bf16)
    for c in range(count):
        x = jnp.concatenate([ref[0, c, first:, :] for ref in refs[:-1]], axis=0)
        refs[-1][c * lanes : (c + 1) * lanes, :] = dot(eye, x, NT).astype(bf16)


def turn(pieces, first):
    _, count, rows, lanes = pieces[0][0].shape
    depth = len(pieces) * (rows - first)
    each = 4 if count % 4 == 0 else 1
    return call(
        functools.partial(turn_kernel, first),
        jax.ShapeDtypeStruct((count * lanes, depth), bf16),
        (2 * lanes * lanes * depth * count, 4 * depth * lanes * count),
        grid=(count // each,),
        in_specs=[
            pl.BlockSpec((1, each, rows, lanes), lambda c, at=at: (at, c, 0, 0)) for _, at in pieces
        ],
        out_specs=pl.BlockSpec((each * lanes, depth), lambda c: (c, 0)),
        name="turn",
    )(*[in_hbm(array) for array, _ in pieces])


def hidden_kernel(dp, per_owner, steps, h_ref, out_ref):
    width = h_ref.shape[0]
    eye = jnp.where(iota((PAD, width), 0) == iota((PAD, width), 1), 1.0, 0.0).astype(bf16)
    placed = dot(h_ref[...], token_picker(dp, per_owner, steps)).astype(bf16)
    out_ref[...] = dot(eye, placed)


def cache_kernel(ctx_ref, q_ref, kv_ref, tok_ref, acc_ref, side_ref):
    at = pl.program_id(0)
    scale = QKD ** (-0.5)
    steps, _, heads, width = q_ref.shape
    rows = steps * heads
    query = q_ref[...].reshape(rows, width)
    keys = kv_ref[0]
    toks = tok_ref[0]
    scores = dot(query, keys) * scale
    scores = jnp.where(iota(scores.shape, 1) < ctx_ref[at], scores, masked_score)
    fresh = dot(query, toks, NT) * scale
    step = iota(fresh.shape, 0) // heads
    fresh = jnp.where(iota(fresh.shape, 1) <= step, fresh, masked_score)
    top = jnp.maximum(
        jnp.max(scores, axis=1, keepdims=True), jnp.max(fresh, axis=1, keepdims=True)
    )
    scores = jnp.exp(scores - top)
    fresh = jnp.exp(fresh - top)
    total = jnp.sum(scores, axis=1, keepdims=True) + jnp.sum(fresh, axis=1, keepdims=True)
    acc_ref[0] = dot(scores.astype(bf16), keys[:LAT], NT) + dot(fresh.astype(bf16), toks[:, :LAT])
    side_ref[0] = jnp.where(iota(side_ref.shape[1:], 1) == 0, top, total)


def attend_cache(ctx_lengths, queries, kv_cache, tokens):
    steps, per_owner, heads, width = queries.shape
    keys = kv_cache.shape[2]
    rows = steps * heads
    side_spec = pl.BlockSpec((1, rows, 128), lambda q: (q, 0, 0))
    return call(
        cache_kernel,
        (pltpu.HBM((per_owner, rows, LAT), f32), pltpu.HBM((per_owner, rows, 128), f32)),
        (2 * per_owner * rows * keys * (width + LAT), 2 * kv_cache.size),
        grid=(per_owner,),
        in_specs=[
            pl.BlockSpec(memory_space=pltpu.SMEM),
            pl.BlockSpec((steps, 1, heads, width), lambda q: (0, q, 0, 0)),
            pl.BlockSpec((1, width, keys), lambda q: (q, 0, 0)),
            pl.BlockSpec((1, tokens.shape[1], width), lambda q: (q, 0, 0)),
        ],
        out_specs=(pl.BlockSpec((1, rows, LAT), lambda q: (q, 0, 0)), side_spec),
        name="attend_cache",
    )(ctx_lengths, queries, kv_cache, tokens)


def merge_kernel(len_ref, q_ref, new_ref, acc_ref, side_ref, uv_ref, out_ref):
    scale = QKD ** (-0.5)
    steps, per_owner, heads, width = q_ref.shape
    rows = steps * heads
    new = new_ref[...]
    query = jnp.concatenate([q_ref[:, q].reshape(rows, width) for q in range(per_owner)], axis=0)
    scores = dot(query, new, NT) * scale
    place = iota(scores.shape, 1) % OWN_TOK
    owner_row = iota(scores.shape, 0) // rows
    first = jnp.zeros(scores.shape, i32)
    last = jnp.zeros(scores.shape, i32)
    start = jnp.int32(0)
    for q in range(per_owner):
        end = start + len_ref[q]
        first = jnp.where(owner_row == q, start, first)
        last = jnp.where(owner_row == q, end, last)
        start = end
    scores = jnp.where((place >= first) & (place < last), scores, masked_score)
    total_rows = per_owner * rows
    side = side_ref[...].reshape(total_rows, 128)
    old_top, old_sum = side[:, :1], side[:, 1:2]
    top = jnp.maximum(jnp.max(scores, axis=1, keepdims=True), old_top)
    scores = jnp.exp(scores - top)
    weight = jnp.exp(old_top - top)
    total = jnp.sum(scores, axis=1, keepdims=True) + old_sum * weight
    acc = acc_ref[...].reshape(total_rows, LAT) * weight + dot(scores.astype(bf16), new[:, :LAT])
    latent = (acc / total).astype(bf16)
    values = uv_ref.shape[2]
    groups = per_owner * steps
    head_of = iota((groups, heads, values), 1)
    for h in range(heads):
        full = dot(latent, uv_ref[h]).reshape(groups, heads, values)
        mine = jnp.sum(jnp.where(head_of == h, full, 0.0), axis=1).astype(bf16)
        each = out_ref.shape[3] // values
        place = (h % each) * values
        out_ref[:, h // each, :, place : place + values] = jnp.broadcast_to(
            mine[None], (out_ref.shape[0], groups, values)
        )


def attend_new(my_lengths, queries, new_rows, acc, side, w_uv, dp, parts):
    steps, per_owner, heads, _ = queries.shape
    whole = pl.BlockSpec(memory_space=pltpu.VMEM)
    return call(
        merge_kernel,
        jax.ShapeDtypeStruct(
            (dp // parts, parts, per_owner * steps, heads // parts * w_uv.shape[2]), bf16
        ),
        (4 * new_rows.size * per_owner * steps * heads, 2 * w_uv.size),
        grid=(1,),
        in_specs=[
            pl.BlockSpec(memory_space=pltpu.SMEM),
            whole,
            whole,
            pl.BlockSpec(acc.shape, lambda c: (0, 0, 0)),
            pl.BlockSpec(side.shape, lambda c: (0, 0, 0)),
            whole,
        ],
        out_specs=whole,
        name="attend_new",
    )(my_lengths, queries, new_rows, in_hbm(acc), in_hbm(side), w_uv)


def project_kernel(rank_ref, x_ref, *refs):
    out_ref = refs[-1]
    ring, tp = out_ref.shape[:2]
    x = x_ref[...].T
    for k, w_ref in enumerate(refs[:-1]):
        heads, columns, _ = w_ref.shape
        width = columns // tp
        weights = jnp.concatenate([w_ref[h] for h in range(heads)], axis=1)
        value = dot(weights, x)
        spare = jnp.zeros((PAD - width, value.shape[1]), f32)
        target = (rank_ref[0] + ring - k) % ring
        for j in range(tp):
            part = jnp.concatenate([value[j * width : (j + 1) * width], spare], axis=0)
            out_ref[target, j] = part.astype(bf16)


def project(rank, pieces, every, tp):
    heads, features, values = pieces[0].shape
    ring, columns = len(pieces), every.shape[0]
    size = ring * heads * features * values
    return call(
        project_kernel,
        jax.ShapeDtypeStruct((ring, tp, PAD, columns), bf16),
        (2 * size * columns, 2 * (size + every.size)),
        grid=(1,),
        in_specs=[
            pl.BlockSpec(memory_space=pltpu.SMEM),
            pl.BlockSpec(every.shape, lambda c: (0, 0)),
        ]
        + [pl.BlockSpec((heads, features, values), lambda c: (0, 0, 0))] * ring,
        out_specs=pl.BlockSpec((ring, tp, PAD, columns), lambda c: (0, 0, 0, 0)),
        name="project",
    )(rank, every, *[in_hbm(piece) for piece in pieces])


def split_sum(value):
    high = value.astype(bf16).astype(f32)
    return high, value - high


def mixed_kernel(width, part_ref, hidden_ref, gain_ref, mixed_ref, out_ref):
    mixed = jnp.sum(part_ref[...].astype(f32), axis=0) + hidden_ref[...]
    mixed_ref[...] = mixed
    high, low = split_sum(jnp.sum(mixed * mixed, axis=0, keepdims=True))
    row = iota(mixed.shape, 0)
    sent = jnp.where(row == width, high, jnp.where(row == width + 1, low, mixed * gain_ref[...]))
    out_ref[...] = jnp.broadcast_to(sent.astype(bf16)[None], out_ref.shape)


def make_mixed(parts, hidden_t, gain, dp, width):
    _, rows, columns = parts.shape
    return call(
        functools.partial(mixed_kernel, width),
        (
            jax.ShapeDtypeStruct((rows, columns), f32),
            jax.ShapeDtypeStruct((dp, rows, columns), bf16),
        ),
        (parts.size, 4 * parts.size),
        name="make_mixed",
    )(parts, hidden_t, gain)


def gate_kernel(width, rank_ref, x_ref, *refs):
    out_ref = refs[-1]
    units = out_ref.shape[1] - 16
    x = x_ref[...]
    depth = x.shape[0]
    place = iota((16, depth), 1) % PAD
    pick = jnp.where((place == width) | (place == width + 1), 1.0, 0.0).astype(bf16)
    squares = dot(pick, x)
    high, low = split_sum(squares)
    row = iota(squares.shape, 0)
    tail = jnp.where(row == 0, high, jnp.where(row == 1, low, 0.0)).astype(bf16)
    for k, w_ref in enumerate(refs[:-1]):
        target = partner(rank_ref[0], len(refs) - 1, k, -1)
        weights = jnp.concatenate([w_ref[0, c] for c in range(w_ref.shape[1])], axis=1)
        out_ref[target, :units, :] = dot(weights, x).astype(bf16)
        out_ref[target, units:, :] = tail


def gate_up(rank, pieces, x, units, width):
    tp, columns = len(pieces), x.shape[1]
    _, count, _, lanes = pieces[0][0].shape
    size = tp * units * x.shape[0]
    out_shape = (tp, units + 16, columns)
    return call(
        functools.partial(gate_kernel, width),
        jax.ShapeDtypeStruct(out_shape, bf16),
        (2 * size * columns, 2 * size + 2 * x.size),
        grid=(1,),
        in_specs=[
            pl.BlockSpec(memory_space=pltpu.SMEM),
            pl.BlockSpec(x.shape, lambda c: (0, 0)),
        ]
        + [
            pl.BlockSpec((1, count, units, lanes), lambda c, at=at: (at, 0, 0, 0)) for _, at in pieces
        ],
        out_specs=pl.BlockSpec(out_shape, lambda c: (0, 0, 0)),
        name="gate_up",
    )(rank, x, *[in_hbm(array) for array, _ in pieces])


def activate_kernel(model_width, units, part_ref, out_ref):
    sums = jnp.sum(part_ref[...].astype(f32), axis=0)
    squares = sums[2 * units : 2 * units + 1] + sums[2 * units + 1 : 2 * units + 2]
    factor = lax.rsqrt(squares / model_width + norm_eps)
    gate = sums[:units] * factor
    up = sums[units : 2 * units] * factor
    value = gate / (1.0 + jnp.exp(-gate)) * up
    spare = out_ref.shape[1] - units
    if spare:
        value = jnp.concatenate([value, jnp.zeros((spare, value.shape[1]), f32)], axis=0)
    out_ref[...] = jnp.broadcast_to(value.astype(bf16)[None], out_ref.shape)


def activate(parts, model_width, units, unit_pad):
    tp, _, columns = parts.shape
    return call(
        functools.partial(activate_kernel, model_width, units),
        jax.ShapeDtypeStruct((tp, unit_pad, columns), bf16),
        (10 * parts.size, 4 * parts.size),
        name="activate",
    )(parts)


def down_kernel(rank_ref, w_ref, x_ref, out_ref):
    tp = x_ref.shape[0]
    x = jnp.concatenate([x_ref[partner(rank_ref[0], tp, k, -1)] for k in range(tp)], axis=0)
    out_ref[...] = dot(w_ref[...], x).astype(bf16).reshape(out_ref.shape)


def down(rank, turned, x, dp):
    rows, depth = turned.shape
    columns = x.shape[2]
    block = 256 if rows % 256 == 0 else 128
    return call(
        down_kernel,
        jax.ShapeDtypeStruct((dp, PAD, columns), bf16),
        (2 * turned.size * columns, 2 * turned.size + 2 * x.size),
        grid=(rows // block,),
        in_specs=[
            pl.BlockSpec(memory_space=pltpu.SMEM),
            pl.BlockSpec((block, depth), lambda c: (c, 0)),
            pl.BlockSpec(x.shape, lambda c: (0, 0, 0)),
        ],
        out_specs=pl.BlockSpec((block // PAD, PAD, columns), lambda c: (c, 0, 0)),
        name="down",
    )(rank, turned, x)


def finish_kernel(dp, per_owner, steps, part_ref, mixed_ref, out_ref):
    value = jnp.sum(part_ref[...].astype(f32), axis=0) + mixed_ref[...]
    picked = dot(value.astype(bf16), token_picker(dp, per_owner, steps), NT)
    picked = picked[: out_ref.shape[0]].astype(bf16)
    each = out_ref.shape[2]
    for s in range(steps):
        out_ref[:, s, :] = picked[:, s * each : (s + 1) * each]


def exchange(x, axis):
    return lax.all_to_all(x, axis, split_axis=0, concat_axis=0, tiled=True)


def shards(
    prefill_latent,
    request_slot,
    new_lengths,
    ctx_lengths,
    kv_cache,
    queries,
    step_latents,
    w_uv,
    w_out,
    hidden,
    ffn_gain,
    w_gate,
    w_up,
    w_down,
):
    both = ("z", "y")
    ring = lax.axis_size("y")
    dp, tp = lax.axis_size("z") * ring, lax.axis_size("tp")
    dp_rank, tp_rank = lax.axis_index(both), lax.axis_index("tp")
    steps, per_owner = queries.shape[:2]
    width = hidden.shape[2]
    model_width = width * dp * tp
    units = w_gate.shape[1]
    unit_pad = -(-units // 16) * 16
    total = hidden.shape[0] * hidden.shape[1]

    routed = route(request_slot, new_lengths, prefill_latent)
    incoming = exchange(routed.reshape(dp, OWN_TOK, -1), both).reshape(dp * OWN_TOK, -1)

    rank = tp_rank.astype(i32).reshape(1)
    arrays = reshard(rank, w_gate, w_up, w_down, dp, tp, width, unit_pad)

    ctx_lengths, _ = lax.optimization_barrier((ctx_lengths, arrays[0]))
    tokens = jnp.pad(step_latents.transpose(1, 0, 2), ((0, 0), (0, 16 - steps), (0, 0)))
    acc, side = attend_cache(
        ctx_lengths, queries, in_hbm(kv_cache.transpose(0, 2, 1)), tokens
    )
    my_lengths = lax.dynamic_index_in_dim(new_lengths, dp_rank, 0, keepdims=False)
    heads_out = attend_new(my_lengths, queries, incoming, acc, side, w_uv, dp, ring)
    every = exchange(heads_out.reshape((dp,) + heads_out.shape[2:]), both).reshape(total, -1)

    def along_x(piece, k, sign):
        return lax.ppermute(piece, "tp", [(j, partner(j, tp, k, sign)) for j in range(tp)])

    y_rank = lax.axis_index("y").astype(i32).reshape(1)
    each = w_out.shape[0] // ring
    w_turned = w_out.transpose(0, 2, 1)
    out_pieces = [
        lax.dynamic_slice_in_dim(w_turned, (y_rank[0] + k) % ring * each, each, 0)
        for k in range(ring)
    ]
    for k in range(1, ring):
        pairs = [(j, (j + k) % ring) for j in range(ring)]
        out_pieces[k] = lax.ppermute(out_pieces[k], "y", pairs)
    pieces = {k: (arrays[n], at) for k, (n, at) in piece_places(tp).items()}
    if tp > 2:
        plus, minus = along_x(arrays[2], 2, 1), along_x(arrays[3], 2, -1)
        far, _ = lax.optimization_barrier((arrays[4:6], (plus, minus)))
        far = [along_x(far[0], 2, 1), along_x(far[1], 2, -1)]
        every, _ = lax.optimization_barrier((every, (plus, minus, far)))
    parts = project(y_rank, out_pieces, every, tp)
    parts = exchange(parts.reshape((ring * tp,) + parts.shape[2:]), ("y", "tp"))
    if tp > 2:
        pieces[2], pieces[6] = (plus, 0), (minus, 0)
        pieces[3] = along_x(plus[1:], 1, 1), 0
        pieces[7] = along_x(minus[1:], 1, 1), 0
        pieces[4] = along_x(far[0], 2, 1), 0
        pieces[5] = along_x(far[1], 3, -1), 0
    pieces[1] = along_x(arrays[1], 1, 1), 0
    pieces = [pieces[k] for k in range(tp)]
    hidden_t = call(
        functools.partial(hidden_kernel, dp, per_owner, steps),
        jax.ShapeDtypeStruct((PAD, total), f32),
        name="turn_hidden",
    )(hidden.transpose(2, 0, 1).reshape(width, total))
    gain = lax.dynamic_slice_in_dim(ffn_gain, (dp_rank * tp + tp_rank) * width, width)
    gain = jnp.pad(gain, (0, PAD - width)).reshape(PAD, 1)

    mixed, sent = make_mixed(parts, hidden_t, gain, dp, width)
    x = exchange(sent, both).reshape(dp * PAD, total)
    parts = exchange(gate_up(rank, pieces, x, 2 * units, width), "tp")
    act = exchange(activate(parts, model_width, units, unit_pad), "tp")
    turned_down = turn(pieces, 2 * units)
    parts = exchange(down(rank, turned_down, act, dp), both)
    out = call(
        functools.partial(finish_kernel, dp, per_owner, steps),
        jax.ShapeDtypeStruct((width, steps, total // steps), bf16),
        name="finish",
    )(parts, mixed)
    return out.transpose(1, 2, 0)


def solution(mesh):
    devices = mesh.devices
    ring = 2
    devices = devices.reshape(devices.shape[0] // ring, ring, devices.shape[1])
    dp, tp = ("z", "y"), "tp"
    every = ("z", "y", "tp")
    return jax.shard_map(
        shards,
        mesh=jax.sharding.Mesh(devices, every),
        in_specs=(
            P(dp, None),
            P(),
            P(),
            P(dp),
            P(dp, None, None),
            P(None, dp, tp, None),
            P(None, dp, None),
            P(tp, None, None),
            P(tp, None, dp),
            P(None, None, every),
            P(),
            P(None, every),
            P(None, every),
            P(every, None),
        ),
        out_specs=P(None, None, every),
        check_vma=False,
    )
```

time: 227 us -> 167 us (0.74)
  waiting for transfers between devices: 75.4 us -> 36.8 us
  local copies, waits for them, and re-layouts: 24.2 us -> 6.89 us
  blocking collectives: 56.6 us -> 40.2 us
  starting transfers between devices: 39.3 us -> 48.9 us
  Pallas kernels: 28.8 us -> 32.2 us
    all_to_all x6 -> x5, waiting for transfers between devices: 75.4 us -> 13.9 us  [exchange(): return lax.all_to_all(x, axis, split_axis=0, concat_axis=0, tiled=True)]
    ppermute x0 -> x10, waiting for transfers between devices: none -> 22.9 us  [the longest x9 17.7 us: along_x(): lax.ppermute(piece, 'tp', [(j, partner(j, tp, k, sign)) for j in range(tp)])]
    unnamed x36 -> x29, local copies, waits for them, and re-layouts: 21.5 us -> 1.75 us
    all_to_all x3 -> x2, blocking collectives: 56.6 us -> 40.2 us  [exchange(): return lax.all_to_all(x, axis, split_axis=0, concat_axis=0, tiled=True)]
    ppermute x0 -> x10, starting transfers between devices: none -> 11.2 us  [the longest x9 10.3 us: along_x(): lax.ppermute(piece, 'tp', [(j, partner(j, tp, k, sign)) for j in range(tp)])]
    all_to_all x6 -> x5, starting transfers between devices: 39.3 us -> 37.6 us  [exchange(): return lax.all_to_all(x, axis, split_axis=0, concat_axis=0, tiled=True)]
    pallas_call x7 -> x6, Pallas kernels: 24.6 us -> 25.2 us  [the longest x1 8.69 us: reshard(): call(functools.partial(reshard_kernel, tp, width), tuple((pltpu.HBM((size...]
  transfers between devices with their start and end apart: 6 -> 15, of which waited for: 5 -> 8; matrix products, arithmetic and copies ran while one was open for 6% -> 3% of each run, Pallas kernels for 9% -> 13%
where the time goes in v2:
time: 167 us; the launch traced here: 165 us
  starting transfers between devices  48.9 us (29%)
  blocking collectives  40.2 us (24%)
  waiting for transfers between devices  36.8 us (22%)
  Pallas kernels  32.2 us (19%)
  local copies, waits for them, and re-layouts  6.89 us (4%)
    all_to_all x2, blocking collectives, exchange(): return lax.all_to_all(x, axis, split_axis=0, concat_axis=0, tiled=True)  40.2 us
    all_to_all x5, starting transfers between devices, exchange(): return lax.all_to_all(x, axis, split_axis=0, concat_axis=0, tiled=True)  37.6 us
    ppermute x9, waiting for transfers between devices, along_x(): lax.ppermute(piece, 'tp', [(j, partner(j, tp, k, sign)) for j in range(tp)])  17.7 us
    all_to_all x5, waiting for transfers between devices, exchange(): return lax.all_to_all(x, axis, split_axis=0, concat_axis=0, tiled=True)  13.9 us
    ppermute x9, starting transfers between devices, along_x(): lax.ppermute(piece, 'tp', [(j, partner(j, tp, k, sign)) for j in range(tp)])  10.3 us
    pallas_call x1, Pallas kernels, reshard(): call(functools.partial(reshard_kernel, tp, width), tuple((pltpu.HBM((size...  8.69 us
    pallas_call x1, Pallas kernels, attend_cache(): call(cache_kernel, (pltpu.HBM((per_owner, rows, LAT), f32), pltpu.HBM((pe...  6 us
    ppermute x1, waiting for transfers between devices, shards(): out_pieces[k] = lax.ppermute(out_pieces[k], 'y', pairs)  5.26 us
  transfers between devices with their start and end apart: 15, of which 8 were waited for; matrix products, arithmetic and copies ran while one was open for 3% of the time, Pallas kernels for 13%

profile of v2, /device:TPU:1, one launch (start us, length us, event | category | flops | bytes accessed | tf_op | source)
XLA Modules:
  0.0 165.2 jit_solution(15227795110862689084)
XLA Ops:
  0.0 2.9 %route.1 = bf16[512,576]{1,0:T(8,128)(2,1)} custom-call(s32[1,128]{1,0:T(1,128)} %bitcast.40, s32[4,32]{1,0:T(4,128)} %bitcast.39, bf16[576,512]{1,0:T(8,128)(2,1)} %bitcast.35), custom_call_target="tpu_custom_call" | custom-call | flops 301989888 | bytes 1179648 | tf_op jit(solution)/shard_map/route/pallas_call | solution.py:98
  2.9 12.2 %all-to-all-start = ((bf16[32,16,576]{2,1,0:T(8,128)(2,1)}), bf16[32,16,576]{2,1,0:T(8,128)(2,1)S(1)}, u32[]{:S(2)}, u32[]{:S(2)}) async-start(bf16[32,16,576]{2,1,0:T(8,128)(2,1)} %bitcast.7), calls=%async_computation | async-start | bytes 1310720 | tf_op jit(solution)/shard_map/all_to_all | solution.py:472
  15.1 8.7 %reshard.1 = (bf16[1,8,224,128]{3,2,1,0:T(8,128)(2,1)}, bf16[1,8,224,128]{3,2,1,0:T(8,128)(2,1)}, bf16[2,8,224,128]{3,2,1,0:T(8,128)(2,1)}, bf16[2,8,224,128]{3,...) custom-call(s32[1]{0:T(128)} %bitcast.rank_ref, bf16[72,7168]{1,0:T(8,128)(2,1)} %bitcast.33, ...), custom_call_target="tpu_custom_call" | custom-call | flops 792723456 | bytes 7225344 | tf_op jit(solution)/shard_map/reshard/pallas_call | solution.py:155
  23.8 1.2 collective-permute-start.1
  25.0 1.5 collective-permute-start.3
  26.5 0.0 copy-done.11
  26.5 0.2 dynamic-slice_reduce_fusion.len_ref
  26.7 0.0 copy-done.10
  26.7 0.0 copy-done.1
  26.7 0.0 copy-done.2
  26.7 0.0 copy-start
  26.8 6.0 %attend_cache.1 = (f32[4,32,512]{2,1,0:T(8,128)}, f32[4,32,128]{2,1,0:T(8,128)}) custom-call(s32[4]{0:T(128)S(1)} %copy-done.2, bf16[2,4,16,576]{3,2,1,0:T(8,128)(2,1)S(1)} %copy-done.1, bf16[4,576,1024]{2,1,0:T(8,128)(2,1)} %bitcast.32, bf16[4,16,576]{2,1,0:T(8,128)(2,1)S(1)} %pad.8.tok_ref), custom_call_target="tpu_custom_call" | custom-call | flops 285212672 | bytes 4718592 | tf_op jit(solution)/shard_map/attend_cache/pallas_call | solution.py:233
  32.8 1.1 all-to-all-done
  33.8 0.0 copy-done
  33.8 3.2 %attend_new.1 = bf16[16,2,8,1024]{3,2,1,0:T(8,128)(2,1)} custom-call(s32[4]{0:T(128)S(1)} %dynamic-slice_reduce_fusion.len_ref, bf16[2,4,16,576]{3,2,1,0:T(8,128)(2,1)S(1)} %copy-done.1, bf16[512,576]{1,0:T(8,128)(2,1)S(1)} %bitcast.28, f32[4,32,512]{2,1,0:T(8,128)} %get-tuple-element.28.acc_ref, f32[4,32,128]{2,1,0:T(8,128)} %get-tuple-element.29.side_ref, ...), custom_call_target="tpu_custom_call" | custom-call | flops 150994944 | bytes 2097152 | tf_op jit(solution)/shard_map/attend_new/pallas_call | solution.py:292
  37.0 8.1 %all-to-all-start.1 = ((bf16[32,8,1024]{2,1,0:T(8,128)(2,1)}), bf16[32,8,1024]{2,1,0:T(8,128)(2,1)S(1)}, u32[]{:S(2)}, u32[]{:S(2)}) async-start(bf16[32,8,1024]{2,1,0:T(8,128)(2,1)} %bitcast.11), calls=%async_computation.1 | async-start | bytes 1048576 | tf_op jit(solution)/shard_map/all_to_all | solution.py:472
  45.2 0.0 copy-start.9
  45.2 1.0 collective-permute-done.1.refs_2_
  46.2 0.0 collective-permute-done.3.refs_6_
  46.2 0.9 collective-permute-start.4
  47.2 1.8 %collective-permute-start.6 = (bf16[1,8,224,128]{3,2,1,0:T(8,128)(2,1)}, bf16[1,8,224,128]{3,2,1,0:T(8,128)(2,1)}, u32[]{:S(2)}, u32[]{:S(2)}) collective-permute-start(bf16[1,8,224,128]{3,2,1,0:T(8,128)(2,1)} %get-tuple-element.26), channel_id=1, source_target_pairs={{0,6},{1,7},{2,0},{3,1},{4,2},{5,3},{6,4},{7,5},{8,14},{9,15},{10,... | collective-permute-start | bytes 1376264 | tf_op jit(solution)/shard_map/ppermute | solution.py:518
  48.9 2.0 %dynamic-slice_bitcast_fusion = (bf16[8,224,128]{2,1,0:T(8,128)(2,1)S(1)}, bf16[8,224,128]{2,1,0:T(8,128)(2,1)}) fusion(bf16[16,128,224]{1,2,0:T(8,128)(2,1)} %param.22, s32[]{:T(128)S(6)} %select_n.28, s32[]{:T(128)S(6)} %select_n.26), kind=kLoop, calls=%fused_computation | loop fusion | bytes 1835016 | tf_op jit(solution)/shard_map/dynamic_slice | solution.py:524
  50.9 0.9 collective-permute-start.9
  51.8 6.1 %collective-permute-done.4 = bf16[1,8,224,128]{3,2,1,0:T(8,128)(2,1)} collective-permute-done((bf16[1,8,224,128]{3,2,1,0:T(8,128)(2,1)}, bf16[1,8,224,128]{3,2,1,0:T(8,128)(2,1)}, u32[]{:S(2)}, u32[]{:S(2)}) %collective-permute-start.4) | collective-permute-done | bytes 458784 | tf_op jit(solution)/shard_map/ppermute | solution.py:518
  57.9 0.0 collective-permute-done.6
  57.9 2.1 %all-to-all-done.1 = bf16[32,8,1024]{2,1,0:T(8,128)(2,1)S(1)} async-done(((bf16[32,8,1024]{2,1,0:T(8,128)(2,1)}), bf16[32,8,1024]{2,1,0:T(8,128)(2,1)S(1)}, u32[]{:S(2)}, u32[]{:S(2)}) %all-to-all-start.1) | async-done | bytes 524320 | tf_op jit(solution)/shard_map/all_to_all | solution.py:472
  60.1 5.3 %collective-permute-done.9.refs_1_ = bf16[8,224,128]{2,1,0:T(8,128)(2,1)S(1)} collective-permute-done((bf16[8,224,128]{2,1,0:T(8,128)(2,1)S(1)}, bf16[8,224,128]{2,1,0:T(8,128)(2,1)S(1)}, u32[]{:S(2)}, u32[]{:S(2)}) %collective-permute-start.9) | collective-permute-done | bytes 458784 | tf_op jit(solution)/shard_map/ppermute | solution.py:529
  65.3 0.8 copy-done.8
  66.1 2.4 %project.1 = bf16[2,8,32,256]{3,2,1,0:T(8,128)(2,1)} custom-call(s32[1]{0:T(128)} %bitcast.3.rank_ref, bf16[256,1024]{1,0:T(8,128)(2,1)S(1)} %bitcast.30, bf16[8,224,128]{2,1,0:T(8,128)(2,1)} %get-tuple-element.34.refs_0_, bf16[8,224,128]{2,1,0:T(8,128)(2,1)} %copy-done.8), custom_call_target="tpu_custom_call" | custom-call | flops 234881024 | bytes 1441792 | tf_op jit(solution)/shard_map/project/pallas_call | solution.py:332
  68.5 5.1 %all-to-all-start.2 = ((bf16[16,32,256]{2,1,0:T(8,128)(2,1)}), bf16[16,32,256]{2,1,0:T(8,128)(2,1)S(1)}, u32[]{:S(2)}, u32[]{:S(2)}) async-start(bf16[16,32,256]{2,1,0:T(8,128)(2,1)} %bitcast.15), calls=%async_computation.2 | async-start | bytes 524288 | tf_op jit(solution)/shard_map/all_to_all | solution.py:472
  73.5 0.8 dynamic_slice.16
  74.3 0.1 copy.16.gain_ref
  74.4 0.0 copy-done.9
  74.4 0.3 turn_hidden.1.hidden_ref
  74.7 6.1 %all-to-all-done.2.part_ref = bf16[16,32,256]{2,1,0:T(8,128)(2,1)S(1)} async-done(((bf16[16,32,256]{2,1,0:T(8,128)(2,1)}), bf16[16,32,256]{2,1,0:T(8,128)(2,1)S(1)}, u32[]{:S(2)}, u32[]{:S(2)}) %all-to-all-start.2) | async-done | bytes 262176 | tf_op jit(solution)/shard_map/all_to_all | solution.py:472
  80.8 0.9 make_mixed.1
  81.7 8.0 %all-to-all-start.3 = ((bf16[32,32,256]{2,1,0:T(8,128)(2,1)}), bf16[32,32,256]{2,1,0:T(8,128)(2,1)S(1)}, u32[]{:S(2)}, u32[]{:S(2)}) async-start(bf16[32,32,256]{2,1,0:T(8,128)(2,1)} %get-tuple-element.31), calls=%async_computation.3 | async-start | bytes 1048576 | tf_op jit(solution)/shard_map/all_to_all | solution.py:472
  89.7 0.0 copy-done.12
  89.7 1.2 collective-permute-start
  90.9 1.0 slice.8
  92.0 0.3 collective-permute-start.2
  92.2 1.0 slice.9
  93.3 0.6 collective-permute-start.8
  93.9 0.0 collective-permute-start.5
  93.9 2.9 %collective-permute-start.7 = (bf16[1,8,224,128]{3,2,1,0:T(8,128)(2,1)}, bf16[1,8,224,128]{3,2,1,0:T(8,128)(2,1)S(1)}, u32[]{:S(2)}, u32[]{:S(2)}) collective-permute-start(bf16[1,8,224,128]{3,2,1,0:T(8,128)(2,1)} %collective-permute-done.6), channel_id=1, source_target_pairs={{0,7},{1,6},{2,1},{3,0},{4,3},{5,2},{6,5},{7,4},{8,15},{9,14},{10,... | collective-permute-start | bytes 1376264 | tf_op jit(solution)/shard_map/ppermute | solution.py:518
  96.8 0.0 collective-permute-done.refs_1_
  96.8 0.0 collective-permute-done.2.refs_3_
  96.8 0.0 copy-start.4
  96.8 0.0 collective-permute-done.8.refs_7_
  96.8 0.0 copy-start.5
  96.8 10.5 %collective-permute-done.5.refs_4_ = bf16[1,8,224,128]{3,2,1,0:T(8,128)(2,1)S(1)} collective-permute-done((bf16[1,8,224,128]{3,2,1,0:T(8,128)(2,1)}, bf16[1,8,224,128]{3,2,1,0:T(8,128)(2,1)S(1)}, u32[]{:S(2)}, u32[]{:S(2)}) %collective-permute-start.5) | collective-permute-done | bytes 458784 | tf_op jit(solution)/shard_map/ppermute | solution.py:518
  107.4 0.0 collective-permute-done.7.refs_5_
  107.4 0.0 all-to-all-done.3
  107.4 0.7 copy-done.6
  108.2 0.2 copy-done.7
  108.3 2.4 %gate_up.1 = bf16[8,160,256]{2,1,0:T(8,128)(2,1)S(1)} custom-call(s32[1]{0:T(128)} %bitcast.rank_ref, bf16[1024,256]{1,0:T(8,128)(2,1)S(1)} %bitcast.29, bf16[1,8,224,128]{3,2,1,0:T(8,128)(2,1)} %get-tuple-element.19.refs_0_, bf16[1,8,224,128]{3,2,1,0:T(8,128)(2,1)} %copy-done.3, bf16[2,8,224,128]{3,2,1,0:T(8,128)(2,1)} %collective-permute-done.1.refs_2_, ...), custom_call_target="tpu_custom_call" | custom-call | flops 603979776 | bytes 2883584 | tf_op jit(solution)/shard_map/gate_up/pallas_call | solution.py:397
  110.8 15.6 %all_to_all.35.part_ref = bf16[8,160,256]{2,1,0:T(8,128)(2,1)S(1)} all-to-all(bf16[8,160,256]{2,1,0:T(8,128)(2,1)S(1)} %gate_up.1), channel_id=1, replica_groups=mesh['z'=16,'y'=2,'tp'=8] {'tp'}, dimensions={0} | all-to-all | bytes 1310720 | tf_op jit(solution)/shard_map/all_to_all | solution.py:472
  126.3 0.8 activate.1
  127.2 4.2 %all-to-all-start.5 = ((bf16[8,80,256]{2,1,0:T(8,128)(2,1)}), bf16[8,80,256]{2,1,0:T(8,128)(2,1)S(1)}, u32[]{:S(2)}, u32[]{:S(2)}) async-start(bf16[8,80,256]{2,1,0:T(8,128)(2,1)} %activate.1), calls=%async_computation.5 | async-start | bytes 655360 | tf_op jit(solution)/shard_map/all_to_all | solution.py:472
  131.4 2.5 %turn.1.w_ref = bf16[1024,640]{1,0:T(8,128)(2,1)S(1)} custom-call(bf16[1,8,224,128]{3,2,1,0:T(8,128)(2,1)} %get-tuple-element.19.refs_0_, bf16[1,8,224,128]{3,2,1,0:T(8,128)(2,1)} %copy-done.3, bf16[2,8,224,128]{3,2,1,0:T(8,128)(2,1)} %collective-permute-done.1.refs_2_, bf16[1,8,224,128]{3,2,1,0:T(8,128)(2,1)} %copy-done.4, ...), custom_call_target="tpu_custom_call" | custom-call | flops 167772160 | bytes 2621440 | tf_op jit(solution)/shard_map/turn/pallas_call | solution.py:185
  133.9 4.6 %all-to-all-done.5.x_ref = bf16[8,80,256]{2,1,0:T(8,128)(2,1)S(1)} async-done(((bf16[8,80,256]{2,1,0:T(8,128)(2,1)}), bf16[8,80,256]{2,1,0:T(8,128)(2,1)S(1)}, u32[]{:S(2)}, u32[]{:S(2)}) %all-to-all-start.5) | async-done | bytes 327712 | tf_op jit(solution)/shard_map/all_to_all | solution.py:472
  138.5 1.2 down.1
  139.7 24.6 %all_to_all.36.part_ref = bf16[32,32,256]{2,1,0:T(8,128)(2,1)S(1)} all-to-all(bf16[32,32,256]{2,1,0:T(8,128)(2,1)S(1)} %down.1), channel_id=1, replica_groups=mesh['z'=16,'y'=2,'tp'=8] {'z','y'}, dimensions={0} | all-to-all | bytes 1048576 | tf_op jit(solution)/shard_map/all_to_all | solution.py:472
  164.3 0.9 finish.1
  (17 shorter events, 0.1 us)
Async XLA Ops:
  2.9 23.6 %copy-start.11 = (s32[32,4]{0,1:T(4,128)S(1)}, s32[32,4]{0,1:T(4,128)}, u32[]{:S(2)}) copy-start(s32[32,4]{0,1:T(4,128)} %param.16) | copy-start | bytes 1540
  2.9 23.8 %copy-start.10 = (bf16[2,4,576]{2,1,0:T(4,128)(2,1)S(1)}, bf16[2,4,576]{2,1,0:T(4,128)(2,1)}, u32[]{:S(2)}) copy-start(bf16[2,4,576]{2,1,0:T(4,128)(2,1)} %param.20) | copy-start | bytes 27652
  2.9 23.8 %copy-start.1 = (bf16[2,4,16,576]{3,2,1,0:T(8,128)(2,1)S(1)}, bf16[2,4,16,576]{3,2,1,0:T(8,128)(2,1)}, u32[]{:S(2)}) copy-start(bf16[2,4,16,576]{3,2,1,0:T(8,128)(2,1)} %q_ref.3) | copy-start | bytes 442372
  2.9 23.8 %copy-start.2 = (s32[4]{0:T(128)S(1)}, s32[4]{0:T(128)}, u32[]{:S(2)}) copy-start(s32[4]{0:T(128)} %ctx_ref) | copy-start | bytes 52
  2.9 30.9 %all-to-all-start = ((bf16[32,16,576]{2,1,0:T(8,128)(2,1)}), bf16[32,16,576]{2,1,0:T(8,128)(2,1)S(1)}, u32[]{:S(2)}, u32[]{:S(2)}) async-start(bf16[32,16,576]{2,1,0:T(8,128)(2,1)} %bitcast.7), calls=%async_computation | async-start | bytes 1310720 | tf_op jit(solution)/shard_map/all_to_all | solution.py:472
  23.8 22.4 %collective-permute-start.1 = (bf16[2,8,224,128]{3,2,1,0:T(8,128)(2,1)}, bf16[2,8,224,128]{3,2,1,0:T(8,128)(2,1)}, u32[]{:S(2)}, u32[]{:S(2)}) collective-permute-start(bf16[2,8,224,128]{3,2,1,0:T(8,128)(2,1)} %get-tuple-element.21), channel_id=1, source_target_pairs={{0,2},{1,3},{2,4},{3,5},{4,6},{5,7},{6,0},{7,1},{8,10},{9,11},{10,... | collective-permute-start | bytes 2752520 | tf_op jit(solution)/shard_map/ppermute | solution.py:518
  25.0 21.2 %collective-permute-start.3 = (bf16[2,8,224,128]{3,2,1,0:T(8,128)(2,1)}, bf16[2,8,224,128]{3,2,1,0:T(8,128)(2,1)}, u32[]{:S(2)}, u32[]{:S(2)}) collective-permute-start(bf16[2,8,224,128]{3,2,1,0:T(8,128)(2,1)} %get-tuple-element.24), channel_id=1, source_target_pairs={{0,6},{1,7},{2,0},{3,1},{4,2},{5,3},{6,4},{7,5},{8,14},{9,15},{10,... | collective-permute-start | bytes 2752520 | tf_op jit(solution)/shard_map/ppermute | solution.py:518
  26.7 7.1 %copy-start = (bf16[16,512,128]{2,1,0:T(8,128)(2,1)S(1)}, bf16[16,512,128]{2,1,0:T(8,128)(2,1)}, u32[]{:S(2)}) copy-start(bf16[16,512,128]{2,1,0:T(8,128)(2,1)} %uv_ref.1) | copy-start | bytes 6291460
  37.0 23.0 %all-to-all-start.1 = ((bf16[32,8,1024]{2,1,0:T(8,128)(2,1)}), bf16[32,8,1024]{2,1,0:T(8,128)(2,1)S(1)}, u32[]{:S(2)}, u32[]{:S(2)}) async-start(bf16[32,8,1024]{2,1,0:T(8,128)(2,1)} %bitcast.11), calls=%async_computation.1 | async-start | bytes 1048576 | tf_op jit(solution)/shard_map/all_to_all | solution.py:472
  45.2 29.2 %copy-start.9 = (bf16[2,128,28]{1,0,2:T(2,128)(2,1)S(1)}, bf16[2,128,28]{1,0,2:T(2,128)(2,1)}, u32[]{:S(2)}) copy-start(bf16[2,128,28]{1,0,2:T(2,128)(2,1)} %param.23) | copy-start | bytes 43012
  46.2 11.7 %collective-permute-start.4 = (bf16[1,8,224,128]{3,2,1,0:T(8,128)(2,1)}, bf16[1,8,224,128]{3,2,1,0:T(8,128)(2,1)}, u32[]{:S(2)}, u32[]{:S(2)}) collective-permute-start(bf16[1,8,224,128]{3,2,1,0:T(8,128)(2,1)} %get-tuple-element.25), channel_id=1, source_target_pairs={{0,2},{1,3},{2,4},{3,5},{4,6},{5,7},{6,0},{7,1},{8,10},{9,11},{10,... | collective-permute-start | bytes 1376264 | tf_op jit(solution)/shard_map/ppermute | solution.py:518
  47.2 10.8 %collective-permute-start.6 = (bf16[1,8,224,128]{3,2,1,0:T(8,128)(2,1)}, bf16[1,8,224,128]{3,2,1,0:T(8,128)(2,1)}, u32[]{:S(2)}, u32[]{:S(2)}) collective-permute-start(bf16[1,8,224,128]{3,2,1,0:T(8,128)(2,1)} %get-tuple-element.26), channel_id=1, source_target_pairs={{0,6},{1,7},{2,0},{3,1},{4,2},{5,3},{6,4},{7,5},{8,14},{9,15},{10,... | collective-permute-start | bytes 1376264 | tf_op jit(solution)/shard_map/ppermute | solution.py:518
  50.9 38.8 %copy-start.12 = (bf16[1,8,224,128]{3,2,1,0:T(8,128)(2,1)S(1)}, bf16[1,8,224,128]{3,2,1,0:T(8,128)(2,1)}, u32[]{:S(2)}) copy-start(bf16[1,8,224,128]{3,2,1,0:T(8,128)(2,1)} %get-tuple-element.20) | copy-start | bytes 1376260
  50.9 14.4 %collective-permute-start.9 = (bf16[8,224,128]{2,1,0:T(8,128)(2,1)S(1)}, bf16[8,224,128]{2,1,0:T(8,128)(2,1)S(1)}, u32[]{:S(2)}, u32[]{:S(2)}) collective-permute-start(bf16[8,224,128]{2,1,0:T(8,128)(2,1)S(1)} %get-tuple-element.33), channel_id=1, source_target_pairs={{0,8},{8,0},{1,9},{9,1},{2,10},{10,2},{3,11},{11,3},{4,12},{12,4},... | collective-permute-start | bytes 1376264 | tf_op jit(solution)/shard_map/ppermute | solution.py:529
  65.3 0.8 copy-start.8
  68.5 12.3 %all-to-all-start.2 = ((bf16[16,32,256]{2,1,0:T(8,128)(2,1)}), bf16[16,32,256]{2,1,0:T(8,128)(2,1)S(1)}, u32[]{:S(2)}, u32[]{:S(2)}) async-start(bf16[16,32,256]{2,1,0:T(8,128)(2,1)} %bitcast.15), calls=%async_computation.2 | async-start | bytes 524288 | tf_op jit(solution)/shard_map/all_to_all | solution.py:472
  81.7 25.7 %all-to-all-start.3 = ((bf16[32,32,256]{2,1,0:T(8,128)(2,1)}), bf16[32,32,256]{2,1,0:T(8,128)(2,1)S(1)}, u32[]{:S(2)}, u32[]{:S(2)}) async-start(bf16[32,32,256]{2,1,0:T(8,128)(2,1)} %get-tuple-element.31), calls=%async_computation.3 | async-start | bytes 1048576 | tf_op jit(solution)/shard_map/all_to_all | solution.py:472
  89.7 7.1 %collective-permute-start = (bf16[1,8,224,128]{3,2,1,0:T(8,128)(2,1)S(1)}, bf16[1,8,224,128]{3,2,1,0:T(8,128)(2,1)S(1)}, u32[]{:S(2)}, u32[]{:S(2)}) collective-permute-start(bf16[1,8,224,128]{3,2,1,0:T(8,128)(2,1)S(1)} %copy-done.12), channel_id=1, source_target_pairs={{0,1},{1,0},{2,3},{3,2},{4,5},{5,4},{6,7},{7,6},{8,9},{9,8},{10,11... | collective-permute-start | bytes 1376264 | tf_op jit(solution)/shard_map/ppermute | solution.py:518
  92.0 4.9 %collective-permute-start.2 = (bf16[1,8,224,128]{3,2,1,0:T(8,128)(2,1)S(1)}, bf16[1,8,224,128]{3,2,1,0:T(8,128)(2,1)S(1)}, u32[]{:S(2)}, u32[]{:S(2)}) collective-permute-start(bf16[1,8,224,128]{3,2,1,0:T(8,128)(2,1)S(1)} %slice.8), channel_id=1, source_target_pairs={{0,1},{1,0},{2,3},{3,2},{4,5},{5,4},{6,7},{7,6},{8,9},{9,8},{10,11... | collective-permute-start | bytes 1376264 | tf_op jit(solution)/shard_map/ppermute | solution.py:518
  93.3 3.5 %collective-permute-start.8 = (bf16[1,8,224,128]{3,2,1,0:T(8,128)(2,1)S(1)}, bf16[1,8,224,128]{3,2,1,0:T(8,128)(2,1)S(1)}, u32[]{:S(2)}, u32[]{:S(2)}) collective-permute-start(bf16[1,8,224,128]{3,2,1,0:T(8,128)(2,1)S(1)} %slice.9), channel_id=1, source_target_pairs={{0,1},{1,0},{2,3},{3,2},{4,5},{5,4},{6,7},{7,6},{8,9},{9,8},{10,11... | collective-permute-start | bytes 1376264 | tf_op jit(solution)/shard_map/ppermute | solution.py:518
  93.9 13.5 %collective-permute-start.5 = (bf16[1,8,224,128]{3,2,1,0:T(8,128)(2,1)}, bf16[1,8,224,128]{3,2,1,0:T(8,128)(2,1)S(1)}, u32[]{:S(2)}, u32[]{:S(2)}) collective-permute-start(bf16[1,8,224,128]{3,2,1,0:T(8,128)(2,1)} %collective-permute-done.4), channel_id=1, source_target_pairs={{0,2},{1,3},{2,4},{3,5},{4,6},{5,7},{6,0},{7,1},{8,10},{9,11},{10,... | collective-permute-start | bytes 1376264 | tf_op jit(solution)/shard_map/ppermute | solution.py:518
  93.9 13.5 %collective-permute-start.7 = (bf16[1,8,224,128]{3,2,1,0:T(8,128)(2,1)}, bf16[1,8,224,128]{3,2,1,0:T(8,128)(2,1)S(1)}, u32[]{:S(2)}, u32[]{:S(2)}) collective-permute-start(bf16[1,8,224,128]{3,2,1,0:T(8,128)(2,1)} %collective-permute-done.6), channel_id=1, source_target_pairs={{0,7},{1,6},{2,1},{3,0},{4,3},{5,2},{6,5},{7,4},{8,15},{9,14},{10,... | collective-permute-start | bytes 1376264 | tf_op jit(solution)/shard_map/ppermute | solution.py:518
  96.8 10.6 %copy-start.3 = (bf16[1,8,224,128]{3,2,1,0:T(8,128)(2,1)}, bf16[1,8,224,128]{3,2,1,0:T(8,128)(2,1)S(1)}, u32[]{:S(2)}) copy-start(bf16[1,8,224,128]{3,2,1,0:T(8,128)(2,1)S(1)} %collective-permute-done.refs_1_) | copy-start | bytes 1376260
  96.8 10.6 %copy-start.4 = (bf16[1,8,224,128]{3,2,1,0:T(8,128)(2,1)}, bf16[1,8,224,128]{3,2,1,0:T(8,128)(2,1)S(1)}, u32[]{:S(2)}) copy-start(bf16[1,8,224,128]{3,2,1,0:T(8,128)(2,1)S(1)} %collective-permute-done.2.refs_3_) | copy-start | bytes 1376260
  96.8 10.6 %copy-start.5 = (bf16[1,8,224,128]{3,2,1,0:T(8,128)(2,1)}, bf16[1,8,224,128]{3,2,1,0:T(8,128)(2,1)S(1)}, u32[]{:S(2)}) copy-start(bf16[1,8,224,128]{3,2,1,0:T(8,128)(2,1)S(1)} %collective-permute-done.8.refs_7_) | copy-start | bytes 1376260
  107.4 0.8 copy-start.6
  107.4 0.9 copy-start.7
  127.2 11.3 %all-to-all-start.5 = ((bf16[8,80,256]{2,1,0:T(8,128)(2,1)}), bf16[8,80,256]{2,1,0:T(8,128)(2,1)S(1)}, u32[]{:S(2)}, u32[]{:S(2)}) async-start(bf16[8,80,256]{2,1,0:T(8,128)(2,1)} %activate.1), calls=%async_computation.5 | async-start | bytes 655360 | tf_op jit(solution)/shard_map/all_to_all | solution.py:472

commit v3 on v2

--- a/solution.py
+++ b/solution.py
@@ -43,12 +43,18 @@
     return pltpu.with_memory_space_constraint(x, pltpu.HBM)
 
 
-def share_picker(tp, width):
-    shape = (tp * PAD, tp * width)
-    row = iota(shape, 0)
-    place = row % PAD
-    wanted = (row // PAD) * width + place
-    return jnp.where((iota(shape, 1) == wanted) & (place < width), 1.0, 0.0).astype(bf16)
+def share_picker(tp, width, turn):
+    shape = (tp * width, -(-tp // GROUP) * GROUP * PAD)
+    column = iota(shape, 1)
+    place = column % PAD
+    slot = (column // PAD) % GROUP
+    rank = column // (GROUP * PAD) * GROUP + (slot + GROUP - turn) % GROUP
+    hit = (iota(shape, 0) == rank * width + place) & (place < width)
+    return jnp.where(hit, 1.0, 0.0).astype(bf16)
+
+
+def source_in_group(rank, slot):
+    return (slot + GROUP - rank % GROUP) % GROUP
 
 
 def partner(rank, tp, k, sign):
@@ -117,38 +123,49 @@
     return {k: (n, at) for n, ks in enumerate(arrays) for at, k in enumerate(ks)}
 
 
-def reshard_kernel(tp, width, rank_ref, wg_ref, wu_ref, wd_ref, *refs):
-    *outs, all_scr, sorted_scr = refs
+def reshard_kernel(tp, width, rank_ref, gain_ref, wg_ref, wu_ref, wd_ref, *refs):
+    *outs, all_scr, pick_scr, sort_scr = refs
     block = tp * width
     units = wg_ref.shape[0]
-    picker = share_picker(tp, width)
     lanes = GROUP * PAD
-    all_scr[3 * units :, :] = jnp.zeros((all_scr.shape[0] - 3 * units, all_scr.shape[1]), bf16)
+
+    @pl.when(pl.program_id(0) == 0)
+    def _():
+        for i in range(GROUP):
+            pick_scr[i] = share_picker(tp, width, i)
+        all_scr[3 * units :, :] = jnp.zeros((all_scr.shape[0] - 3 * units, all_scr.shape[1]), bf16)
+
     for n, w_ref in enumerate((wg_ref, wu_ref, wd_ref)):
-        all_scr[n * units : (n + 1) * units, :] = w_ref[...]
+        value = w_ref[...]
+        if n < 2:
+            value = (value.astype(f32) * gain_ref[...]).astype(bf16)
+        all_scr[n * units : (n + 1) * units, :] = value
+    slot_of = iota((all_scr.shape[0], lanes), 1) // PAD
     places = piece_places(tp)
     for u in range(outs[0].shape[1]):
-        picked = [
-            dot(all_scr[:, i * block : (i + 1) * block], picker, NT).astype(bf16)
-            for i in range(u * GROUP, (u + 1) * GROUP)
-        ]
-        for j in range(tp):
-            part = [value[:, j * PAD : (j + 1) * PAD] for value in picked]
-            sorted_scr[u, :, j * lanes : (j + 1) * lanes] = jnp.concatenate(part, axis=1)
+        for i in range(GROUP):
+            first = (u * GROUP + i) * block
+            sort_scr[u, i] = dot(all_scr[:, first : first + block], pick_scr[i]).astype(bf16)
         for k in range(tp):
-            first = pl.multiple_of(partner(rank_ref[0], tp, k, 1) * lanes, lanes)
+            target = partner(rank_ref[0], tp, k, 1)
+            tile = pl.multiple_of(target // GROUP * lanes, lanes)
+            value = None
+            for slot in range(GROUP):
+                part = sort_scr[u, source_in_group(target, slot), :, pl.ds(tile, lanes)]
+                value = part if value is None else jnp.where(slot_of == slot, part, value)
             array, at = places[k]
-            outs[array][at, u] = sorted_scr[u, :, pl.ds(first, lanes)]
-
-
-def reshard(rank, w_gate, w_up, w_down, dp, tp, width, unit_pad):
+            outs[array][at, u] = value
+
+
+def reshard(rank, gain, w_gate, w_up, w_down, dp, tp, width, unit_pad):
     units = w_gate.shape[1]
     count = dp // GROUP
-    each = count // 2 if count % 2 == 0 else count
+    each = 2 if count % 2 == 0 else 1
     block = tp * width * GROUP * each
     lanes = GROUP * PAD
     rows = 2 * units + unit_pad
     w_spec = pl.BlockSpec((units, block), lambda c: (0, c))
+    tiles = -(-tp // GROUP)
     places = piece_places(tp)
     owners = [n for n, _ in places.values()]
     sizes = [owners.count(n) for n in range(max(owners) + 1)]
@@ -157,17 +174,24 @@
         tuple(pltpu.HBM((size, count, rows, lanes), bf16) for size in sizes),
         (2 * 3 * dp * tp * PAD * tp * width * units, 14 * w_gate.size),
         grid=(count // each,),
-        in_specs=[pl.BlockSpec(memory_space=pltpu.SMEM), w_spec, w_spec, w_spec],
+        in_specs=[
+            pl.BlockSpec(memory_space=pltpu.SMEM),
+            pl.BlockSpec((1, block), lambda c: (0, c)),
+            w_spec,
+            w_spec,
+            w_spec,
+        ],
         out_specs=tuple(
             pl.BlockSpec((size, each, rows, lanes), lambda c: (0, c, 0, 0)) for size in sizes
         ),
         scratch_shapes=[
             pltpu.VMEM((rows, block), bf16),
-            pltpu.VMEM((each, rows, tp * lanes), bf16),
+            pltpu.VMEM((GROUP, tp * width, tiles * lanes), bf16),
+            pltpu.VMEM((each, GROUP, rows, tiles * lanes), bf16),
         ],
         name="reshard",
         mib=24,
-    )(rank, in_hbm(w_gate.T), in_hbm(w_up.T), in_hbm(w_down))
+    )(rank, gain.reshape(1, -1), in_hbm(w_gate.T), in_hbm(w_up.T), in_hbm(w_down))
 
 
 def turn_kernel(first, *refs):
@@ -178,7 +202,7 @@
         refs[-1][c * lanes : (c + 1) * lanes, :] = dot(eye, x, NT).astype(bf16)
 
 
-def turn(pieces, first):
+def turn(pieces, places, first):
     _, count, rows, lanes = pieces[0][0].shape
     depth = len(pieces) * (rows - first)
     each = 4 if count % 4 == 0 else 1
@@ -192,7 +216,7 @@
         ],
         out_specs=pl.BlockSpec((each * lanes, depth), lambda c: (c, 0)),
         name="turn",
-    )(*[in_hbm(array) for array, _ in pieces])
+    )(*[place(array) for (array, _), place in zip(pieces, places)])
 
 
 def hidden_kernel(dp, per_owner, steps, h_ref, out_ref):
@@ -275,14 +299,15 @@
     latent = (acc / total).astype(bf16)
     values = uv_ref.shape[2]
     groups = per_owner * steps
-    head_of = iota((groups, heads, values), 1)
-    for h in range(heads):
-        full = dot(latent, uv_ref[h]).reshape(groups, heads, values)
-        mine = jnp.sum(jnp.where(head_of == h, full, 0.0), axis=1).astype(bf16)
-        each = out_ref.shape[3] // values
+    each = out_ref.shape[3] // values
+    for h in range(0, heads, 2):
+        full = dot(latent, jnp.concatenate([uv_ref[h], uv_ref[h + 1]], axis=1))
+        full = full.reshape(groups, heads, 2 * values)
+        wanted = h + iota(full.shape, 2) // values
+        mine = jnp.sum(jnp.where(iota(full.shape, 1) == wanted, full, 0.0), axis=1).astype(bf16)
         place = (h % each) * values
-        out_ref[:, h // each, :, place : place + values] = jnp.broadcast_to(
-            mine[None], (out_ref.shape[0], groups, values)
+        out_ref[:, h // each, :, place : place + 2 * values] = jnp.broadcast_to(
+            mine[None], (out_ref.shape[0], groups, 2 * values)
         )
 
 
@@ -309,39 +334,59 @@
     )(my_lengths, queries, new_rows, in_hbm(acc), in_hbm(side), w_uv)
 
 
-def project_kernel(rank_ref, x_ref, *refs):
+def gather_heads_kernel(rank_ref, *refs):
     out_ref = refs[-1]
+    ring = len(refs) - 1
+    for k, w_ref in enumerate(refs[:-1]):
+        heads, _, values = w_ref.shape
+        target = (rank_ref[0] + ring - k) % ring
+        for h in range(heads):
+            out_ref[target, :, h * values : (h + 1) * values] = w_ref[h]
+
+
+def gather_heads(rank, own, pieces):
+    heads, features, values = pieces[0].shape
+    ring = 1 + len(pieces)
+    block = (heads, features, values)
+    return call(
+        gather_heads_kernel,
+        jax.ShapeDtypeStruct((ring, features, heads * values), bf16),
+        (0, 4 * ring * heads * features * values),
+        grid_spec=pltpu.PrefetchScalarGridSpec(
+            num_scalar_prefetch=1,
+            grid=(1,),
+            in_specs=[pl.BlockSpec(block, lambda c, rank: (rank[0], 0, 0))]
+            + [pl.BlockSpec(block, lambda c, rank: (0, 0, 0))] * len(pieces),
+            out_specs=pl.BlockSpec(memory_space=pltpu.VMEM),
+        ),
+        name="gather_heads",
+    )(rank, in_hbm(own), *[in_hbm(piece) for piece in pieces])
+
+
+def project_kernel(w_ref, x_ref, out_ref):
     ring, tp = out_ref.shape[:2]
     x = x_ref[...].T
-    for k, w_ref in enumerate(refs[:-1]):
-        heads, columns, _ = w_ref.shape
-        width = columns // tp
-        weights = jnp.concatenate([w_ref[h] for h in range(heads)], axis=1)
-        value = dot(weights, x)
+    for n in range(ring):
+        width = w_ref.shape[1] // tp
+        value = dot(w_ref[n], x)
         spare = jnp.zeros((PAD - width, value.shape[1]), f32)
-        target = (rank_ref[0] + ring - k) % ring
         for j in range(tp):
             part = jnp.concatenate([value[j * width : (j + 1) * width], spare], axis=0)
-            out_ref[target, j] = part.astype(bf16)
-
-
-def project(rank, pieces, every, tp):
-    heads, features, values = pieces[0].shape
-    ring, columns = len(pieces), every.shape[0]
-    size = ring * heads * features * values
+            out_ref[n, j] = part.astype(bf16)
+
+
+def project(weights, every, tp):
+    ring, features, depth = weights.shape
+    columns = every.shape[0]
+    whole = pl.BlockSpec(memory_space=pltpu.VMEM)
     return call(
         project_kernel,
         jax.ShapeDtypeStruct((ring, tp, PAD, columns), bf16),
-        (2 * size * columns, 2 * (size + every.size)),
-        grid=(1,),
-        in_specs=[
-            pl.BlockSpec(memory_space=pltpu.SMEM),
-            pl.BlockSpec(every.shape, lambda c: (0, 0)),
-        ]
-        + [pl.BlockSpec((heads, features, values), lambda c: (0, 0, 0))] * ring,
-        out_specs=pl.BlockSpec((ring, tp, PAD, columns), lambda c: (0, 0, 0, 0)),
+        (2 * weights.size * columns, 2 * (weights.size + every.size)),
+        in_specs=[whole, whole],
+        out_specs=whole,
         name="project",
-    )(rank, every, *[in_hbm(piece) for piece in pieces])
+    )(weights, every)
 
 
 def split_sum(value):
@@ -349,66 +394,115 @@
     return high, value - high
 
 
-def mixed_kernel(width, part_ref, hidden_ref, gain_ref, mixed_ref, out_ref):
+def stack_halves(value, width):
+    half = value.shape[1] // 2
+    return jnp.concatenate([value[:width, :half], value[:width, half:]], axis=0)
+
+
+def mixed_kernel(width, part_ref, hidden_ref, mixed_ref, out_ref):
     mixed = jnp.sum(part_ref[...].astype(f32), axis=0) + hidden_ref[...]
     mixed_ref[...] = mixed
-    high, low = split_sum(jnp.sum(mixed * mixed, axis=0, keepdims=True))
-    row = iota(mixed.shape, 0)
-    sent = jnp.where(row == width, high, jnp.where(row == width + 1, low, mixed * gain_ref[...]))
-    out_ref[...] = jnp.broadcast_to(sent.astype(bf16)[None], out_ref.shape)
-
-
-def make_mixed(parts, hidden_t, gain, dp, width):
+    sent = stack_halves(mixed, width).astype(bf16)
+    out_ref[...] = jnp.broadcast_to(sent[None], out_ref.shape)
+
+
+def make_mixed(parts, hidden_t, dp, width):
     _, rows, columns = parts.shape
     return call(
         functools.partial(mixed_kernel, width),
         (
             jax.ShapeDtypeStruct((rows, columns), f32),
-            jax.ShapeDtypeStruct((dp, rows, columns), bf16),
+            jax.ShapeDtypeStruct((dp, 2 * width, columns // 2), bf16),
         ),
         (parts.size, 4 * parts.size),
         name="make_mixed",
-    )(parts, hidden_t, gain)
-
-
-def gate_kernel(width, rank_ref, x_ref, *refs):
-    out_ref = refs[-1]
-    units = out_ref.shape[1] - 16
-    x = x_ref[...]
-    depth = x.shape[0]
-    place = iota((16, depth), 1) % PAD
-    pick = jnp.where((place == width) | (place == width + 1), 1.0, 0.0).astype(bf16)
-    squares = dot(pick, x)
-    high, low = split_sum(squares)
-    row = iota(squares.shape, 0)
+    )(parts, hidden_t)
+
+
+def gate_kernel(groups, rank_ref, x_ref, *refs):
+    *w_refs, keep_ref, send_ref = refs
+    units = w_refs[0].shape[1]
+    width = x_ref.shape[1] // 2
+    blocks = []
+    for c in range(0, x_ref.shape[0], GROUP):
+        for slot in range(GROUP):
+            piece = x_ref[c + source_in_group(rank_ref[0], slot)].astype(f32)
+            spare = jnp.zeros((PAD - width, piece.shape[1]), f32)
+            right = jnp.concatenate([piece[width:], spare], axis=0)
+            blocks.append(jnp.concatenate([piece[:PAD], right], axis=1))
+    x = jnp.concatenate(blocks, axis=0)
+    squares = jnp.where(iota(x.shape, 0) % PAD < width, x * x, 0.0)
+    high, low = split_sum(jnp.sum(squares, axis=0, keepdims=True))
+    row = iota((16, x.shape[1]), 0)
     tail = jnp.where(row == 0, high, jnp.where(row == 1, low, 0.0)).astype(bf16)
-    for k, w_ref in enumerate(refs[:-1]):
-        target = partner(rank_ref[0], len(refs) - 1, k, -1)
-        weights = jnp.concatenate([w_ref[0, c] for c in range(w_ref.shape[1])], axis=1)
-        out_ref[target, :units, :] = dot(weights, x).astype(bf16)
-        out_ref[target, units:, :] = tail
-
-
-def gate_up(rank, pieces, x, units, width):
-    tp, columns = len(pieces), x.shape[1]
+    x = x.astype(bf16)
+    for w_ref, group in zip(w_refs, groups):
+        for at, k in enumerate(group):
+            n = partner(rank_ref[0], 2 * keep_ref.shape[0], k, -1) // 2
+            out_ref = send_ref if k % 2 else keep_ref
+            out_ref[n, :units, :] = dot(w_ref[at], x).astype(bf16)
+            out_ref[n, units:, :] = tail
+
+
+def collect_kernel(*refs):
+    for n, w_ref in enumerate(refs[:-1]):
+        lanes = w_ref.shape[3]
+        for c in range(w_ref.shape[1]):
+            refs[-1][n, :, c * lanes : (c + 1) * lanes] = w_ref[0, c]
+
+
+def collect(pieces, places, units):
+    tp = len(pieces)
     _, count, _, lanes = pieces[0][0].shape
-    size = tp * units * x.shape[0]
-    out_shape = (tp, units + 16, columns)
-    return call(
-        functools.partial(gate_kernel, width),
+    out_shape = (tp, units, count * lanes)
+    return call(
+        collect_kernel,
         jax.ShapeDtypeStruct(out_shape, bf16),
-        (2 * size * columns, 2 * size + 2 * x.size),
+        (0, 4 * tp * units * count * lanes),
         grid=(1,),
         in_specs=[
-            pl.BlockSpec(memory_space=pltpu.SMEM),
-            pl.BlockSpec(x.shape, lambda c: (0, 0)),
-        ]
-        + [
             pl.BlockSpec((1, count, units, lanes), lambda c, at=at: (at, 0, 0, 0)) for _, at in pieces
         ],
-        out_specs=pl.BlockSpec(out_shape, lambda c: (0, 0, 0)),
+        out_specs=pl.BlockSpec(memory_space=pltpu.VMEM),
+        name="collect",
+    )(*[place(array) for (array, _), place in zip(pieces, places)])
+
+
+def gate_up(rank, weights, groups, x):
+    tp = sum(len(group) for group in groups)
+    _, units, depth = weights[0].shape
+    size = tp * units * depth
+    columns = 2 * x.shape[2]
+    whole = pl.BlockSpec(memory_space=pltpu.VMEM)
+    out = jax.ShapeDtypeStruct((tp // 2, units + 16, columns), bf16)
+    return call(
+        functools.partial(gate_kernel, groups),
+        (out, out),
+        (2 * size * columns, 2 * size + 2 * x.size),
+        in_specs=[pl.BlockSpec(memory_space=pltpu.SMEM)] + [whole] * (1 + len(weights)),
+        out_specs=(whole, whole),
         name="gate_up",
-    )(rank, x, *[in_hbm(array) for array, _ in pieces])
+    )(rank, x, *weights)
+
+
+def add_kernel(units, a_ref, b_ref, out_ref):
+    out_ref[:, :units, :] = (
+        a_ref[:, :units, :].astype(f32) + b_ref[:, :units, :].astype(f32)
+    ).astype(bf16)
+    tail = a_ref[:, units:, :].astype(f32) + b_ref[:, units:, :].astype(f32)
+    high, low = split_sum(tail[:, 0:1] + tail[:, 1:2])
+    row = iota(tail.shape, 1)
+    tail = jnp.where(row == 0, high, jnp.where(row == 1, low, 0.0))
+    out_ref[:, units:, :] = tail.astype(bf16)
+
+
+def add_cores(a, b, units):
+    return call(
+        functools.partial(add_kernel, units),
+        jax.ShapeDtypeStruct(a.shape, bf16),
+        (2 * a.size, 6 * a.size),
+        name="add_cores",
+    )(a, b)
 
 
 def activate_kernel(model_width, units, part_ref, out_ref):
@@ -434,42 +528,61 @@
     )(parts)
 
 
-def down_kernel(rank_ref, w_ref, x_ref, out_ref):
-    tp = x_ref.shape[0]
-    x = jnp.concatenate([x_ref[partner(rank_ref[0], tp, k, -1)] for k in range(tp)], axis=0)
-    out_ref[...] = dot(w_ref[...], x).astype(bf16).reshape(out_ref.shape)
-
-
-def down(rank, turned, x, dp):
+def down_kernel(rank_ref, w_ref, same_ref, other_ref, out_ref):
+    tp = 2 * same_ref.shape[0]
+    refs = (same_ref, other_ref)
+    sources = [partner(rank_ref[0], tp, k, -1) // 2 for k in range(tp)]
+    x = jnp.concatenate([refs[k % 2][n] for k, n in enumerate(sources)], axis=0)
+    value = dot(w_ref[...], x)
+    count, rows, _ = out_ref.shape
+    value = value.reshape(count, PAD, value.shape[1])
+    for n in range(count):
+        first, slot = n // GROUP * GROUP, n % GROUP
+        out_ref[first + source_in_group(rank_ref[0], slot)] = stack_halves(
+            value[n], rows // 2
+        ).astype(bf16)
+
+
+def down(rank, turned, same, other, dp, width):
     rows, depth = turned.shape
-    columns = x.shape[2]
+    columns = same.shape[2]
     block = 256 if rows % 256 == 0 else 128
+    x_spec = pl.BlockSpec(same.shape, lambda c: (0, 0, 0))
     return call(
         down_kernel,
-        jax.ShapeDtypeStruct((dp, PAD, columns), bf16),
-        (2 * turned.size * columns, 2 * turned.size + 2 * x.size),
+        jax.ShapeDtypeStruct((dp, 2 * width, columns // 2), bf16),
+        (2 * turned.size * columns, 2 * turned.size + 4 * same.size),
         grid=(rows // block,),
         in_specs=[
             pl.BlockSpec(memory_space=pltpu.SMEM),
             pl.BlockSpec((block, depth), lambda c: (c, 0)),
-            pl.BlockSpec(x.shape, lambda c: (0, 0, 0)),
+            x_spec,
+            x_spec,
         ],
-        out_specs=pl.BlockSpec((block // PAD, PAD, columns), lambda c: (c, 0, 0)),
+        out_specs=pl.BlockSpec((block // PAD, 2 * width, columns // 2), lambda c: (c, 0, 0)),
         name="down",
-    )(rank, turned, x)
+    )(rank, turned, same, other)
 
 
 def finish_kernel(dp, per_owner, steps, part_ref, mixed_ref, out_ref):
-    value = jnp.sum(part_ref[...].astype(f32), axis=0) + mixed_ref[...]
+    value = jnp.sum(part_ref[...].astype(f32), axis=0)
+    width = value.shape[0] // 2
+    value = jnp.concatenate([value[:width], value[width:]], axis=1) + mixed_ref[:width]
     picked = dot(value.astype(bf16), token_picker(dp, per_owner, steps), NT)
-    picked = picked[: out_ref.shape[0]].astype(bf16)
+    picked = picked.astype(bf16)
     each = out_ref.shape[2]
     for s in range(steps):
         out_ref[:, s, :] = picked[:, s * each : (s + 1) * each]
 
 
-def exchange(x, axis):
-    return lax.all_to_all(x, axis, split_axis=0, concat_axis=0, tiled=True)
+def exchange(x, axis, groups=None):
+    return lax.all_to_all(
+        x, axis, split_axis=0, concat_axis=0, tiled=True, axis_index_groups=groups
+    )
+
+
+def swap_cores(x):
+    return lax.ppermute(x, "tp", [(j, j ^ 1) for j in range(lax.axis_size("tp"))])
 
 
 def shards(
@@ -503,7 +616,17 @@
     incoming = exchange(routed.reshape(dp, OWN_TOK, -1), both).reshape(dp * OWN_TOK, -1)
 
     rank = tp_rank.astype(i32).reshape(1)
-    arrays = reshard(rank, w_gate, w_up, w_down, dp, tp, width, unit_pad)
+    arrays = reshard(rank, ffn_gain, w_gate, w_up, w_down, dp, tp, width, unit_pad)
+
+    y_rank = lax.axis_index("y").astype(i32).reshape(1)
+    each = w_out.shape[0] // ring
+    w_turned = w_out.transpose(0, 2, 1)
+    out_pieces = []
+    for k in range(1, ring):
+        piece = lax.dynamic_slice_in_dim(w_turned, (y_rank[0] + k) % ring * each, each, 0)
+        pairs = [(j, (j + k) % ring) for j in range(ring)]
+        out_pieces.append(lax.ppermute(piece, "y", pairs))
+    incoming, _ = lax.optimization_barrier((incoming, out_pieces))
 
     ctx_lengths, _ = lax.optimization_barrier((ctx_lengths, arrays[0]))
     tokens = jnp.pad(step_latents.transpose(1, 0, 2), ((0, 0), (0, 16 - steps), (0, 0)))
@@ -517,28 +640,19 @@
     def along_x(piece, k, sign):
         return lax.ppermute(piece, "tp", [(j, partner(j, tp, k, sign)) for j in range(tp)])
 
-    y_rank = lax.axis_index("y").astype(i32).reshape(1)
-    each = w_out.shape[0] // ring
-    w_turned = w_out.transpose(0, 2, 1)
-    out_pieces = [
-        lax.dynamic_slice_in_dim(w_turned, (y_rank[0] + k) % ring * each, each, 0)
-        for k in range(ring)
-    ]
-    for k in range(1, ring):
-        pairs = [(j, (j + k) % ring) for j in range(ring)]
-        out_pieces[k] = lax.ppermute(out_pieces[k], "y", pairs)
     pieces = {k: (arrays[n], at) for k, (n, at) in piece_places(tp).items()}
     if tp > 2:
         plus, minus = along_x(arrays[2], 2, 1), along_x(arrays[3], 2, -1)
         far, _ = lax.optimization_barrier((arrays[4:6], (plus, minus)))
         far = [along_x(far[0], 2, 1), along_x(far[1], 2, -1)]
         every, _ = lax.optimization_barrier((every, (plus, minus, far)))
-    parts = project(y_rank, out_pieces, every, tp)
+    parts = project(gather_heads(y_rank, w_turned, out_pieces), every, tp)
     parts = exchange(parts.reshape((ring * tp,) + parts.shape[2:]), ("y", "tp"))
     if tp > 2:
         pieces[2], pieces[6] = (plus, 0), (minus, 0)
-        pieces[3] = along_x(plus[1:], 1, 1), 0
-        pieces[7] = along_x(minus[1:], 1, 1), 0
+        swapped = [along_x(plus[1:], 1, 1), along_x(minus[1:], 1, 1)]
+        parts, _ = lax.optimization_barrier((parts, swapped))
+        pieces[3], pieces[7] = (swapped[0], 0), (swapped[1], 0)
         pieces[4] = along_x(far[0], 2, 1), 0
         pieces[5] = along_x(far[1], 3, -1), 0
     pieces[1] = along_x(arrays[1], 1, 1), 0
@@ -548,15 +662,22 @@
         jax.ShapeDtypeStruct((PAD, total), f32),
         name="turn_hidden",
     )(hidden.transpose(2, 0, 1).reshape(width, total))
-    gain = lax.dynamic_slice_in_dim(ffn_gain, (dp_rank * tp + tp_rank) * width, width)
-    gain = jnp.pad(gain, (0, PAD - width)).reshape(PAD, 1)
-
-    mixed, sent = make_mixed(parts, hidden_t, gain, dp, width)
-    x = exchange(sent, both).reshape(dp * PAD, total)
-    parts = exchange(gate_up(rank, pieces, x, 2 * units, width), "tp")
-    act = exchange(activate(parts, model_width, units, unit_pad), "tp")
-    turned_down = turn(pieces, 2 * units)
-    parts = exchange(down(rank, turned_down, act, dp), both)
+    mixed, sent = make_mixed(parts, hidden_t, dp, width)
+    x = exchange(sent, both)
+    groups = [[k for k in range(tp) if k // 2 != 2], [k for k in range(tp) if k // 2 == 2]]
+    groups = [group for group in groups if group]
+    places = [(lambda array: array) if k // 2 == 2 else in_hbm for k in range(tp)]
+    weights = [
+        collect([pieces[k] for k in group], [places[k] for k in group], 2 * units)
+        for group in groups
+    ]
+    keep, send = gate_up(rank, weights, groups, x)
+    along = [[2 * n + core for n in range(tp // 2)] for core in range(2)]
+    parts = exchange(add_cores(keep, swap_cores(send), 2 * units), "tp", along)
+    parts, turned_down = lax.optimization_barrier((parts, turn(pieces, [in_hbm] * tp, 2 * units)))
+    same = exchange(activate(parts, model_width, units, unit_pad), "tp", along)
+    other = swap_cores(same)
+    parts = exchange(down(rank, turned_down, same, other, dp, width), both)
     out = call(
         functools.partial(finish_kernel, dp, per_owner, steps),
         jax.ShapeDtypeStruct((width, steps, total // steps), bf16),

time: 167 us -> 154 us (0.922)
  blocking collectives: 40.2 us -> 30.7 us
  waiting for transfers between devices: 36.8 us -> 29.1 us
  starting transfers between devices: 48.9 us -> 55.5 us
  local copies, waits for them, and re-layouts: 6.89 us -> 4.75 us
    all_to_all x2, blocking collectives: 40.2 us -> 30.7 us  [exchange(): lax.all_to_all(x, axis, split_axis=0, concat_axis=0, tiled=True, axis_ind...]
    ppermute x9, waiting for transfers between devices: 17.7 us -> 9.98 us  [along_x(): lax.ppermute(piece, 'tp', [(j, partner(j, tp, k, sign)) for j in range(tp)])]
    ppermute x1 -> x3, starting transfers between devices: 0.92 us -> 6.08 us  [the longest x2 4.85 us: swap_cores(): lax.ppermute(x, 'tp', [(j, j ^ 1) for j in range(lax.axis_size('tp'))])]
    pallas_call x2 -> x6, Pallas kernels: 3.59 us -> 7.47 us  [the longest x2 2.06 us: collect(): call(collect_kernel, jax.ShapeDtypeStruct(out_shape, bf16), (0, 4 * tp *...]
    ppermute x9, starting transfers between devices: 10.3 us -> 12.2 us  [along_x(): lax.ppermute(piece, 'tp', [(j, partner(j, tp, k, sign)) for j in range(tp)])]
    ppermute x1 -> x3, waiting for transfers between devices: 5.26 us -> 3.9 us  [the longest x2 2.28 us: swap_cores(): lax.ppermute(x, 'tp', [(j, j ^ 1) for j in range(lax.axis_size('tp'))])]
  transfers between devices with their start and end apart: 15 -> 17, of which waited for: 8 -> 8; matrix products, arithmetic and copies ran while one was open for 3% -> 3% of each run, Pallas kernels for 13% -> 15%
where the time goes in v3:
time: 154 us; the launch traced here: 153 us
  starting transfers between devices  55.5 us (36%)
  Pallas kernels  32.4 us (21%)
  blocking collectives  30.7 us (20%)
  waiting for transfers between devices  29.1 us (19%)
  local copies, waits for them, and re-layouts  4.75 us (3%)
    all_to_all x5, starting transfers between devices, exchange(): lax.all_to_all(x, axis, split_axis=0, concat_axis=0, tiled=True, axis_ind...  37.2 us
    all_to_all x2, blocking collectives, exchange(): lax.all_to_all(x, axis, split_axis=0, concat_axis=0, tiled=True, axis_ind...  30.7 us
    all_to_all x5, waiting for transfers between devices, exchange(): lax.all_to_all(x, axis, split_axis=0, concat_axis=0, tiled=True, axis_ind...  15.3 us
    ppermute x9, starting transfers between devices, along_x(): lax.ppermute(piece, 'tp', [(j, partner(j, tp, k, sign)) for j in range(tp)])  12.2 us
    ppermute x9, waiting for transfers between devices, along_x(): lax.ppermute(piece, 'tp', [(j, partner(j, tp, k, sign)) for j in range(tp)])  9.98 us
    pallas_call x1, Pallas kernels, reshard(): call(functools.partial(reshard_kernel, tp, width), tuple((pltpu.HBM((size...  7.03 us
    pallas_call x1, Pallas kernels, attend_cache(): call(cache_kernel, (pltpu.HBM((per_owner, rows, LAT), f32), pltpu.HBM((pe...  5.99 us
    ppermute x2, starting transfers between devices, swap_cores(): lax.ppermute(x, 'tp', [(j, j ^ 1) for j in range(lax.axis_size('tp'))])  4.85 us
  transfers between devices with their start and end apart: 17, of which 8 were waited for; matrix products, arithmetic and copies ran while one was open for 3% of the time, Pallas kernels for 15%

profile of v3, /device:TPU:1, one launch (start us, length us, event | category | flops | bytes accessed | tf_op | source)
XLA Modules:
  0.0 152.8 jit_solution(11021971085049102137)
XLA Ops:
  0.0 3.0 %route.1 = bf16[512,576]{1,0:T(8,128)(2,1)} custom-call(s32[1,128]{1,0:T(1,128)} %bitcast.38, s32[4,32]{1,0:T(4,128)} %bitcast.37, bf16[576,512]{1,0:T(8,128)(2,1)} %bitcast.33), custom_call_target="tpu_custom_call" | custom-call | flops 301989888 | bytes 1179648 | tf_op jit(solution)/shard_map/route/pallas_call | solution.py:104
  3.0 12.0 %all-to-all-start = ((bf16[32,16,576]{2,1,0:T(8,128)(2,1)}), bf16[32,16,576]{2,1,0:T(8,128)(2,1)S(1)}, u32[]{:S(2)}, u32[]{:S(2)}) async-start(bf16[32,16,576]{2,1,0:T(8,128)(2,1)} %bitcast.7), calls=%async_computation | async-start | bytes 1310720 | tf_op jit(solution)/shard_map/all_to_all | solution.py:579
  15.0 0.0 copy-start.13
  15.0 0.0 copy-start.12
  15.1 0.0 copy-start.3
  15.1 0.0 copy-start.5
  15.1 0.8 dynamic-slice_bitcast_fusion
  15.9 1.2 collective-permute-start
  17.2 0.0 copy-done.4
  17.2 7.0 %reshard.1 = (bf16[1,8,224,128]{3,2,1,0:T(8,128)(2,1)}, bf16[1,8,224,128]{3,2,1,0:T(8,128)(2,1)}, bf16[2,8,224,128]{3,2,1,0:T(8,128)(2,1)}, bf16[2,8,224,128]{3,...) custom-call(s32[1]{0:T(128)} %bitcast.rank_ref, f32[1,7168]{1,0:T(1,128)S(1)} %bitcast.28, ...), custom_call_target="tpu_custom_call" | custom-call | flops 792723456 | bytes 7225344 | tf_op jit(solution)/shard_map/reshard/pallas_call | solution.py:172
  24.2 1.2 collective-permute-start.1
  25.4 1.5 collective-permute-start.2
  26.9 0.2 dynamic-slice_reduce_fusion.len_ref
  27.1 0.0 copy-start
  27.1 6.0 %attend_cache.1 = (f32[4,32,512]{2,1,0:T(8,128)}, f32[4,32,128]{2,1,0:T(8,128)}) custom-call(s32[4]{0:T(128)S(1)} %copy-done.5, bf16[2,4,16,576]{3,2,1,0:T(8,128)(2,1)S(1)} %copy-done.3, bf16[4,576,1024]{2,1,0:T(8,128)(2,1)} %bitcast.29, bf16[4,16,576]{2,1,0:T(8,128)(2,1)S(1)} %pad.4.tok_ref), custom_call_target="tpu_custom_call" | custom-call | flops 285212672 | bytes 4718592 | tf_op jit(solution)/shard_map/attend_cache/pallas_call | solution.py:257
  33.1 1.6 %collective-permute-done.refs_1_ = bf16[8,224,128]{2,1,0:T(8,128)(2,1)S(1)} collective-permute-done((bf16[8,224,128]{2,1,0:T(8,128)(2,1)}, bf16[8,224,128]{2,1,0:T(8,128)(2,1)S(1)}, u32[]{:S(2)}, u32[]{:S(2)}) %collective-permute-start) | collective-permute-done | bytes 458784 | tf_op jit(solution)/shard_map/ppermute | solution.py:628
  34.7 0.0 all-to-all-done
  34.8 3.1 %attend_new.1 = bf16[16,2,8,1024]{3,2,1,0:T(8,128)(2,1)} custom-call(s32[4]{0:T(128)S(1)} %dynamic-slice_reduce_fusion.len_ref, bf16[2,4,16,576]{3,2,1,0:T(8,128)(2,1)S(1)} %copy-done.3, bf16[512,576]{1,0:T(8,128)(2,1)S(1)} %bitcast.25, f32[4,32,512]{2,1,0:T(8,128)} %get-tuple-element.28.acc_ref, f32[4,32,128]{2,1,0:T(8,128)} %get-tuple-element.29.side_ref, ...), custom_call_target="tpu_custom_call" | custom-call | flops 150994944 | bytes 2097152 | tf_op jit(solution)/shard_map/attend_new/pallas_call | solution.py:317
  37.9 8.5 %all-to-all-start.1 = ((bf16[32,8,1024]{2,1,0:T(8,128)(2,1)}), bf16[32,8,1024]{2,1,0:T(8,128)(2,1)S(1)}, u32[]{:S(2)}, u32[]{:S(2)}) async-start(bf16[32,8,1024]{2,1,0:T(8,128)(2,1)} %bitcast.14), calls=%async_computation.1 | async-start | bytes 1048576 | tf_op jit(solution)/shard_map/all_to_all | solution.py:579
  46.4 0.0 collective-permute-done.1.refs_2_
  46.4 0.0 collective-permute-done.2.refs_4_.refs_6_
  46.4 1.3 collective-permute-start.3
  47.7 1.5 collective-permute-start.4
  49.2 1.0 slice.8
  50.3 2.6 %collective-permute-start.5 = (bf16[1,8,224,128]{3,2,1,0:T(8,128)(2,1)S(1)}, bf16[1,8,224,128]{3,2,1,0:T(8,128)(2,1)S(1)}, u32[]{:S(2)}, u32[]{:S(2)}) collective-permute-start(bf16[1,8,224,128]{3,2,1,0:T(8,128)(2,1)S(1)} %slice.8), channel_id=1, source_target_pairs={{0,1},{1,0},{2,3},{3,2},{4,5},{5,4},{6,7},{7,6},{8,9},{9,8},{10,11... | collective-permute-start | bytes 1376264 | tf_op jit(solution)/shard_map/ppermute | solution.py:641
  52.9 1.8 %slice.9 = bf16[1,8,224,128]{3,2,1,0:T(8,128)(2,1)} slice(bf16[2,8,224,128]{3,2,1,0:T(8,128)(2,1)} %collective-permute-done.2.refs_4_.refs_6_), slice={[1:2], [0:8], [0:224], [0:128]} | slice | bytes 917504 | tf_op jit(solution)/shard_map/slice | solution.py:653
  54.7 0.0 collective-permute-start.6
  54.7 1.4 gather_heads.1.w_ref
  56.1 2.0 %collective-permute-done.3 = bf16[1,8,224,128]{3,2,1,0:T(8,128)(2,1)} collective-permute-done((bf16[1,8,224,128]{3,2,1,0:T(8,128)(2,1)}, bf16[1,8,224,128]{3,2,1,0:T(8,128)(2,1)}, u32[]{:S(2)}, u32[]{:S(2)}) %collective-permute-start.3) | collective-permute-done | bytes 458784 | tf_op jit(solution)/shard_map/ppermute | solution.py:641
  58.1 0.0 collective-permute-done.4
  58.1 3.9 %all-to-all-done.1 = bf16[32,8,1024]{2,1,0:T(8,128)(2,1)S(1)} async-done(((bf16[32,8,1024]{2,1,0:T(8,128)(2,1)}), bf16[32,8,1024]{2,1,0:T(8,128)(2,1)S(1)}, u32[]{:S(2)}, u32[]{:S(2)}) %all-to-all-start.1) | async-done | bytes 524320 | tf_op jit(solution)/shard_map/all_to_all | solution.py:579
  62.0 1.2 project.1
  63.2 7.8 %all-to-all-start.2 = ((bf16[16,32,256]{2,1,0:T(8,128)(2,1)}), bf16[16,32,256]{2,1,0:T(8,128)(2,1)S(1)}, u32[]{:S(2)}, u32[]{:S(2)}) async-start(bf16[16,32,256]{2,1,0:T(8,128)(2,1)} %bitcast.16), calls=%async_computation.2 | async-start | bytes 524288 | tf_op jit(solution)/shard_map/all_to_all | solution.py:579
  71.0 0.3 turn_hidden.1.hidden_ref
  71.2 0.0 collective-permute-done.5.refs_3_
  71.2 0.0 copy-start.7
  71.3 0.0 collective-permute-done.6.refs_5_.refs_7_
  71.3 6.8 %all-to-all-done.2.part_ref = bf16[16,32,256]{2,1,0:T(8,128)(2,1)S(1)} async-done(((bf16[16,32,256]{2,1,0:T(8,128)(2,1)}), bf16[16,32,256]{2,1,0:T(8,128)(2,1)S(1)}, u32[]{:S(2)}, u32[]{:S(2)}) %all-to-all-start.2) | async-done | bytes 262176 | tf_op jit(solution)/shard_map/all_to_all | solution.py:579
  78.1 0.8 make_mixed.1
  79.0 5.4 %all-to-all-start.3 = ((bf16[32,56,128]{2,1,0:T(8,128)(2,1)}), bf16[32,56,128]{2,1,0:T(8,128)(2,1)}, u32[]{:S(2)}, u32[]{:S(2)}) async-start(bf16[32,56,128]{2,1,0:T(8,128)(2,1)} %get-tuple-element.38), calls=%async_computation.3 | async-start | bytes 917504 | tf_op jit(solution)/shard_map/all_to_all | solution.py:579
  84.4 1.2 collective-permute-start.7
  85.6 0.0 collective-permute-start.8
  85.6 2.9 %collective-permute-start.9 = (bf16[1,8,224,128]{3,2,1,0:T(8,128)(2,1)}, bf16[1,8,224,128]{3,2,1,0:T(8,128)(2,1)S(1)}, u32[]{:S(2)}, u32[]{:S(2)}) collective-permute-start(bf16[1,8,224,128]{3,2,1,0:T(8,128)(2,1)} %collective-permute-done.4), channel_id=1, source_target_pairs={{0,7},{1,6},{2,1},{3,0},{4,3},{5,2},{6,5},{7,4},{8,15},{9,14},{10,... | collective-permute-start | bytes 1376264 | tf_op jit(solution)/shard_map/ppermute | solution.py:641
  88.5 0.0 collective-permute-done.7.refs_1_
  88.5 0.8 copy-done.9
  89.3 1.9 %collect.2.refs_0_ = bf16[6,144,1024]{2,1,0:T(8,128)(2,1)S(1)} custom-call(bf16[1,8,224,128]{3,2,1,0:T(8,128)(2,1)} %get-tuple-element.26.refs_0_, bf16[1,8,224,128]{3,2,1,0:T(8,128)(2,1)} %copy-done.9, bf16[2,8,224,128]{3,2,1,0:T(8,128)(2,1)} %collective-permute-done.1.refs_2_, bf16[1,8,224,128]{3,2,1,0:T(8,128)(2,1)} %copy-done.7, ...), custom_call_target="tpu_custom_call" | custom-call | bytes 3538944 | tf_op jit(solution)/shard_map/collect/pallas_call | solution.py:458
  91.2 8.0 %collective-permute-done.8.refs_0_.refs_4_ = bf16[1,8,224,128]{3,2,1,0:T(8,128)(2,1)S(1)} collective-permute-done((bf16[1,8,224,128]{3,2,1,0:T(8,128)(2,1)}, bf16[1,8,224,128]{3,2,1,0:T(8,128)(2,1)S(1)}, u32[]{:S(2)}, u32[]{:S(2)}) %collective-permute-start.8) | collective-permute-done | bytes 458784 | tf_op jit(solution)/shard_map/ppermute | solution.py:641
  99.2 0.0 collective-permute-done.9.refs_1_.refs_5_
  99.2 0.2 collect.3.refs_1_
  99.4 0.0 all-to-all-done.3.x_ref
  99.4 2.0 %gate_up.1 = (bf16[4,160,256]{2,1,0:T(8,128)(2,1)S(1)}, bf16[4,160,256]{2,1,0:T(8,128)(2,1)S(1)}) custom-call(s32[1]{0:T(128)} %bitcast.rank_ref, bf16[32,56,128]{2,1,0:T(8,128)(2,1)} %all-to-all-done.3.x_ref, bf16[6,144,1024]{2,1,0:T(8,128)(2,1)S(1)} %collect.2.refs_0_, bf16[2,144,1024]{2,1,0:T(8,128)(2,1)S(1)} %collect.3.refs_1_), custom_call_target="tpu_custom_call" | custom-call | flops 603979776 | bytes 2818048 | tf_op jit(solution)/shard_map/gate_up/pallas_call | solution.py:478
  101.4 2.5 %collective-permute-start.10 = (bf16[4,160,256]{2,1,0:T(8,128)(2,1)S(1)}, bf16[4,160,256]{2,1,0:T(8,128)(2,1)S(1)}, u32[]{:S(2)}, u32[]{:S(2)}) collective-permute-start(bf16[4,160,256]{2,1,0:T(8,128)(2,1)S(1)} %get-tuple-element.41), channel_id=1, source_target_pairs={{0,1},{1,0},{2,3},{3,2},{4,5},{5,4},{6,7},{7,6},{8,9},{9,8},{10,11... | collective-permute-start | bytes 983048 | tf_op jit(solution)/shard_map/ppermute | solution.py:585
  103.9 1.3 collective-permute-done.10.b_ref
  105.1 0.8 add_cores.1
  106.0 3.5 %all-to-all-start.4 = ((bf16[4,160,256]{2,1,0:T(8,128)(2,1)}), bf16[4,160,256]{2,1,0:T(8,128)(2,1)S(1)}, u32[]{:S(2)}, u32[]{:S(2)}) async-start(bf16[4,160,256]{2,1,0:T(8,128)(2,1)} %add_cores.1), calls=%async_computation.4 | async-start | bytes 655360 | tf_op jit(solution)/shard_map/all_to_all | solution.py:579
  109.4 2.5 %turn.1.w_ref = bf16[1024,640]{1,0:T(8,128)(2,1)S(1)} custom-call(bf16[1,8,224,128]{3,2,1,0:T(8,128)(2,1)} %get-tuple-element.26.refs_0_, bf16[1,8,224,128]{3,2,1,0:T(8,128)(2,1)} %copy-done.9, bf16[2,8,224,128]{3,2,1,0:T(8,128)(2,1)} %collective-permute-done.1.refs_2_, bf16[1,8,224,128]{3,2,1,0:T(8,128)(2,1)} %copy-done.7, ...), custom_call_target="tpu_custom_call" | custom-call | flops 167772160 | bytes 2621440 | tf_op jit(solution)/shard_map/turn/pallas_call | solution.py:209
  112.0 4.5 %all-to-all-done.4.part_ref = bf16[4,160,256]{2,1,0:T(8,128)(2,1)S(1)} async-done(((bf16[4,160,256]{2,1,0:T(8,128)(2,1)}), bf16[4,160,256]{2,1,0:T(8,128)(2,1)S(1)}, u32[]{:S(2)}, u32[]{:S(2)}) %all-to-all-start.4) | async-done | bytes 327712 | tf_op jit(solution)/shard_map/all_to_all | solution.py:579
  116.5 0.1 activate.1
  116.6 7.4 %all_to_all.35.same_ref = bf16[4,80,256]{2,1,0:T(8,128)(2,1)S(1)} all-to-all(bf16[4,80,256]{2,1,0:T(8,128)(2,1)S(1)} %activate.1), channel_id=1, replica_groups={{0,2,4,6},{1,3,5,7},{8,10,12,14},{9,11,13,15},{16,18,20,22},{17,19,21,2..., dimensions={0} | all-to-all | bytes 327680 | tf_op jit(solution)/shard_map/all_to_all | solution.py:579
  123.9 2.4 %collective-permute-start.11 = (bf16[4,80,256]{2,1,0:T(8,128)(2,1)S(1)}, bf16[4,80,256]{2,1,0:T(8,128)(2,1)S(1)}, u32[]{:S(2)}, u32[]{:S(2)}) collective-permute-start(bf16[4,80,256]{2,1,0:T(8,128)(2,1)S(1)} %all_to_all.35.same_ref), channel_id=1, source_target_pairs={{0,1},{1,0},{2,3},{3,2},{4,5},{5,4},{6,7},{7,6},{8,9},{9,8},{10,11... | collective-permute-start | bytes 491528 | tf_op jit(solution)/shard_map/ppermute | solution.py:585
  126.3 1.0 collective-permute-done.11.other_ref
  127.3 1.2 down.1
  128.5 23.4 %all_to_all.36.part_ref = bf16[32,56,128]{2,1,0:T(8,128)(2,1)S(1)} all-to-all(bf16[32,56,128]{2,1,0:T(8,128)(2,1)S(1)} %down.1), channel_id=1, replica_groups=mesh['z'=16,'y'=2,'tp'=8] {'z','y'}, dimensions={0} | all-to-all | bytes 917504 | tf_op jit(solution)/shard_map/all_to_all | solution.py:579
  151.9 0.9 finish.1
  (24 shorter events, 0.1 us)
Async XLA Ops:
  0.0 15.1 %copy-start.6 = (bf16[16,128,224]{1,2,0:T(8,128)(2,1)S(1)}, bf16[16,128,224]{1,2,0:T(8,128)(2,1)}, u32[]{:S(2)}) copy-start(bf16[16,128,224]{1,2,0:T(8,128)(2,1)} %param.22) | copy-start | bytes 2752516
  0.0 17.2 %copy-start.4 = (f32[7168]{0:T(1024)S(1)}, f32[7168]{0:T(1024)}, u32[]{:S(2)}) copy-start(f32[7168]{0:T(1024)} %param.24) | copy-start | bytes 86020
  3.0 31.8 %all-to-all-start = ((bf16[32,16,576]{2,1,0:T(8,128)(2,1)}), bf16[32,16,576]{2,1,0:T(8,128)(2,1)S(1)}, u32[]{:S(2)}, u32[]{:S(2)}) async-start(bf16[32,16,576]{2,1,0:T(8,128)(2,1)} %bitcast.7), calls=%async_computation | async-start | bytes 1310720 | tf_op jit(solution)/shard_map/all_to_all | solution.py:579
  15.0 11.8 %copy-start.13 = (s32[32,4]{0,1:T(4,128)S(1)}, s32[32,4]{0,1:T(4,128)}, u32[]{:S(2)}) copy-start(s32[32,4]{0,1:T(4,128)} %param.16) | copy-start | bytes 1540
  15.0 12.0 %copy-start.12 = (bf16[2,4,576]{2,1,0:T(4,128)(2,1)S(1)}, bf16[2,4,576]{2,1,0:T(4,128)(2,1)}, u32[]{:S(2)}) copy-start(bf16[2,4,576]{2,1,0:T(4,128)(2,1)} %param.20) | copy-start | bytes 27652
  15.1 12.0 %copy-start.3 = (bf16[2,4,16,576]{3,2,1,0:T(8,128)(2,1)S(1)}, bf16[2,4,16,576]{3,2,1,0:T(8,128)(2,1)}, u32[]{:S(2)}) copy-start(bf16[2,4,16,576]{3,2,1,0:T(8,128)(2,1)} %q_ref.3) | copy-start | bytes 442372
  15.1 12.0 %copy-start.5 = (s32[4]{0:T(128)S(1)}, s32[4]{0:T(128)}, u32[]{:S(2)}) copy-start(s32[4]{0:T(128)} %ctx_ref) | copy-start | bytes 52
  15.9 18.8 %collective-permute-start = (bf16[8,224,128]{2,1,0:T(8,128)(2,1)}, bf16[8,224,128]{2,1,0:T(8,128)(2,1)S(1)}, u32[]{:S(2)}, u32[]{:S(2)}) collective-permute-start(bf16[8,224,128]{2,1,0:T(8,128)(2,1)} %dynamic-slice_bitcast_fusion), channel_id=1, source_target_pairs={{0,8},{8,0},{1,9},{9,1},{2,10},{10,2},{3,11},{11,3},{4,12},{12,4},... | collective-permute-start | bytes 1376264 | tf_op jit(solution)/shard_map/ppermute | solution.py:628
  24.2 22.2 %collective-permute-start.1 = (bf16[2,8,224,128]{3,2,1,0:T(8,128)(2,1)}, bf16[2,8,224,128]{3,2,1,0:T(8,128)(2,1)}, u32[]{:S(2)}, u32[]{:S(2)}) collective-permute-start(bf16[2,8,224,128]{3,2,1,0:T(8,128)(2,1)} %get-tuple-element.30), channel_id=1, source_target_pairs={{0,2},{1,3},{2,4},{3,5},{4,6},{5,7},{6,0},{7,1},{8,10},{9,11},{10,... | collective-permute-start | bytes 2752520 | tf_op jit(solution)/shard_map/ppermute | solution.py:641
  25.4 21.0 %collective-permute-start.2 = (bf16[2,8,224,128]{3,2,1,0:T(8,128)(2,1)}, bf16[2,8,224,128]{3,2,1,0:T(8,128)(2,1)}, u32[]{:S(2)}, u32[]{:S(2)}) collective-permute-start(bf16[2,8,224,128]{3,2,1,0:T(8,128)(2,1)} %get-tuple-element.31), channel_id=1, source_target_pairs={{0,6},{1,7},{2,0},{3,1},{4,2},{5,3},{6,4},{7,5},{8,14},{9,15},{10,... | collective-permute-start | bytes 2752520 | tf_op jit(solution)/shard_map/ppermute | solution.py:641
  27.1 7.6 %copy-start = (bf16[16,512,128]{2,1,0:T(8,128)(2,1)S(1)}, bf16[16,512,128]{2,1,0:T(8,128)(2,1)}, u32[]{:S(2)}) copy-start(bf16[16,512,128]{2,1,0:T(8,128)(2,1)} %uv_ref.1) | copy-start | bytes 6291460
  34.7 3.1 %copy-start.10 = (bf16[8,224,128]{2,1,0:T(8,128)(2,1)}, bf16[8,224,128]{2,1,0:T(8,128)(2,1)S(1)}, u32[]{:S(2)}) copy-start(bf16[8,224,128]{2,1,0:T(8,128)(2,1)S(1)} %collective-permute-done.refs_1_) | copy-start | bytes 1376260
  37.9 24.1 %all-to-all-start.1 = ((bf16[32,8,1024]{2,1,0:T(8,128)(2,1)}), bf16[32,8,1024]{2,1,0:T(8,128)(2,1)S(1)}, u32[]{:S(2)}, u32[]{:S(2)}) async-start(bf16[32,8,1024]{2,1,0:T(8,128)(2,1)} %bitcast.14), calls=%async_computation.1 | async-start | bytes 1048576 | tf_op jit(solution)/shard_map/all_to_all | solution.py:579
  46.4 11.6 %collective-permute-start.3 = (bf16[1,8,224,128]{3,2,1,0:T(8,128)(2,1)}, bf16[1,8,224,128]{3,2,1,0:T(8,128)(2,1)}, u32[]{:S(2)}, u32[]{:S(2)}) collective-permute-start(bf16[1,8,224,128]{3,2,1,0:T(8,128)(2,1)} %get-tuple-element.34), channel_id=1, source_target_pairs={{0,2},{1,3},{2,4},{3,5},{4,6},{5,7},{6,0},{7,1},{8,10},{9,11},{10,... | collective-permute-start | bytes 1376264 | tf_op jit(solution)/shard_map/ppermute | solution.py:641
  47.7 10.3 %collective-permute-start.4 = (bf16[1,8,224,128]{3,2,1,0:T(8,128)(2,1)}, bf16[1,8,224,128]{3,2,1,0:T(8,128)(2,1)}, u32[]{:S(2)}, u32[]{:S(2)}) collective-permute-start(bf16[1,8,224,128]{3,2,1,0:T(8,128)(2,1)} %get-tuple-element.35), channel_id=1, source_target_pairs={{0,6},{1,7},{2,0},{3,1},{4,2},{5,3},{6,4},{7,5},{8,14},{9,15},{10,... | collective-permute-start | bytes 1376264 | tf_op jit(solution)/shard_map/ppermute | solution.py:641
  50.3 21.0 %collective-permute-start.5 = (bf16[1,8,224,128]{3,2,1,0:T(8,128)(2,1)S(1)}, bf16[1,8,224,128]{3,2,1,0:T(8,128)(2,1)S(1)}, u32[]{:S(2)}, u32[]{:S(2)}) collective-permute-start(bf16[1,8,224,128]{3,2,1,0:T(8,128)(2,1)S(1)} %slice.8), channel_id=1, source_target_pairs={{0,1},{1,0},{2,3},{3,2},{4,5},{5,4},{6,7},{7,6},{8,9},{9,8},{10,11... | collective-permute-start | bytes 1376264 | tf_op jit(solution)/shard_map/ppermute | solution.py:641
  54.7 16.6 %collective-permute-start.6 = (bf16[1,8,224,128]{3,2,1,0:T(8,128)(2,1)}, bf16[1,8,224,128]{3,2,1,0:T(8,128)(2,1)S(1)}, u32[]{:S(2)}, u32[]{:S(2)}) collective-permute-start(bf16[1,8,224,128]{3,2,1,0:T(8,128)(2,1)} %slice.9), channel_id=1, source_target_pairs={{0,1},{1,0},{2,3},{3,2},{4,5},{5,4},{6,7},{7,6},{8,9},{9,8},{10,11... | collective-permute-start | bytes 1376264 | tf_op jit(solution)/shard_map/ppermute | solution.py:641
  54.7 16.2 %copy-start.11 = (bf16[2,128,28]{1,0,2:T(2,128)(2,1)S(1)}, bf16[2,128,28]{1,0,2:T(2,128)(2,1)}, u32[]{:S(2)}) copy-start(bf16[2,128,28]{1,0,2:T(2,128)(2,1)} %param.23) | copy-start | bytes 43012
  63.2 14.9 %all-to-all-start.2 = ((bf16[16,32,256]{2,1,0:T(8,128)(2,1)}), bf16[16,32,256]{2,1,0:T(8,128)(2,1)S(1)}, u32[]{:S(2)}, u32[]{:S(2)}) async-start(bf16[16,32,256]{2,1,0:T(8,128)(2,1)} %bitcast.16), calls=%async_computation.2 | async-start | bytes 524288 | tf_op jit(solution)/shard_map/all_to_all | solution.py:579
  71.2 17.3 %copy-start.7 = (bf16[1,8,224,128]{3,2,1,0:T(8,128)(2,1)}, bf16[1,8,224,128]{3,2,1,0:T(8,128)(2,1)S(1)}, u32[]{:S(2)}) copy-start(bf16[1,8,224,128]{3,2,1,0:T(8,128)(2,1)S(1)} %collective-permute-done.5.refs_3_) | copy-start | bytes 1376260
  71.3 13.1 %copy-start.8 = (bf16[1,8,224,128]{3,2,1,0:T(8,128)(2,1)}, bf16[1,8,224,128]{3,2,1,0:T(8,128)(2,1)S(1)}, u32[]{:S(2)}) copy-start(bf16[1,8,224,128]{3,2,1,0:T(8,128)(2,1)S(1)} %collective-permute-done.6.refs_5_.refs_7_) | copy-start | bytes 1376260
  79.0 20.4 %all-to-all-start.3 = ((bf16[32,56,128]{2,1,0:T(8,128)(2,1)}), bf16[32,56,128]{2,1,0:T(8,128)(2,1)}, u32[]{:S(2)}, u32[]{:S(2)}) async-start(bf16[32,56,128]{2,1,0:T(8,128)(2,1)} %get-tuple-element.38), calls=%async_computation.3 | async-start | bytes 917504 | tf_op jit(solution)/shard_map/all_to_all | solution.py:579
  84.4 4.1 %collective-permute-start.7 = (bf16[1,8,224,128]{3,2,1,0:T(8,128)(2,1)}, bf16[1,8,224,128]{3,2,1,0:T(8,128)(2,1)S(1)}, u32[]{:S(2)}, u32[]{:S(2)}) collective-permute-start(bf16[1,8,224,128]{3,2,1,0:T(8,128)(2,1)} %get-tuple-element.39), channel_id=1, source_target_pairs={{0,1},{1,0},{2,3},{3,2},{4,5},{5,4},{6,7},{7,6},{8,9},{9,8},{10,11... | collective-permute-start | bytes 1376264 | tf_op jit(solution)/shard_map/ppermute | solution.py:641
  85.6 13.6 %collective-permute-start.8 = (bf16[1,8,224,128]{3,2,1,0:T(8,128)(2,1)}, bf16[1,8,224,128]{3,2,1,0:T(8,128)(2,1)S(1)}, u32[]{:S(2)}, u32[]{:S(2)}) collective-permute-start(bf16[1,8,224,128]{3,2,1,0:T(8,128)(2,1)} %collective-permute-done.3), channel_id=1, source_target_pairs={{0,2},{1,3},{2,4},{3,5},{4,6},{5,7},{6,0},{7,1},{8,10},{9,11},{10,... | collective-permute-start | bytes 1376264 | tf_op jit(solution)/shard_map/ppermute | solution.py:641
  85.6 13.6 %collective-permute-start.9 = (bf16[1,8,224,128]{3,2,1,0:T(8,128)(2,1)}, bf16[1,8,224,128]{3,2,1,0:T(8,128)(2,1)S(1)}, u32[]{:S(2)}, u32[]{:S(2)}) collective-permute-start(bf16[1,8,224,128]{3,2,1,0:T(8,128)(2,1)} %collective-permute-done.4), channel_id=1, source_target_pairs={{0,7},{1,6},{2,1},{3,0},{4,3},{5,2},{6,5},{7,4},{8,15},{9,14},{10,... | collective-permute-start | bytes 1376264 | tf_op jit(solution)/shard_map/ppermute | solution.py:641
  88.5 0.8 copy-start.9
  99.2 2.2 %copy-start.1 = (bf16[1,8,224,128]{3,2,1,0:T(8,128)(2,1)}, bf16[1,8,224,128]{3,2,1,0:T(8,128)(2,1)S(1)}, u32[]{:S(2)}) copy-start(bf16[1,8,224,128]{3,2,1,0:T(8,128)(2,1)S(1)} %collective-permute-done.8.refs_0_.refs_4_) | copy-start | bytes 1376260
  99.2 2.2 %copy-start.2 = (bf16[1,8,224,128]{3,2,1,0:T(8,128)(2,1)}, bf16[1,8,224,128]{3,2,1,0:T(8,128)(2,1)S(1)}, u32[]{:S(2)}) copy-start(bf16[1,8,224,128]{3,2,1,0:T(8,128)(2,1)S(1)} %collective-permute-done.9.refs_1_.refs_5_) | copy-start | bytes 1376260
  101.4 3.8 %collective-permute-start.10 = (bf16[4,160,256]{2,1,0:T(8,128)(2,1)S(1)}, bf16[4,160,256]{2,1,0:T(8,128)(2,1)S(1)}, u32[]{:S(2)}, u32[]{:S(2)}) collective-permute-start(bf16[4,160,256]{2,1,0:T(8,128)(2,1)S(1)} %get-tuple-element.41), channel_id=1, source_target_pairs={{0,1},{1,0},{2,3},{3,2},{4,5},{5,4},{6,7},{7,6},{8,9},{9,8},{10,11... | collective-permute-start | bytes 983048 | tf_op jit(solution)/shard_map/ppermute | solution.py:585
  106.0 10.5 %all-to-all-start.4 = ((bf16[4,160,256]{2,1,0:T(8,128)(2,1)}), bf16[4,160,256]{2,1,0:T(8,128)(2,1)S(1)}, u32[]{:S(2)}, u32[]{:S(2)}) async-start(bf16[4,160,256]{2,1,0:T(8,128)(2,1)} %add_cores.1), calls=%async_computation.4 | async-start | bytes 655360 | tf_op jit(solution)/shard_map/all_to_all | solution.py:579
  123.9 3.4 %collective-permute-start.11 = (bf16[4,80,256]{2,1,0:T(8,128)(2,1)S(1)}, bf16[4,80,256]{2,1,0:T(8,128)(2,1)S(1)}, u32[]{:S(2)}, u32[]{:S(2)}) collective-permute-start(bf16[4,80,256]{2,1,0:T(8,128)(2,1)S(1)} %all_to_all.35.same_ref), channel_id=1, source_target_pairs={{0,1},{1,0},{2,3},{3,2},{4,5},{5,4},{6,7},{7,6},{8,9},{9,8},{10,11... | collective-permute-start | bytes 491528 | tf_op jit(solution)/shard_map/ppermute | solution.py:585

commit v4 on v3

--- a/solution.py
+++ b/solution.py
@@ -71,7 +71,7 @@
     return jnp.where(iota(shape, 1) == wanted, 1.0, 0.0).astype(bf16)
 
 
-def route_kernel(slot_ref, len_ref, rows_ref, out_ref):
+def route_kernel(rank_ref, slot_ref, len_ref, rows_ref, out_ref):
     count = slot_ref.shape[1]
     per_owner, owners = len_ref.shape
     total = rows_ref.shape[1]
@@ -95,25 +95,29 @@
     inside = (at >= start_col) & (at < start_col + rows_col)
     shift = jnp.sum(jnp.where(inside, target_col - start_col, 0), axis=0, keepdims=True)
     target = iota((1, total), 1) + shift
-    pick = jnp.where(iota((total, total), 0) == target, 1.0, 0.0).astype(bf16)
+    half = OWN_TOK // 2
+    row = iota((total // 2, total), 0)
+    wanted = row // half * OWN_TOK + rank_ref[0] % 2 * half + row % half
+    pick = jnp.where(wanted == target, 1.0, 0.0).astype(bf16)
     out_ref[...] = dot(pick, rows_ref[...], NT).astype(bf16)
 
 
-def route(request_slot, new_lengths, prefill_latent):
+def route(rank, request_slot, new_lengths, prefill_latent):
     total, width = prefill_latent.shape
     return call(
         route_kernel,
-        jax.ShapeDtypeStruct((total, width), bf16),
-        (2 * total * total * width, 4 * total * width),
+        jax.ShapeDtypeStruct((total // 2, width), bf16),
+        (total * total * width, 3 * total * width),
         grid=(1,),
         in_specs=[
+            pl.BlockSpec(memory_space=pltpu.SMEM),
             pl.BlockSpec((1, request_slot.size), lambda c: (0, 0)),
             pl.BlockSpec(new_lengths.shape[::-1], lambda c: (0, 0)),
             pl.BlockSpec((width, total), lambda c: (0, 0)),
         ],
-        out_specs=pl.BlockSpec((total, width), lambda c: (0, 0)),
+        out_specs=pl.BlockSpec((total // 2, width), lambda c: (0, 0)),
         name="route",
-    )(in_hbm(request_slot.reshape(1, -1)), in_hbm(new_lengths.T), in_hbm(prefill_latent.T))
+    )(rank, in_hbm(request_slot.reshape(1, -1)), in_hbm(new_lengths.T), in_hbm(prefill_latent.T))
 
 
 def piece_places(tp):
@@ -270,14 +274,17 @@
     )(ctx_lengths, queries, kv_cache, tokens)
 
 
-def merge_kernel(len_ref, q_ref, new_ref, acc_ref, side_ref, uv_ref, out_ref):
+def merge_kernel(rank_ref, len_ref, q_ref, new_ref, other_ref, acc_ref, side_ref, uv_ref, out_ref):
     scale = QKD ** (-0.5)
     steps, per_owner, heads, width = q_ref.shape
     rows = steps * heads
-    new = new_ref[...]
+    new = jnp.concatenate([new_ref[...], other_ref[...]], axis=0)
     query = jnp.concatenate([q_ref[:, q].reshape(rows, width) for q in range(per_owner)], axis=0)
     scores = dot(query, new, NT) * scale
-    place = iota(scores.shape, 1) % OWN_TOK
+    half = OWN_TOK // 2
+    column = iota(scores.shape, 1)
+    core = jnp.where(column < scores.shape[1] // 2, rank_ref[0] % 2, 1 - rank_ref[0] % 2)
+    place = core * half + column % half
     owner_row = iota(scores.shape, 0) // rows
     first = jnp.zeros(scores.shape, i32)
     last = jnp.zeros(scores.shape, i32)
@@ -311,7 +318,7 @@
         )
 
 
-def attend_new(my_lengths, queries, new_rows, acc, side, w_uv, dp, parts):
+def attend_new(rank, my_lengths, queries, new_rows, other_rows, acc, side, w_uv, dp, parts):
     steps, per_owner, heads, _ = queries.shape
     whole = pl.BlockSpec(memory_space=pltpu.VMEM)
     return call(
@@ -319,10 +326,12 @@
         jax.ShapeDtypeStruct(
             (dp // parts, parts, per_owner * steps, heads // parts * w_uv.shape[2]), bf16
         ),
-        (4 * new_rows.size * per_owner * steps * heads, 2 * w_uv.size),
+        (8 * new_rows.size * per_owner * steps * heads, 2 * w_uv.size),
         grid=(1,),
         in_specs=[
             pl.BlockSpec(memory_space=pltpu.SMEM),
+            pl.BlockSpec(memory_space=pltpu.SMEM),
+            whole,
             whole,
             whole,
             pl.BlockSpec(acc.shape, lambda c: (0, 0, 0)),
@@ -331,7 +340,7 @@
         ],
         out_specs=whole,
         name="attend_new",
-    )(my_lengths, queries, new_rows, in_hbm(acc), in_hbm(side), w_uv)
+    )(rank, my_lengths, queries, new_rows, other_rows, in_hbm(acc), in_hbm(side), w_uv)
 
 
 def gather_heads_kernel(rank_ref, *refs):
@@ -360,7 +369,7 @@
             out_specs=pl.BlockSpec(memory_space=pltpu.VMEM),
         ),
         name="gather_heads",
-    )(rank, in_hbm(own), *[in_hbm(piece) for piece in pieces])
+    )(rank, in_hbm(own), *pieces)
 
 
 def project_kernel(w_ref, x_ref, out_ref):
@@ -612,10 +621,10 @@
     unit_pad = -(-units // 16) * 16
     total = hidden.shape[0] * hidden.shape[1]
 
-    routed = route(request_slot, new_lengths, prefill_latent)
-    incoming = exchange(routed.reshape(dp, OWN_TOK, -1), both).reshape(dp * OWN_TOK, -1)
-
     rank = tp_rank.astype(i32).reshape(1)
+    routed = route(rank, request_slot, new_lengths, prefill_latent)
+    incoming = exchange(routed.reshape(dp, OWN_TOK // 2, -1), both).reshape(routed.shape)
+
     arrays = reshard(rank, ffn_gain, w_gate, w_up, w_down, dp, tp, width, unit_pad)
 
     y_rank = lax.axis_index("y").astype(i32).reshape(1)
@@ -626,7 +635,6 @@
         piece = lax.dynamic_slice_in_dim(w_turned, (y_rank[0] + k) % ring * each, each, 0)
         pairs = [(j, (j + k) % ring) for j in range(ring)]
         out_pieces.append(lax.ppermute(piece, "y", pairs))
-    incoming, _ = lax.optimization_barrier((incoming, out_pieces))
 
     ctx_lengths, _ = lax.optimization_barrier((ctx_lengths, arrays[0]))
     tokens = jnp.pad(step_latents.transpose(1, 0, 2), ((0, 0), (0, 16 - steps), (0, 0)))
@@ -634,7 +642,9 @@
         ctx_lengths, queries, in_hbm(kv_cache.transpose(0, 2, 1)), tokens
     )
     my_lengths = lax.dynamic_index_in_dim(new_lengths, dp_rank, 0, keepdims=False)
-    heads_out = attend_new(my_lengths, queries, incoming, acc, side, w_uv, dp, ring)
+    heads_out = attend_new(
+        rank, my_lengths, queries, incoming, swap_cores(incoming), acc, side, w_uv, dp, ring
+    )
     every = exchange(heads_out.reshape((dp,) + heads_out.shape[2:]), both).reshape(total, -1)
 
     def along_x(piece, k, sign):
@@ -651,10 +661,10 @@
     if tp > 2:
         pieces[2], pieces[6] = (plus, 0), (minus, 0)
         swapped = [along_x(plus[1:], 1, 1), along_x(minus[1:], 1, 1)]
-        parts, _ = lax.optimization_barrier((parts, swapped))
+        far = [along_x(far[0], 2, 1), along_x(far[1], 3, -1)]
+        parts, _ = lax.optimization_barrier((parts, (swapped, far)))
         pieces[3], pieces[7] = (swapped[0], 0), (swapped[1], 0)
-        pieces[4] = along_x(far[0], 2, 1), 0
-        pieces[5] = along_x(far[1], 3, -1), 0
+        pieces[4], pieces[5] = (far[0], 0), (far[1], 0)
     pieces[1] = along_x(arrays[1], 1, 1), 0
     pieces = [pieces[k] for k in range(tp)]
     hidden_t = call(

time: 154 us -> 153 us (level)
  blocking collectives: 30.7 us -> 26.8 us
  waiting for transfers between devices: 29.1 us -> 31.7 us
  starting transfers between devices: 55.5 us -> 57.3 us
    all_to_all x5, waiting for transfers between devices: 15.3 us -> 22.1 us  [exchange(): lax.all_to_all(x, axis, split_axis=0, concat_axis=0, tiled=True, axis_ind...]
    ppermute x9, waiting for transfers between devices: 9.98 us -> 5.39 us  [along_x(): lax.ppermute(piece, 'tp', [(j, partner(j, tp, k, sign)) for j in range(tp)])]
    all_to_all x2, blocking collectives: 30.7 us -> 26.8 us  [exchange(): lax.all_to_all(x, axis, split_axis=0, concat_axis=0, tiled=True, axis_ind...]
    ppermute x2 -> x3, starting transfers between devices: 4.85 us -> 8.01 us  [swap_cores(): lax.ppermute(x, 'tp', [(j, j ^ 1) for j in range(lax.axis_size('tp'))])]
    all_to_all x5, starting transfers between devices: 37.2 us -> 34.5 us  [exchange(): lax.all_to_all(x, axis, split_axis=0, concat_axis=0, tiled=True, axis_ind...]
  transfers between devices with their start and end apart: 17 -> 18, of which waited for: 8 -> 9; matrix products, arithmetic and copies ran while one was open for 3% -> 2% of each run, Pallas kernels for 15% -> 15%
where the time goes in v4:
time: 153 us; the launch traced here: 152 us
  starting transfers between devices  57.3 us (37%)
  Pallas kernels  31.7 us (21%)
  waiting for transfers between devices  31.7 us (21%)
  blocking collectives  26.8 us (18%)
  local copies, waits for them, and re-layouts  4.5 us (3%)
    all_to_all x5, starting transfers between devices, exchange(): lax.all_to_all(x, axis, split_axis=0, concat_axis=0, tiled=True, axis_ind...  34.5 us
    all_to_all x2, blocking collectives, exchange(): lax.all_to_all(x, axis, split_axis=0, concat_axis=0, tiled=True, axis_ind...  26.8 us
    all_to_all x5, waiting for transfers between devices, exchange(): lax.all_to_all(x, axis, split_axis=0, concat_axis=0, tiled=True, axis_ind...  22.1 us
    ppermute x9, starting transfers between devices, along_x(): lax.ppermute(piece, 'tp', [(j, partner(j, tp, k, sign)) for j in range(tp)])  13.5 us
    ppermute x3, starting transfers between devices, swap_cores(): lax.ppermute(x, 'tp', [(j, j ^ 1) for j in range(lax.axis_size('tp'))])  8.01 us
    pallas_call x1, Pallas kernels, reshard(): call(functools.partial(reshard_kernel, tp, width), tuple((pltpu.HBM((size...  7.03 us
    pallas_call x1, Pallas kernels, attend_cache(): call(cache_kernel, (pltpu.HBM((per_owner, rows, LAT), f32), pltpu.HBM((pe...  5.99 us
    ppermute x9, waiting for transfers between devices, along_x(): lax.ppermute(piece, 'tp', [(j, partner(j, tp, k, sign)) for j in range(tp)])  5.39 us
  transfers between devices with their start and end apart: 18, of which 9 were waited for; matrix products, arithmetic and copies ran while one was open for 2% of the time, Pallas kernels for 15%

profile of v4, /device:TPU:1, one launch (start us, length us, event | category | flops | bytes accessed | tf_op | source)
XLA Modules:
  0.0 152.3 jit_solution(1758204344945851461)
XLA Ops:
  0.0 2.6 %route.1 = bf16[256,576]{1,0:T(8,128)(2,1)} custom-call(s32[1]{0:T(128)} %bitcast.rank_ref, s32[1,128]{1,0:T(1,128)} %bitcast.39, s32[4,32]{1,0:T(4,128)} %bitcast.38, bf16[576,512]{1,0:T(8,128)(2,1)} %bitcast.34), custom_call_target="tpu_custom_call" | custom-call | flops 150994944 | bytes 884736 | tf_op jit(solution)/shard_map/route/pallas_call | solution.py:107
  2.6 12.2 %all-to-all-start = ((bf16[32,8,576]{2,1,0:T(8,128)(2,1)}), bf16[32,8,576]{2,1,0:T(8,128)(2,1)S(1)}, u32[]{:S(2)}, u32[]{:S(2)}) async-start(bf16[32,8,576]{2,1,0:T(8,128)(2,1)} %bitcast.7), calls=%async_computation | async-start | bytes 655360 | tf_op jit(solution)/shard_map/all_to_all | solution.py:588
  14.8 0.0 copy-start.4
  14.8 0.7 copy-done.4
  15.6 7.0 %reshard.1 = (bf16[1,8,224,128]{3,2,1,0:T(8,128)(2,1)}, bf16[1,8,224,128]{3,2,1,0:T(8,128)(2,1)}, bf16[2,8,224,128]{3,2,1,0:T(8,128)(2,1)}, bf16[2,8,224,128]{3,...) custom-call(s32[1]{0:T(128)} %bitcast.rank_ref, f32[1,7168]{1,0:T(1,128)S(1)} %bitcast.29, ...), custom_call_target="tpu_custom_call" | custom-call | flops 792723456 | bytes 7225344 | tf_op jit(solution)/shard_map/reshard/pallas_call | solution.py:176
  22.6 1.2 collective-permute-start.2
  23.8 1.5 collective-permute-start.3
  25.3 2.1 %all-to-all-done = bf16[32,8,576]{2,1,0:T(8,128)(2,1)S(1)} async-done(((bf16[32,8,576]{2,1,0:T(8,128)(2,1)}), bf16[32,8,576]{2,1,0:T(8,128)(2,1)S(1)}, u32[]{:S(2)}, u32[]{:S(2)}) %all-to-all-start) | async-done | bytes 294944 | tf_op jit(solution)/shard_map/all_to_all | solution.py:588
  27.4 2.4 %collective-permute-start.1 = (bf16[256,576]{1,0:T(8,128)(2,1)S(1)}, bf16[256,576]{1,0:T(8,128)(2,1)S(1)}, u32[]{:S(2)}, u32[]{:S(2)}) collective-permute-start(bf16[256,576]{1,0:T(8,128)(2,1)S(1)} %bitcast.26), channel_id=1, source_target_pairs={{0,1},{1,0},{2,3},{3,2},{4,5},{5,4},{6,7},{7,6},{8,9},{9,8},{10,11... | collective-permute-start | bytes 884744 | tf_op jit(solution)/shard_map/ppermute | solution.py:594
  29.8 0.2 dynamic-slice_reduce_fusion.len_ref
  30.0 0.0 copy-start
  30.0 6.0 %attend_cache.1 = (f32[4,32,512]{2,1,0:T(8,128)}, f32[4,32,128]{2,1,0:T(8,128)}) custom-call(s32[4]{0:T(128)S(1)} %copy-done.5, bf16[2,4,16,576]{3,2,1,0:T(8,128)(2,1)S(1)} %copy-done.3, bf16[4,576,1024]{2,1,0:T(8,128)(2,1)} %bitcast.30, bf16[4,16,576]{2,1,0:T(8,128)(2,1)S(1)} %pad.4.tok_ref), custom_call_target="tpu_custom_call" | custom-call | flops 285212672 | bytes 4718592 | tf_op jit(solution)/shard_map/attend_cache/pallas_call | solution.py:261
  36.0 0.0 collective-permute-done.1.other_ref
  36.0 0.0 copy-done
  36.0 0.0 copy-start.7
  36.0 3.1 %attend_new.1 = bf16[16,2,8,1024]{3,2,1,0:T(8,128)(2,1)} custom-call(s32[1]{0:T(128)} %bitcast.rank_ref, s32[4]{0:T(128)S(1)} %dynamic-slice_reduce_fusion.len_ref, bf16[2,4,16,576]{3,2,1,0:T(8,128)(2,1)S(1)} %copy-done.3, bf16[256,576]{1,0:T(8,128)(2,1)S(1)} %bitcast.27, bf16[256,576]{1,0:T(8,128)(2,1)S(1)} %collective-permute-done.1.other_ref, ...), custom_call_target="tpu_custom_call" | custom-call | flops 150994944 | bytes 2097152 | tf_op jit(solution)/shard_map/attend_new/pallas_call | solution.py:324
  39.1 6.5 %all-to-all-start.1 = ((bf16[32,8,1024]{2,1,0:T(8,128)(2,1)}), bf16[32,8,1024]{2,1,0:T(8,128)(2,1)S(1)}, u32[]{:S(2)}, u32[]{:S(2)}) async-start(bf16[32,8,1024]{2,1,0:T(8,128)(2,1)} %bitcast.14), calls=%async_computation.1 | async-start | bytes 1048576 | tf_op jit(solution)/shard_map/all_to_all | solution.py:588
  45.6 0.0 collective-permute-done.2.refs_2_
  45.7 0.0 collective-permute-done.3.refs_4_.refs_6_
  45.7 0.3 collective-permute-start.4
  45.9 2.5 %collective-permute-start.5 = (bf16[1,8,224,128]{3,2,1,0:T(8,128)(2,1)S(1)}, bf16[1,8,224,128]{3,2,1,0:T(8,128)(2,1)}, u32[]{:S(2)}, u32[]{:S(2)}) collective-permute-start(bf16[1,8,224,128]{3,2,1,0:T(8,128)(2,1)S(1)} %copy-done.13), channel_id=1, source_target_pairs={{0,6},{1,7},{2,0},{3,1},{4,2},{5,3},{6,4},{7,5},{8,14},{9,15},{10,... | collective-permute-start | bytes 1376264 | tf_op jit(solution)/shard_map/ppermute | solution.py:651
  48.5 1.3 collective-permute-start
  49.8 0.8 slice.8
  50.6 2.0 %collective-permute-start.6 = (bf16[1,8,224,128]{3,2,1,0:T(8,128)(2,1)}, bf16[1,8,224,128]{3,2,1,0:T(8,128)(2,1)S(1)}, u32[]{:S(2)}, u32[]{:S(2)}) collective-permute-start(bf16[1,8,224,128]{3,2,1,0:T(8,128)(2,1)} %slice.8), channel_id=1, source_target_pairs={{0,1},{1,0},{2,3},{3,2},{4,5},{5,4},{6,7},{7,6},{8,9},{9,8},{10,11... | collective-permute-start | bytes 1376264 | tf_op jit(solution)/shard_map/ppermute | solution.py:651
  52.6 1.8 %slice.9 = bf16[1,8,224,128]{3,2,1,0:T(8,128)(2,1)} slice(bf16[2,8,224,128]{3,2,1,0:T(8,128)(2,1)} %collective-permute-done.3.refs_4_.refs_6_), slice={[1:2], [0:8], [0:224], [0:128]} | slice | bytes 917504 | tf_op jit(solution)/shard_map/slice | solution.py:663
  54.4 0.0 collective-permute-start.7
  54.4 3.7 %collective-permute-done.4 = bf16[1,8,224,128]{3,2,1,0:T(8,128)(2,1)} collective-permute-done((bf16[1,8,224,128]{3,2,1,0:T(8,128)(2,1)}, bf16[1,8,224,128]{3,2,1,0:T(8,128)(2,1)}, u32[]{:S(2)}, u32[]{:S(2)}) %collective-permute-start.4) | collective-permute-done | bytes 458784 | tf_op jit(solution)/shard_map/ppermute | solution.py:651
  58.1 0.0 collective-permute-start.8
  58.1 0.0 collective-permute-done.5
  58.1 4.9 %collective-permute-start.9 = (bf16[1,8,224,128]{3,2,1,0:T(8,128)(2,1)}, bf16[1,8,224,128]{3,2,1,0:T(8,128)(2,1)S(1)}, u32[]{:S(2)}, u32[]{:S(2)}) collective-permute-start(bf16[1,8,224,128]{3,2,1,0:T(8,128)(2,1)} %collective-permute-done.5), channel_id=1, source_target_pairs={{0,7},{1,6},{2,1},{3,0},{4,3},{5,2},{6,5},{7,4},{8,15},{9,14},{10,... | collective-permute-start | bytes 1376264 | tf_op jit(solution)/shard_map/ppermute | solution.py:651
  63.0 1.9 %collective-permute-done.refs_1_ = bf16[8,224,128]{2,1,0:T(8,128)(2,1)S(1)} collective-permute-done((bf16[8,224,128]{2,1,0:T(8,128)(2,1)S(1)}, bf16[8,224,128]{2,1,0:T(8,128)(2,1)S(1)}, u32[]{:S(2)}, u32[]{:S(2)}) %collective-permute-start) | collective-permute-done | bytes 458784 | tf_op jit(solution)/shard_map/ppermute | solution.py:637
  64.9 1.3 gather_heads.1.w_ref
  66.2 0.0 all-to-all-done.1
  66.2 1.2 project.1
  67.4 4.3 %all-to-all-start.2 = ((bf16[16,32,256]{2,1,0:T(8,128)(2,1)}), bf16[16,32,256]{2,1,0:T(8,128)(2,1)S(1)}, u32[]{:S(2)}, u32[]{:S(2)}) async-start(bf16[16,32,256]{2,1,0:T(8,128)(2,1)} %bitcast.16), calls=%async_computation.2 | async-start | bytes 524288 | tf_op jit(solution)/shard_map/all_to_all | solution.py:588
  71.8 0.3 turn_hidden.1.hidden_ref
  72.1 0.0 collective-permute-done.6.refs_3_
  72.1 0.0 copy-start.8
  72.1 0.0 collective-permute-done.7.refs_5_.refs_7_
  72.1 0.0 collective-permute-done.8.refs_0_.refs_4_
  72.1 0.0 collective-permute-done.9.refs_1_.refs_5_
  72.2 6.9 %all-to-all-done.2.part_ref = bf16[16,32,256]{2,1,0:T(8,128)(2,1)S(1)} async-done(((bf16[16,32,256]{2,1,0:T(8,128)(2,1)}), bf16[16,32,256]{2,1,0:T(8,128)(2,1)S(1)}, u32[]{:S(2)}, u32[]{:S(2)}) %all-to-all-start.2) | async-done | bytes 262176 | tf_op jit(solution)/shard_map/all_to_all | solution.py:588
  79.0 0.8 make_mixed.1
  79.9 8.0 %all-to-all-start.3 = ((bf16[32,56,128]{2,1,0:T(8,128)(2,1)}), bf16[32,56,128]{2,1,0:T(8,128)(2,1)}, u32[]{:S(2)}, u32[]{:S(2)}) async-start(bf16[32,56,128]{2,1,0:T(8,128)(2,1)} %get-tuple-element.36), calls=%async_computation.3 | async-start | bytes 917504 | tf_op jit(solution)/shard_map/all_to_all | solution.py:588
  87.9 1.2 collective-permute-start.10
  89.0 1.7 %collective-permute-done.10.refs_1_ = bf16[1,8,224,128]{3,2,1,0:T(8,128)(2,1)S(1)} collective-permute-done((bf16[1,8,224,128]{3,2,1,0:T(8,128)(2,1)}, bf16[1,8,224,128]{3,2,1,0:T(8,128)(2,1)S(1)}, u32[]{:S(2)}, u32[]{:S(2)}) %collective-permute-start.10) | collective-permute-done | bytes 458784 | tf_op jit(solution)/shard_map/ppermute | solution.py:651
  90.7 0.8 copy-done.9
  91.5 1.9 %collect.2.refs_0_ = bf16[6,144,1024]{2,1,0:T(8,128)(2,1)S(1)} custom-call(bf16[1,8,224,128]{3,2,1,0:T(8,128)(2,1)} %get-tuple-element.24.refs_0_, bf16[1,8,224,128]{3,2,1,0:T(8,128)(2,1)} %copy-done.9, bf16[2,8,224,128]{3,2,1,0:T(8,128)(2,1)} %copy-done.6, bf16[1,8,224,128]{3,2,1,0:T(8,128)(2,1)} %copy-done.8, ...), custom_call_target="tpu_custom_call" | custom-call | bytes 3538944 | tf_op jit(solution)/shard_map/collect/pallas_call | solution.py:467
  93.4 0.2 collect.3.refs_1_
  93.6 8.6 %all-to-all-done.3.x_ref = bf16[32,56,128]{2,1,0:T(8,128)(2,1)} async-done(((bf16[32,56,128]{2,1,0:T(8,128)(2,1)}), bf16[32,56,128]{2,1,0:T(8,128)(2,1)}, u32[]{:S(2)}, u32[]{:S(2)}) %all-to-all-start.3) | async-done | bytes 458784 | tf_op jit(solution)/shard_map/all_to_all | solution.py:588
  102.2 1.8 %gate_up.1 = (bf16[4,160,256]{2,1,0:T(8,128)(2,1)S(1)}, bf16[4,160,256]{2,1,0:T(8,128)(2,1)S(1)}) custom-call(s32[1]{0:T(128)} %bitcast.rank_ref, bf16[32,56,128]{2,1,0:T(8,128)(2,1)} %all-to-all-done.3.x_ref, bf16[6,144,1024]{2,1,0:T(8,128)(2,1)S(1)} %collect.2.refs_0_, bf16[2,144,1024]{2,1,0:T(8,128)(2,1)S(1)} %collect.3.refs_1_), custom_call_target="tpu_custom_call" | custom-call | flops 603979776 | bytes 2818048 | tf_op jit(solution)/shard_map/gate_up/pallas_call | solution.py:487
  104.0 3.3 %collective-permute-start.11 = (bf16[4,160,256]{2,1,0:T(8,128)(2,1)S(1)}, bf16[4,160,256]{2,1,0:T(8,128)(2,1)S(1)}, u32[]{:S(2)}, u32[]{:S(2)}) collective-permute-start(bf16[4,160,256]{2,1,0:T(8,128)(2,1)S(1)} %get-tuple-element.39), channel_id=1, source_target_pairs={{0,1},{1,0},{2,3},{3,2},{4,5},{5,4},{6,7},{7,6},{8,9},{9,8},{10,11... | collective-permute-start | bytes 983048 | tf_op jit(solution)/shard_map/ppermute | solution.py:594
  107.3 1.3 collective-permute-done.11.b_ref
  108.6 0.8 add_cores.1
  109.4 3.5 %all-to-all-start.4 = ((bf16[4,160,256]{2,1,0:T(8,128)(2,1)}), bf16[4,160,256]{2,1,0:T(8,128)(2,1)S(1)}, u32[]{:S(2)}, u32[]{:S(2)}) async-start(bf16[4,160,256]{2,1,0:T(8,128)(2,1)} %add_cores.1), calls=%async_computation.4 | async-start | bytes 655360 | tf_op jit(solution)/shard_map/all_to_all | solution.py:588
  112.9 2.5 %turn.1.w_ref = bf16[1024,640]{1,0:T(8,128)(2,1)S(1)} custom-call(bf16[1,8,224,128]{3,2,1,0:T(8,128)(2,1)} %get-tuple-element.24.refs_0_, bf16[1,8,224,128]{3,2,1,0:T(8,128)(2,1)} %copy-done.9, bf16[2,8,224,128]{3,2,1,0:T(8,128)(2,1)} %copy-done.6, bf16[1,8,224,128]{3,2,1,0:T(8,128)(2,1)} %copy-done.8, bf16[1,8,224,128]{3,2,1,0:T(8,128)(2,1)} %copy-done.1, ...), custom_call_target="tpu_custom_call" | custom-call | flops 167772160 | bytes 2621440 | tf_op jit(solution)/shard_map/turn/pallas_call | solution.py:213
  115.4 4.5 %all-to-all-done.4.part_ref = bf16[4,160,256]{2,1,0:T(8,128)(2,1)S(1)} async-done(((bf16[4,160,256]{2,1,0:T(8,128)(2,1)}), bf16[4,160,256]{2,1,0:T(8,128)(2,1)S(1)}, u32[]{:S(2)}, u32[]{:S(2)}) %all-to-all-start.4) | async-done | bytes 327712 | tf_op jit(solution)/shard_map/all_to_all | solution.py:588
  120.0 0.1 activate.1
  120.0 7.4 %all_to_all.35.same_ref = bf16[4,80,256]{2,1,0:T(8,128)(2,1)S(1)} all-to-all(bf16[4,80,256]{2,1,0:T(8,128)(2,1)S(1)} %activate.1), channel_id=1, replica_groups={{0,2,4,6},{1,3,5,7},{8,10,12,14},{9,11,13,15},{16,18,20,22},{17,19,21,2..., dimensions={0} | all-to-all | bytes 327680 | tf_op jit(solution)/shard_map/all_to_all | solution.py:588
  127.4 2.4 %collective-permute-start.12 = (bf16[4,80,256]{2,1,0:T(8,128)(2,1)S(1)}, bf16[4,80,256]{2,1,0:T(8,128)(2,1)S(1)}, u32[]{:S(2)}, u32[]{:S(2)}) collective-permute-start(bf16[4,80,256]{2,1,0:T(8,128)(2,1)S(1)} %all_to_all.35.same_ref), channel_id=1, source_target_pairs={{0,1},{1,0},{2,3},{3,2},{4,5},{5,4},{6,7},{7,6},{8,9},{9,8},{10,11... | collective-permute-start | bytes 491528 | tf_op jit(solution)/shard_map/ppermute | solution.py:594
  129.7 1.0 collective-permute-done.12.other_ref
  130.8 1.2 down.1
  132.0 19.4 %all_to_all.36.part_ref = bf16[32,56,128]{2,1,0:T(8,128)(2,1)S(1)} all-to-all(bf16[32,56,128]{2,1,0:T(8,128)(2,1)S(1)} %down.1), channel_id=1, replica_groups=mesh['z'=16,'y'=2,'tp'=8] {'z','y'}, dimensions={0} | all-to-all | bytes 917504 | tf_op jit(solution)/shard_map/all_to_all | solution.py:588
  151.4 0.9 finish.1
  (26 shorter events, 0.1 us)
Async XLA Ops:
  2.6 27.1 %copy-start.12 = (s32[32,4]{0,1:T(4,128)S(1)}, s32[32,4]{0,1:T(4,128)}, u32[]{:S(2)}) copy-start(s32[32,4]{0,1:T(4,128)} %param.16) | copy-start | bytes 1540
  2.6 27.3 %copy-start.11 = (bf16[2,4,576]{2,1,0:T(4,128)(2,1)S(1)}, bf16[2,4,576]{2,1,0:T(4,128)(2,1)}, u32[]{:S(2)}) copy-start(bf16[2,4,576]{2,1,0:T(4,128)(2,1)} %param.20) | copy-start | bytes 27652
  2.6 27.4 %copy-start.3 = (bf16[2,4,16,576]{3,2,1,0:T(8,128)(2,1)S(1)}, bf16[2,4,16,576]{3,2,1,0:T(8,128)(2,1)}, u32[]{:S(2)}) copy-start(bf16[2,4,16,576]{3,2,1,0:T(8,128)(2,1)} %q_ref.3) | copy-start | bytes 442372
  2.6 27.4 %copy-start.5 = (s32[4]{0:T(128)S(1)}, s32[4]{0:T(128)}, u32[]{:S(2)}) copy-start(s32[4]{0:T(128)} %ctx_ref) | copy-start | bytes 52
  2.6 24.7 %all-to-all-start = ((bf16[32,8,576]{2,1,0:T(8,128)(2,1)}), bf16[32,8,576]{2,1,0:T(8,128)(2,1)S(1)}, u32[]{:S(2)}, u32[]{:S(2)}) async-start(bf16[32,8,576]{2,1,0:T(8,128)(2,1)} %bitcast.7), calls=%async_computation | async-start | bytes 655360 | tf_op jit(solution)/shard_map/all_to_all | solution.py:588
  14.8 0.8 copy-start.4
  22.6 23.1 %collective-permute-start.2 = (bf16[2,8,224,128]{3,2,1,0:T(8,128)(2,1)}, bf16[2,8,224,128]{3,2,1,0:T(8,128)(2,1)S(1)}, u32[]{:S(2)}, u32[]{:S(2)}) collective-permute-start(bf16[2,8,224,128]{3,2,1,0:T(8,128)(2,1)} %get-tuple-element.28), channel_id=1, source_target_pairs={{0,2},{1,3},{2,4},{3,5},{4,6},{5,7},{6,0},{7,1},{8,10},{9,11},{10,... | collective-permute-start | bytes 2752520 | tf_op jit(solution)/shard_map/ppermute | solution.py:651
  23.8 21.9 %collective-permute-start.3 = (bf16[2,8,224,128]{3,2,1,0:T(8,128)(2,1)}, bf16[2,8,224,128]{3,2,1,0:T(8,128)(2,1)}, u32[]{:S(2)}, u32[]{:S(2)}) collective-permute-start(bf16[2,8,224,128]{3,2,1,0:T(8,128)(2,1)} %get-tuple-element.29), channel_id=1, source_target_pairs={{0,6},{1,7},{2,0},{3,1},{4,2},{5,3},{6,4},{7,5},{8,14},{9,15},{10,... | collective-permute-start | bytes 2752520 | tf_op jit(solution)/shard_map/ppermute | solution.py:651
  27.4 8.6 %collective-permute-start.1 = (bf16[256,576]{1,0:T(8,128)(2,1)S(1)}, bf16[256,576]{1,0:T(8,128)(2,1)S(1)}, u32[]{:S(2)}, u32[]{:S(2)}) collective-permute-start(bf16[256,576]{1,0:T(8,128)(2,1)S(1)} %bitcast.26), channel_id=1, source_target_pairs={{0,1},{1,0},{2,3},{3,2},{4,5},{5,4},{6,7},{7,6},{8,9},{9,8},{10,11... | collective-permute-start | bytes 884744 | tf_op jit(solution)/shard_map/ppermute | solution.py:594
  30.0 6.0 %copy-start = (bf16[16,512,128]{2,1,0:T(8,128)(2,1)S(1)}, bf16[16,512,128]{2,1,0:T(8,128)(2,1)}, u32[]{:S(2)}) copy-start(bf16[16,512,128]{2,1,0:T(8,128)(2,1)} %uv_ref.1) | copy-start | bytes 6291460
  36.0 9.9 %copy-start.13 = (bf16[1,8,224,128]{3,2,1,0:T(8,128)(2,1)S(1)}, bf16[1,8,224,128]{3,2,1,0:T(8,128)(2,1)}, u32[]{:S(2)}) copy-start(bf16[1,8,224,128]{3,2,1,0:T(8,128)(2,1)} %get-tuple-element.33) | copy-start | bytes 1376260
  36.0 12.4 %copy-start.7 = (bf16[16,128,224]{1,2,0:T(8,128)(2,1)S(1)}, bf16[16,128,224]{1,2,0:T(8,128)(2,1)}, u32[]{:S(2)}) copy-start(bf16[16,128,224]{1,2,0:T(8,128)(2,1)} %param.22) | copy-start | bytes 2752516
  39.1 27.1 %all-to-all-start.1 = ((bf16[32,8,1024]{2,1,0:T(8,128)(2,1)}), bf16[32,8,1024]{2,1,0:T(8,128)(2,1)S(1)}, u32[]{:S(2)}, u32[]{:S(2)}) async-start(bf16[32,8,1024]{2,1,0:T(8,128)(2,1)} %bitcast.14), calls=%async_computation.1 | async-start | bytes 1048576 | tf_op jit(solution)/shard_map/all_to_all | solution.py:588
  45.6 8.8 %copy-start.6 = (bf16[2,8,224,128]{3,2,1,0:T(8,128)(2,1)}, bf16[2,8,224,128]{3,2,1,0:T(8,128)(2,1)S(1)}, u32[]{:S(2)}) copy-start(bf16[2,8,224,128]{3,2,1,0:T(8,128)(2,1)S(1)} %collective-permute-done.2.refs_2_) | copy-start | bytes 2752516
  45.7 12.5 %collective-permute-start.4 = (bf16[1,8,224,128]{3,2,1,0:T(8,128)(2,1)}, bf16[1,8,224,128]{3,2,1,0:T(8,128)(2,1)}, u32[]{:S(2)}, u32[]{:S(2)}) collective-permute-start(bf16[1,8,224,128]{3,2,1,0:T(8,128)(2,1)} %get-tuple-element.32), channel_id=1, source_target_pairs={{0,2},{1,3},{2,4},{3,5},{4,6},{5,7},{6,0},{7,1},{8,10},{9,11},{10,... | collective-permute-start | bytes 1376264 | tf_op jit(solution)/shard_map/ppermute | solution.py:651
  45.9 12.2 %collective-permute-start.5 = (bf16[1,8,224,128]{3,2,1,0:T(8,128)(2,1)S(1)}, bf16[1,8,224,128]{3,2,1,0:T(8,128)(2,1)}, u32[]{:S(2)}, u32[]{:S(2)}) collective-permute-start(bf16[1,8,224,128]{3,2,1,0:T(8,128)(2,1)S(1)} %copy-done.13), channel_id=1, source_target_pairs={{0,6},{1,7},{2,0},{3,1},{4,2},{5,3},{6,4},{7,5},{8,14},{9,15},{10,... | collective-permute-start | bytes 1376264 | tf_op jit(solution)/shard_map/ppermute | solution.py:651
  48.5 16.5 %collective-permute-start = (bf16[8,224,128]{2,1,0:T(8,128)(2,1)S(1)}, bf16[8,224,128]{2,1,0:T(8,128)(2,1)S(1)}, u32[]{:S(2)}, u32[]{:S(2)}) collective-permute-start(bf16[8,224,128]{2,1,0:T(8,128)(2,1)S(1)} %dynamic-slice_bitcast_fusion), channel_id=1, source_target_pairs={{0,8},{8,0},{1,9},{9,1},{2,10},{10,2},{3,11},{11,3},{4,12},{12,4},... | collective-permute-start | bytes 1376264 | tf_op jit(solution)/shard_map/ppermute | solution.py:637
  50.6 21.5 %collective-permute-start.6 = (bf16[1,8,224,128]{3,2,1,0:T(8,128)(2,1)}, bf16[1,8,224,128]{3,2,1,0:T(8,128)(2,1)S(1)}, u32[]{:S(2)}, u32[]{:S(2)}) collective-permute-start(bf16[1,8,224,128]{3,2,1,0:T(8,128)(2,1)} %slice.8), channel_id=1, source_target_pairs={{0,1},{1,0},{2,3},{3,2},{4,5},{5,4},{6,7},{7,6},{8,9},{9,8},{10,11... | collective-permute-start | bytes 1376264 | tf_op jit(solution)/shard_map/ppermute | solution.py:651
  54.4 17.7 %collective-permute-start.7 = (bf16[1,8,224,128]{3,2,1,0:T(8,128)(2,1)}, bf16[1,8,224,128]{3,2,1,0:T(8,128)(2,1)}, u32[]{:S(2)}, u32[]{:S(2)}) collective-permute-start(bf16[1,8,224,128]{3,2,1,0:T(8,128)(2,1)} %slice.9), channel_id=1, source_target_pairs={{0,1},{1,0},{2,3},{3,2},{4,5},{5,4},{6,7},{7,6},{8,9},{9,8},{10,11... | collective-permute-start | bytes 1376264 | tf_op jit(solution)/shard_map/ppermute | solution.py:651
  58.1 14.0 %collective-permute-start.8 = (bf16[1,8,224,128]{3,2,1,0:T(8,128)(2,1)}, bf16[1,8,224,128]{3,2,1,0:T(8,128)(2,1)S(1)}, u32[]{:S(2)}, u32[]{:S(2)}) collective-permute-start(bf16[1,8,224,128]{3,2,1,0:T(8,128)(2,1)} %collective-permute-done.4), channel_id=1, source_target_pairs={{0,2},{1,3},{2,4},{3,5},{4,6},{5,7},{6,0},{7,1},{8,10},{9,11},{10,... | collective-permute-start | bytes 1376264 | tf_op jit(solution)/shard_map/ppermute | solution.py:651
  58.1 14.0 %collective-permute-start.9 = (bf16[1,8,224,128]{3,2,1,0:T(8,128)(2,1)}, bf16[1,8,224,128]{3,2,1,0:T(8,128)(2,1)S(1)}, u32[]{:S(2)}, u32[]{:S(2)}) collective-permute-start(bf16[1,8,224,128]{3,2,1,0:T(8,128)(2,1)} %collective-permute-done.5), channel_id=1, source_target_pairs={{0,7},{1,6},{2,1},{3,0},{4,3},{5,2},{6,5},{7,4},{8,15},{9,14},{10,... | collective-permute-start | bytes 1376264 | tf_op jit(solution)/shard_map/ppermute | solution.py:651
  64.9 6.8 %copy-start.10 = (bf16[2,128,28]{1,0,2:T(2,128)(2,1)S(1)}, bf16[2,128,28]{1,0,2:T(2,128)(2,1)}, u32[]{:S(2)}) copy-start(bf16[2,128,28]{1,0,2:T(2,128)(2,1)} %param.23) | copy-start | bytes 43012
  67.4 11.6 %all-to-all-start.2 = ((bf16[16,32,256]{2,1,0:T(8,128)(2,1)}), bf16[16,32,256]{2,1,0:T(8,128)(2,1)S(1)}, u32[]{:S(2)}, u32[]{:S(2)}) async-start(bf16[16,32,256]{2,1,0:T(8,128)(2,1)} %bitcast.16), calls=%async_computation.2 | async-start | bytes 524288 | tf_op jit(solution)/shard_map/all_to_all | solution.py:588
  72.1 18.6 %copy-start.8 = (bf16[1,8,224,128]{3,2,1,0:T(8,128)(2,1)}, bf16[1,8,224,128]{3,2,1,0:T(8,128)(2,1)S(1)}, u32[]{:S(2)}) copy-start(bf16[1,8,224,128]{3,2,1,0:T(8,128)(2,1)S(1)} %collective-permute-done.6.refs_3_) | copy-start | bytes 1376260
  72.1 21.3 %copy-start.1 = (bf16[1,8,224,128]{3,2,1,0:T(8,128)(2,1)}, bf16[1,8,224,128]{3,2,1,0:T(8,128)(2,1)S(1)}, u32[]{:S(2)}) copy-start(bf16[1,8,224,128]{3,2,1,0:T(8,128)(2,1)S(1)} %collective-permute-done.8.refs_0_.refs_4_) | copy-start | bytes 1376260
  72.1 21.3 %copy-start.2 = (bf16[1,8,224,128]{3,2,1,0:T(8,128)(2,1)}, bf16[1,8,224,128]{3,2,1,0:T(8,128)(2,1)S(1)}, u32[]{:S(2)}) copy-start(bf16[1,8,224,128]{3,2,1,0:T(8,128)(2,1)S(1)} %collective-permute-done.9.refs_1_.refs_5_) | copy-start | bytes 1376260
  79.9 22.3 %all-to-all-start.3 = ((bf16[32,56,128]{2,1,0:T(8,128)(2,1)}), bf16[32,56,128]{2,1,0:T(8,128)(2,1)}, u32[]{:S(2)}, u32[]{:S(2)}) async-start(bf16[32,56,128]{2,1,0:T(8,128)(2,1)} %get-tuple-element.36), calls=%async_computation.3 | async-start | bytes 917504 | tf_op jit(solution)/shard_map/all_to_all | solution.py:588
  87.9 2.8 %collective-permute-start.10 = (bf16[1,8,224,128]{3,2,1,0:T(8,128)(2,1)}, bf16[1,8,224,128]{3,2,1,0:T(8,128)(2,1)S(1)}, u32[]{:S(2)}, u32[]{:S(2)}) collective-permute-start(bf16[1,8,224,128]{3,2,1,0:T(8,128)(2,1)} %get-tuple-element.37), channel_id=1, source_target_pairs={{0,1},{1,0},{2,3},{3,2},{4,5},{5,4},{6,7},{7,6},{8,9},{9,8},{10,11... | collective-permute-start | bytes 1376264 | tf_op jit(solution)/shard_map/ppermute | solution.py:651
  90.7 0.8 copy-start.9
  104.0 4.5 %collective-permute-start.11 = (bf16[4,160,256]{2,1,0:T(8,128)(2,1)S(1)}, bf16[4,160,256]{2,1,0:T(8,128)(2,1)S(1)}, u32[]{:S(2)}, u32[]{:S(2)}) collective-permute-start(bf16[4,160,256]{2,1,0:T(8,128)(2,1)S(1)} %get-tuple-element.39), channel_id=1, source_target_pairs={{0,1},{1,0},{2,3},{3,2},{4,5},{5,4},{6,7},{7,6},{8,9},{9,8},{10,11... | collective-permute-start | bytes 983048 | tf_op jit(solution)/shard_map/ppermute | solution.py:594
  109.4 10.5 %all-to-all-start.4 = ((bf16[4,160,256]{2,1,0:T(8,128)(2,1)}), bf16[4,160,256]{2,1,0:T(8,128)(2,1)S(1)}, u32[]{:S(2)}, u32[]{:S(2)}) async-start(bf16[4,160,256]{2,1,0:T(8,128)(2,1)} %add_cores.1), calls=%async_computation.4 | async-start | bytes 655360 | tf_op jit(solution)/shard_map/all_to_all | solution.py:588
  127.4 3.4 %collective-permute-start.12 = (bf16[4,80,256]{2,1,0:T(8,128)(2,1)S(1)}, bf16[4,80,256]{2,1,0:T(8,128)(2,1)S(1)}, u32[]{:S(2)}, u32[]{:S(2)}) collective-permute-start(bf16[4,80,256]{2,1,0:T(8,128)(2,1)S(1)} %all_to_all.35.same_ref), channel_id=1, source_target_pairs={{0,1},{1,0},{2,3},{3,2},{4,5},{5,4},{6,7},{7,6},{8,9},{9,8},{10,11... | collective-permute-start | bytes 491528 | tf_op jit(solution)/shard_map/ppermute | solution.py:594

commit v5 on v4

--- a/solution.py
+++ b/solution.py
@@ -195,7 +195,7 @@
         ],
         name="reshard",
         mib=24,
-    )(rank, gain.reshape(1, -1), in_hbm(w_gate.T), in_hbm(w_up.T), in_hbm(w_down))
+    )(rank, in_hbm(gain.reshape(1, -1)), in_hbm(w_gate.T), in_hbm(w_up.T), in_hbm(w_down))
 
 
 def turn_kernel(first, *refs):
@@ -343,59 +343,59 @@
     )(rank, my_lengths, queries, new_rows, other_rows, in_hbm(acc), in_hbm(side), w_uv)
 
 
-def gather_heads_kernel(rank_ref, *refs):
-    out_ref = refs[-1]
-    ring = len(refs) - 1
-    for k, w_ref in enumerate(refs[:-1]):
-        heads, _, values = w_ref.shape
-        target = (rank_ref[0] + ring - k) % ring
-        for h in range(heads):
-            out_ref[target, :, h * values : (h + 1) * values] = w_ref[h]
-
-
-def gather_heads(rank, own, pieces):
-    heads, features, values = pieces[0].shape
-    ring = 1 + len(pieces)
-    block = (heads, features, values)
-    return call(
-        gather_heads_kernel,
-        jax.ShapeDtypeStruct((ring, features, heads * values), bf16),
-        (0, 4 * ring * heads * features * values),
+def own_heads_kernel(rank_ref, w_ref, out_ref):
+    heads, _, values = w_ref.shape
+    for h in range(heads):
+        out_ref[:, h * values : (h + 1) * values] = w_ref[h]
+
+
+def own_heads(rank, own, ring):
+    total, features, values = own.shape
+    heads = total // ring
+    return call(
+        own_heads_kernel,
+        jax.ShapeDtypeStruct((features, heads * values), bf16),
+        (0, 4 * heads * features * values),
         grid_spec=pltpu.PrefetchScalarGridSpec(
             num_scalar_prefetch=1,
             grid=(1,),
-            in_specs=[pl.BlockSpec(block, lambda c, rank: (rank[0], 0, 0))]
-            + [pl.BlockSpec(block, lambda c, rank: (0, 0, 0))] * len(pieces),
+            in_specs=[pl.BlockSpec((heads, features, values), lambda c, rank: (rank[0], 0, 0))],
             out_specs=pl.BlockSpec(memory_space=pltpu.VMEM),
         ),
-        name="gather_heads",
-    )(rank, in_hbm(own), *pieces)
-
-
-def project_kernel(w_ref, x_ref, out_ref):
+        name="own_heads",
+    )(rank, in_hbm(own))
+
+
+def project_kernel(rank_ref, x_ref, own_ref, *refs):
+    *w_refs, out_ref = refs
     ring, tp = out_ref.shape[:2]
     x = x_ref[...].T
-    for n in range(ring):
-        width = w_ref.shape[1] // tp
-        value = dot(w_ref[n], x)
+    for k in range(ring):
+        if k == 0:
+            weights = own_ref[...]
+        else:
+            w_ref = w_refs[k - 1]
+            weights = jnp.concatenate([w_ref[h] for h in range(w_ref.shape[0])], axis=1)
+        width = weights.shape[0] // tp
+        target = (rank_ref[0] + ring - k) % ring
+        value = dot(weights, x)
         spare = jnp.zeros((PAD - width, value.shape[1]), f32)
         for j in range(tp):
             part = jnp.concatenate([value[j * width : (j + 1) * width], spare], axis=0)
-            out_ref[n, j] = part.astype(bf16)
-
-
-def project(weights, every, tp):
-    ring, features, depth = weights.shape
-    columns = every.shape[0]
+            out_ref[target, j] = part.astype(bf16)
+
+
+def project(rank, own, pieces, every, tp):
+    ring, columns = 1 + len(pieces), every.shape[0]
     whole = pl.BlockSpec(memory_space=pltpu.VMEM)
     return call(
         project_kernel,
         jax.ShapeDtypeStruct((ring, tp, PAD, columns), bf16),
-        (2 * weights.size * columns, 2 * (weights.size + every.size)),
-        in_specs=[whole, whole],
+        (2 * ring * own.size * columns, 2 * (ring * own.size + every.size)),
+        in_specs=[pl.BlockSpec(memory_space=pltpu.SMEM)] + [whole] * (1 + ring),
         out_specs=whole,
         name="project",
-    )(weights, every)
+    )(rank, every, own, *pieces)
 
 
 def split_sum(value):
@@ -656,13 +656,13 @@
         far, _ = lax.optimization_barrier((arrays[4:6], (plus, minus)))
         far = [along_x(far[0], 2, 1), along_x(far[1], 2, -1)]
         every, _ = lax.optimization_barrier((every, (plus, minus, far)))
-    parts = project(gather_heads(y_rank, w_turned, out_pieces), every, tp)
+    parts = project(y_rank, own_heads(y_rank, w_turned, ring), out_pieces, every, tp)
     parts = exchange(parts.reshape((ring * tp,) + parts.shape[2:]), ("y", "tp"))
     if tp > 2:
         pieces[2], pieces[6] = (plus, 0), (minus, 0)
         swapped = [along_x(plus[1:], 1, 1), along_x(minus[1:], 1, 1)]
         far = [along_x(far[0], 2, 1), along_x(far[1], 3, -1)]
-        parts, _ = lax.optimization_barrier((parts, (swapped, far)))
+        parts, _ = lax.optimization_barrier((parts, far))
         pieces[3], pieces[7] = (swapped[0], 0), (swapped[1], 0)
         pieces[4], pieces[5] = (far[0], 0), (far[1], 0)
     pieces[1] = along_x(arrays[1], 1, 1), 0

time: 153 us -> 152 us (level)
  local copies, waits for them, and re-layouts: 4.5 us -> 2.95 us
    ppermute x9, waiting for transfers between devices: 5.39 us -> 9.97 us  [along_x(): lax.ppermute(piece, 'tp', [(j, partner(j, tp, k, sign)) for j in range(tp)])]
    all_to_all x5, waiting for transfers between devices: 22.1 us -> 20.2 us  [exchange(): lax.all_to_all(x, axis, split_axis=0, concat_axis=0, tiled=True, axis_ind...]
    slice x2, local copies, waits for them, and re-layouts: 2.65 us -> 1.08 us  [shards(): swapped = [along_x(plus[1:], 1, 1), along_x(minus[1:], 1, 1)]]
  transfers between devices with their start and end apart: 18 -> 18, of which waited for: 9 -> 11; matrix products, arithmetic and copies ran while one was open for 2% -> 1% of each run, Pallas kernels for 15% -> 15%
where the time goes in v5:
time: 152 us; the launch traced here: 151 us
  starting transfers between devices  56.1 us (37%)
  waiting for transfers between devices  33 us (22%)
  Pallas kernels  31.5 us (21%)
  blocking collectives  26.8 us (18%)
  local copies, waits for them, and re-layouts  2.95 us (2%)
    all_to_all x5, starting transfers between devices, exchange(): lax.all_to_all(x, axis, split_axis=0, concat_axis=0, tiled=True, axis_ind...  34.4 us
    all_to_all x2, blocking collectives, exchange(): lax.all_to_all(x, axis, split_axis=0, concat_axis=0, tiled=True, axis_ind...  26.8 us
    all_to_all x5, waiting for transfers between devices, exchange(): lax.all_to_all(x, axis, split_axis=0, concat_axis=0, tiled=True, axis_ind...  20.2 us
    ppermute x9, starting transfers between devices, along_x(): lax.ppermute(piece, 'tp', [(j, partner(j, tp, k, sign)) for j in range(tp)])  12.5 us
    ppermute x9, waiting for transfers between devices, along_x(): lax.ppermute(piece, 'tp', [(j, partner(j, tp, k, sign)) for j in range(tp)])  9.97 us
    ppermute x3, starting transfers between devices, swap_cores(): lax.ppermute(x, 'tp', [(j, j ^ 1) for j in range(lax.axis_size('tp'))])  8.02 us
    pallas_call x1, Pallas kernels, reshard(): call(functools.partial(reshard_kernel, tp, width), tuple((pltpu.HBM((size...  7.09 us
    pallas_call x1, Pallas kernels, attend_cache(): call(cache_kernel, (pltpu.HBM((per_owner, rows, LAT), f32), pltpu.HBM((pe...  6 us
  transfers between devices with their start and end apart: 18, of which 11 were waited for; matrix products, arithmetic and copies ran while one was open for 1% of the time, Pallas kernels for 15%

profile of v5, /device:TPU:1, one launch (start us, length us, event | category | flops | bytes accessed | tf_op | source)
XLA Modules:
  0.0 150.7 jit_solution(15923050192732808010)
XLA Ops:
  0.0 2.6 %route.1 = bf16[256,576]{1,0:T(8,128)(2,1)} custom-call(s32[1]{0:T(128)} %bitcast.rank_ref, s32[1,128]{1,0:T(1,128)} %bitcast.39, s32[4,32]{1,0:T(4,128)} %bitcast.38, bf16[576,512]{1,0:T(8,128)(2,1)} %bitcast.33), custom_call_target="tpu_custom_call" | custom-call | flops 150994944 | bytes 884736 | tf_op jit(solution)/shard_map/route/pallas_call | solution.py:107
  2.6 12.2 %all-to-all-start = ((bf16[32,8,576]{2,1,0:T(8,128)(2,1)}), bf16[32,8,576]{2,1,0:T(8,128)(2,1)S(1)}, u32[]{:S(2)}, u32[]{:S(2)}) async-start(bf16[32,8,576]{2,1,0:T(8,128)(2,1)} %bitcast.5), calls=%async_computation | async-start | bytes 655360 | tf_op jit(solution)/shard_map/all_to_all | solution.py:588
  14.8 7.1 %reshard.1 = (bf16[1,8,224,128]{3,2,1,0:T(8,128)(2,1)}, bf16[1,8,224,128]{3,2,1,0:T(8,128)(2,1)}, bf16[2,8,224,128]{3,2,1,0:T(8,128)(2,1)}, bf16[2,8,224,128]{3,...) custom-call(s32[1]{0:T(128)} %bitcast.rank_ref, f32[1,7168]{1,0:T(1,128)} %bitcast.36, ...), custom_call_target="tpu_custom_call" | custom-call | flops 792723456 | bytes 7225344 | tf_op jit(solution)/shard_map/reshard/pallas_call | solution.py:176
  21.9 1.3 collective-permute-start.1
  23.2 1.5 collective-permute-start.2
  24.6 2.8 %all-to-all-done = bf16[32,8,576]{2,1,0:T(8,128)(2,1)S(1)} async-done(((bf16[32,8,576]{2,1,0:T(8,128)(2,1)}), bf16[32,8,576]{2,1,0:T(8,128)(2,1)S(1)}, u32[]{:S(2)}, u32[]{:S(2)}) %all-to-all-start) | async-done | bytes 294944 | tf_op jit(solution)/shard_map/all_to_all | solution.py:588
  27.4 2.4 %collective-permute-start = (bf16[256,576]{1,0:T(8,128)(2,1)S(1)}, bf16[256,576]{1,0:T(8,128)(2,1)S(1)}, u32[]{:S(2)}, u32[]{:S(2)}) collective-permute-start(bf16[256,576]{1,0:T(8,128)(2,1)S(1)} %bitcast.26), channel_id=1, source_target_pairs={{0,1},{1,0},{2,3},{3,2},{4,5},{5,4},{6,7},{7,6},{8,9},{9,8},{10,11... | collective-permute-start | bytes 884744 | tf_op jit(solution)/shard_map/ppermute | solution.py:594
  29.8 0.2 dynamic-slice_reduce_fusion.len_ref
  30.0 0.0 copy-done.3
  30.0 0.0 copy-done.4
  30.0 0.0 copy-start
  30.0 6.0 %attend_cache.1 = (f32[4,32,512]{2,1,0:T(8,128)}, f32[4,32,128]{2,1,0:T(8,128)}) custom-call(s32[4]{0:T(128)S(1)} %copy-done.4, bf16[2,4,16,576]{3,2,1,0:T(8,128)(2,1)S(1)} %copy-done.3, bf16[4,576,1024]{2,1,0:T(8,128)(2,1)} %bitcast.29, bf16[4,16,576]{2,1,0:T(8,128)(2,1)S(1)} %pad.4.tok_ref), custom_call_target="tpu_custom_call" | custom-call | flops 285212672 | bytes 4718592 | tf_op jit(solution)/shard_map/attend_cache/pallas_call | solution.py:261
  36.0 0.0 collective-permute-done.other_ref
  36.0 0.0 copy-start.6
  36.0 3.0 %attend_new.1 = bf16[16,2,8,1024]{3,2,1,0:T(8,128)(2,1)} custom-call(s32[1]{0:T(128)} %bitcast.rank_ref, s32[4]{0:T(128)S(1)} %dynamic-slice_reduce_fusion.len_ref, bf16[2,4,16,576]{3,2,1,0:T(8,128)(2,1)S(1)} %copy-done.3, bf16[256,576]{1,0:T(8,128)(2,1)S(1)} %bitcast.27, bf16[256,576]{1,0:T(8,128)(2,1)S(1)} %collective-permute-done.other_ref, ...), custom_call_target="tpu_custom_call" | custom-call | flops 150994944 | bytes 2097152 | tf_op jit(solution)/shard_map/attend_new/pallas_call | solution.py:324
  39.1 5.9 %all-to-all-start.1 = ((bf16[32,8,1024]{2,1,0:T(8,128)(2,1)}), bf16[32,8,1024]{2,1,0:T(8,128)(2,1)S(1)}, u32[]{:S(2)}, u32[]{:S(2)}) async-start(bf16[32,8,1024]{2,1,0:T(8,128)(2,1)} %bitcast.12), calls=%async_computation.1 | async-start | bytes 1048576 | tf_op jit(solution)/shard_map/all_to_all | solution.py:588
  45.0 0.0 collective-permute-done.1.refs_2_
  45.0 0.0 collective-permute-done.2.refs_4_.refs_6_
  45.0 0.3 collective-permute-start.3
  45.3 2.5 %collective-permute-start.4 = (bf16[1,8,224,128]{3,2,1,0:T(8,128)(2,1)}, bf16[1,8,224,128]{3,2,1,0:T(8,128)(2,1)}, u32[]{:S(2)}, u32[]{:S(2)}) collective-permute-start(bf16[1,8,224,128]{3,2,1,0:T(8,128)(2,1)} %get-tuple-element.33), channel_id=1, source_target_pairs={{0,6},{1,7},{2,0},{3,1},{4,2},{5,3},{6,4},{7,5},{8,14},{9,15},{10,... | collective-permute-start | bytes 1376264 | tf_op jit(solution)/shard_map/ppermute | solution.py:651
  47.7 0.8 dynamic-slice_bitcast_fusion
  48.5 1.2 collective-permute-start.5
  49.8 7.7 %collective-permute-done.3 = bf16[1,8,224,128]{3,2,1,0:T(8,128)(2,1)} collective-permute-done((bf16[1,8,224,128]{3,2,1,0:T(8,128)(2,1)}, bf16[1,8,224,128]{3,2,1,0:T(8,128)(2,1)}, u32[]{:S(2)}, u32[]{:S(2)}) %collective-permute-start.3) | collective-permute-done | bytes 458784 | tf_op jit(solution)/shard_map/ppermute | solution.py:651
  57.4 0.0 collective-permute-start.6
  57.4 0.0 collective-permute-done.4
  57.4 4.9 %collective-permute-start.7 = (bf16[1,8,224,128]{3,2,1,0:T(8,128)(2,1)}, bf16[1,8,224,128]{3,2,1,0:T(8,128)(2,1)S(1)}, u32[]{:S(2)}, u32[]{:S(2)}) collective-permute-start(bf16[1,8,224,128]{3,2,1,0:T(8,128)(2,1)} %collective-permute-done.4), channel_id=1, source_target_pairs={{0,7},{1,6},{2,1},{3,0},{4,3},{5,2},{6,5},{7,4},{8,15},{9,14},{10,... | collective-permute-start | bytes 1376264 | tf_op jit(solution)/shard_map/ppermute | solution.py:651
  62.4 1.1 own_heads.1.own_ref
  63.5 0.0 all-to-all-done.1
  63.5 0.6 collective-permute-done.5.refs_0_
  64.1 1.2 project.1
  65.3 4.8 %all-to-all-start.2 = ((bf16[16,32,256]{2,1,0:T(8,128)(2,1)}), bf16[16,32,256]{2,1,0:T(8,128)(2,1)S(1)}, u32[]{:S(2)}, u32[]{:S(2)}) async-start(bf16[16,32,256]{2,1,0:T(8,128)(2,1)} %bitcast.16), calls=%async_computation.2 | async-start | bytes 524288 | tf_op jit(solution)/shard_map/all_to_all | solution.py:588
  70.2 0.3 turn_hidden.1.hidden_ref
  70.4 0.0 collective-permute-done.6.refs_0_.refs_4_
  70.4 0.0 copy-start.1
  70.5 0.9 collective-permute-done.7.refs_1_.refs_5_
  71.3 6.0 %all-to-all-done.2.part_ref = bf16[16,32,256]{2,1,0:T(8,128)(2,1)S(1)} async-done(((bf16[16,32,256]{2,1,0:T(8,128)(2,1)}), bf16[16,32,256]{2,1,0:T(8,128)(2,1)S(1)}, u32[]{:S(2)}, u32[]{:S(2)}) %all-to-all-start.2) | async-done | bytes 262176 | tf_op jit(solution)/shard_map/all_to_all | solution.py:588
  77.4 0.8 make_mixed.1
  78.2 8.1 %all-to-all-start.3 = ((bf16[32,56,128]{2,1,0:T(8,128)(2,1)}), bf16[32,56,128]{2,1,0:T(8,128)(2,1)}, u32[]{:S(2)}, u32[]{:S(2)}) async-start(bf16[32,56,128]{2,1,0:T(8,128)(2,1)} %get-tuple-element.36), calls=%async_computation.3 | async-start | bytes 917504 | tf_op jit(solution)/shard_map/all_to_all | solution.py:588
  86.3 1.2 collective-permute-start.8
  87.5 0.3 collective-permute-start.9
  87.8 1.0 slice.9
  88.9 0.6 collective-permute-start.10
  89.5 0.0 collective-permute-done.8.refs_1_
  89.5 0.2 collective-permute-done.9.refs_3_
  89.6 1.3 collective-permute-done.10.refs_5_.refs_7_
  90.9 0.0 copy-done.7
  90.9 0.8 copy-done.9
  91.7 1.9 %collect.2.refs_0_ = bf16[6,144,1024]{2,1,0:T(8,128)(2,1)S(1)} custom-call(bf16[1,8,224,128]{3,2,1,0:T(8,128)(2,1)} %get-tuple-element.24.refs_0_, bf16[1,8,224,128]{3,2,1,0:T(8,128)(2,1)} %copy-done.7, bf16[2,8,224,128]{3,2,1,0:T(8,128)(2,1)} %copy-done.5, bf16[1,8,224,128]{3,2,1,0:T(8,128)(2,1)} %copy-done.8, ...), custom_call_target="tpu_custom_call" | custom-call | bytes 3538944 | tf_op jit(solution)/shard_map/collect/pallas_call | solution.py:467
  93.6 0.2 collect.3.refs_1_
  93.8 6.9 %all-to-all-done.3.x_ref = bf16[32,56,128]{2,1,0:T(8,128)(2,1)} async-done(((bf16[32,56,128]{2,1,0:T(8,128)(2,1)}), bf16[32,56,128]{2,1,0:T(8,128)(2,1)}, u32[]{:S(2)}, u32[]{:S(2)}) %all-to-all-start.3) | async-done | bytes 458784 | tf_op jit(solution)/shard_map/all_to_all | solution.py:588
  100.7 1.8 %gate_up.1 = (bf16[4,160,256]{2,1,0:T(8,128)(2,1)S(1)}, bf16[4,160,256]{2,1,0:T(8,128)(2,1)S(1)}) custom-call(s32[1]{0:T(128)} %bitcast.rank_ref, bf16[32,56,128]{2,1,0:T(8,128)(2,1)} %all-to-all-done.3.x_ref, bf16[6,144,1024]{2,1,0:T(8,128)(2,1)S(1)} %collect.2.refs_0_, bf16[2,144,1024]{2,1,0:T(8,128)(2,1)S(1)} %collect.3.refs_1_), custom_call_target="tpu_custom_call" | custom-call | flops 603979776 | bytes 2818048 | tf_op jit(solution)/shard_map/gate_up/pallas_call | solution.py:487
  102.5 3.3 %collective-permute-start.11 = (bf16[4,160,256]{2,1,0:T(8,128)(2,1)S(1)}, bf16[4,160,256]{2,1,0:T(8,128)(2,1)S(1)}, u32[]{:S(2)}, u32[]{:S(2)}) collective-permute-start(bf16[4,160,256]{2,1,0:T(8,128)(2,1)S(1)} %get-tuple-element.39), channel_id=1, source_target_pairs={{0,1},{1,0},{2,3},{3,2},{4,5},{5,4},{6,7},{7,6},{8,9},{9,8},{10,11... | collective-permute-start | bytes 983048 | tf_op jit(solution)/shard_map/ppermute | solution.py:594
  105.8 1.3 collective-permute-done.11.b_ref
  107.0 0.8 add_cores.1
  107.8 3.5 %all-to-all-start.4 = ((bf16[4,160,256]{2,1,0:T(8,128)(2,1)}), bf16[4,160,256]{2,1,0:T(8,128)(2,1)S(1)}, u32[]{:S(2)}, u32[]{:S(2)}) async-start(bf16[4,160,256]{2,1,0:T(8,128)(2,1)} %add_cores.1), calls=%async_computation.4 | async-start | bytes 655360 | tf_op jit(solution)/shard_map/all_to_all | solution.py:588
  111.3 2.5 %turn.1.w_ref = bf16[1024,640]{1,0:T(8,128)(2,1)S(1)} custom-call(bf16[1,8,224,128]{3,2,1,0:T(8,128)(2,1)} %get-tuple-element.24.refs_0_, bf16[1,8,224,128]{3,2,1,0:T(8,128)(2,1)} %copy-done.7, bf16[2,8,224,128]{3,2,1,0:T(8,128)(2,1)} %copy-done.5, bf16[1,8,224,128]{3,2,1,0:T(8,128)(2,1)} %copy-done.8, bf16[1,8,224,128]{3,2,1,0:T(8,128)(2,1)} %copy-done.1, ...), custom_call_target="tpu_custom_call" | custom-call | flops 167772160 | bytes 2621440 | tf_op jit(solution)/shard_map/turn/pallas_call | solution.py:213
  113.9 4.5 %all-to-all-done.4.part_ref = bf16[4,160,256]{2,1,0:T(8,128)(2,1)S(1)} async-done(((bf16[4,160,256]{2,1,0:T(8,128)(2,1)}), bf16[4,160,256]{2,1,0:T(8,128)(2,1)S(1)}, u32[]{:S(2)}, u32[]{:S(2)}) %all-to-all-start.4) | async-done | bytes 327712 | tf_op jit(solution)/shard_map/all_to_all | solution.py:588
  118.4 0.1 activate.1
  118.5 7.4 %all_to_all.35.same_ref = bf16[4,80,256]{2,1,0:T(8,128)(2,1)S(1)} all-to-all(bf16[4,80,256]{2,1,0:T(8,128)(2,1)S(1)} %activate.1), channel_id=1, replica_groups={{0,2,4,6},{1,3,5,7},{8,10,12,14},{9,11,13,15},{16,18,20,22},{17,19,21,2..., dimensions={0} | all-to-all | bytes 327680 | tf_op jit(solution)/shard_map/all_to_all | solution.py:588
  125.8 2.4 %collective-permute-start.12 = (bf16[4,80,256]{2,1,0:T(8,128)(2,1)S(1)}, bf16[4,80,256]{2,1,0:T(8,128)(2,1)S(1)}, u32[]{:S(2)}, u32[]{:S(2)}) collective-permute-start(bf16[4,80,256]{2,1,0:T(8,128)(2,1)S(1)} %all_to_all.35.same_ref), channel_id=1, source_target_pairs={{0,1},{1,0},{2,3},{3,2},{4,5},{5,4},{6,7},{7,6},{8,9},{9,8},{10,11... | collective-permute-start | bytes 491528 | tf_op jit(solution)/shard_map/ppermute | solution.py:594
  128.2 1.0 collective-permute-done.12.other_ref
  129.2 1.2 down.1
  130.4 19.4 %all_to_all.36.part_ref = bf16[32,56,128]{2,1,0:T(8,128)(2,1)S(1)} all-to-all(bf16[32,56,128]{2,1,0:T(8,128)(2,1)S(1)} %down.1), channel_id=1, replica_groups=mesh['z'=16,'y'=2,'tp'=8] {'z','y'}, dimensions={0} | all-to-all | bytes 917504 | tf_op jit(solution)/shard_map/all_to_all | solution.py:588
  149.8 0.9 finish.1
  (24 shorter events, 0.1 us)
Async XLA Ops:
  2.6 27.1 %copy-start.12 = (s32[32,4]{0,1:T(4,128)S(1)}, s32[32,4]{0,1:T(4,128)}, u32[]{:S(2)}) copy-start(s32[32,4]{0,1:T(4,128)} %param.16) | copy-start | bytes 1540
  2.6 27.3 %copy-start.11 = (bf16[2,4,576]{2,1,0:T(4,128)(2,1)S(1)}, bf16[2,4,576]{2,1,0:T(4,128)(2,1)}, u32[]{:S(2)}) copy-start(bf16[2,4,576]{2,1,0:T(4,128)(2,1)} %param.20) | copy-start | bytes 27652
  2.6 27.4 %copy-start.3 = (bf16[2,4,16,576]{3,2,1,0:T(8,128)(2,1)S(1)}, bf16[2,4,16,576]{3,2,1,0:T(8,128)(2,1)}, u32[]{:S(2)}) copy-start(bf16[2,4,16,576]{3,2,1,0:T(8,128)(2,1)} %q_ref.3) | copy-start | bytes 442372
  2.6 27.4 %copy-start.4 = (s32[4]{0:T(128)S(1)}, s32[4]{0:T(128)}, u32[]{:S(2)}) copy-start(s32[4]{0:T(128)} %ctx_ref) | copy-start | bytes 52
  2.6 24.7 %all-to-all-start = ((bf16[32,8,576]{2,1,0:T(8,128)(2,1)}), bf16[32,8,576]{2,1,0:T(8,128)(2,1)S(1)}, u32[]{:S(2)}, u32[]{:S(2)}) async-start(bf16[32,8,576]{2,1,0:T(8,128)(2,1)} %bitcast.5), calls=%async_computation | async-start | bytes 655360 | tf_op jit(solution)/shard_map/all_to_all | solution.py:588
  21.9 23.1 %collective-permute-start.1 = (bf16[2,8,224,128]{3,2,1,0:T(8,128)(2,1)}, bf16[2,8,224,128]{3,2,1,0:T(8,128)(2,1)S(1)}, u32[]{:S(2)}, u32[]{:S(2)}) collective-permute-start(bf16[2,8,224,128]{3,2,1,0:T(8,128)(2,1)} %get-tuple-element.28), channel_id=1, source_target_pairs={{0,2},{1,3},{2,4},{3,5},{4,6},{5,7},{6,0},{7,1},{8,10},{9,11},{10,... | collective-permute-start | bytes 2752520 | tf_op jit(solution)/shard_map/ppermute | solution.py:651
  23.2 21.8 %collective-permute-start.2 = (bf16[2,8,224,128]{3,2,1,0:T(8,128)(2,1)}, bf16[2,8,224,128]{3,2,1,0:T(8,128)(2,1)}, u32[]{:S(2)}, u32[]{:S(2)}) collective-permute-start(bf16[2,8,224,128]{3,2,1,0:T(8,128)(2,1)} %get-tuple-element.29), channel_id=1, source_target_pairs={{0,6},{1,7},{2,0},{3,1},{4,2},{5,3},{6,4},{7,5},{8,14},{9,15},{10,... | collective-permute-start | bytes 2752520 | tf_op jit(solution)/shard_map/ppermute | solution.py:651
  27.4 8.6 %collective-permute-start = (bf16[256,576]{1,0:T(8,128)(2,1)S(1)}, bf16[256,576]{1,0:T(8,128)(2,1)S(1)}, u32[]{:S(2)}, u32[]{:S(2)}) collective-permute-start(bf16[256,576]{1,0:T(8,128)(2,1)S(1)} %bitcast.26), channel_id=1, source_target_pairs={{0,1},{1,0},{2,3},{3,2},{4,5},{5,4},{6,7},{7,6},{8,9},{9,8},{10,11... | collective-permute-start | bytes 884744 | tf_op jit(solution)/shard_map/ppermute | solution.py:594
  30.0 6.0 %copy-start = (bf16[16,512,128]{2,1,0:T(8,128)(2,1)S(1)}, bf16[16,512,128]{2,1,0:T(8,128)(2,1)}, u32[]{:S(2)}) copy-start(bf16[16,512,128]{2,1,0:T(8,128)(2,1)} %uv_ref.1) | copy-start | bytes 6291460
  36.0 11.7 %copy-start.6 = (bf16[16,128,224]{1,2,0:T(8,128)(2,1)S(1)}, bf16[16,128,224]{1,2,0:T(8,128)(2,1)}, u32[]{:S(2)}) copy-start(bf16[16,128,224]{1,2,0:T(8,128)(2,1)} %param.22) | copy-start | bytes 2752516
  39.1 24.4 %all-to-all-start.1 = ((bf16[32,8,1024]{2,1,0:T(8,128)(2,1)}), bf16[32,8,1024]{2,1,0:T(8,128)(2,1)S(1)}, u32[]{:S(2)}, u32[]{:S(2)}) async-start(bf16[32,8,1024]{2,1,0:T(8,128)(2,1)} %bitcast.12), calls=%async_computation.1 | async-start | bytes 1048576 | tf_op jit(solution)/shard_map/all_to_all | solution.py:588
  45.0 42.5 %copy-start.5 = (bf16[2,8,224,128]{3,2,1,0:T(8,128)(2,1)}, bf16[2,8,224,128]{3,2,1,0:T(8,128)(2,1)S(1)}, u32[]{:S(2)}) copy-start(bf16[2,8,224,128]{3,2,1,0:T(8,128)(2,1)S(1)} %collective-permute-done.1.refs_2_) | copy-start | bytes 2752516
  45.0 12.4 %collective-permute-start.3 = (bf16[1,8,224,128]{3,2,1,0:T(8,128)(2,1)}, bf16[1,8,224,128]{3,2,1,0:T(8,128)(2,1)}, u32[]{:S(2)}, u32[]{:S(2)}) collective-permute-start(bf16[1,8,224,128]{3,2,1,0:T(8,128)(2,1)} %get-tuple-element.32), channel_id=1, source_target_pairs={{0,2},{1,3},{2,4},{3,5},{4,6},{5,7},{6,0},{7,1},{8,10},{9,11},{10,... | collective-permute-start | bytes 1376264 | tf_op jit(solution)/shard_map/ppermute | solution.py:651
  45.3 12.1 %collective-permute-start.4 = (bf16[1,8,224,128]{3,2,1,0:T(8,128)(2,1)}, bf16[1,8,224,128]{3,2,1,0:T(8,128)(2,1)}, u32[]{:S(2)}, u32[]{:S(2)}) collective-permute-start(bf16[1,8,224,128]{3,2,1,0:T(8,128)(2,1)} %get-tuple-element.33), channel_id=1, source_target_pairs={{0,6},{1,7},{2,0},{3,1},{4,2},{5,3},{6,4},{7,5},{8,14},{9,15},{10,... | collective-permute-start | bytes 1376264 | tf_op jit(solution)/shard_map/ppermute | solution.py:651
  47.7 22.4 %copy-start.10 = (bf16[2,128,28]{1,0,2:T(2,128)(2,1)S(1)}, bf16[2,128,28]{1,0,2:T(2,128)(2,1)}, u32[]{:S(2)}) copy-start(bf16[2,128,28]{1,0,2:T(2,128)(2,1)} %param.23) | copy-start | bytes 43012
  48.5 15.6 %collective-permute-start.5 = (bf16[8,224,128]{2,1,0:T(8,128)(2,1)}, bf16[8,224,128]{2,1,0:T(8,128)(2,1)S(1)}, u32[]{:S(2)}, u32[]{:S(2)}) collective-permute-start(bf16[8,224,128]{2,1,0:T(8,128)(2,1)} %dynamic-slice_bitcast_fusion), channel_id=1, source_target_pairs={{0,8},{8,0},{1,9},{9,1},{2,10},{10,2},{3,11},{11,3},{4,12},{12,4},... | collective-permute-start | bytes 1376264 | tf_op jit(solution)/shard_map/ppermute | solution.py:637
  57.4 13.0 %collective-permute-start.6 = (bf16[1,8,224,128]{3,2,1,0:T(8,128)(2,1)}, bf16[1,8,224,128]{3,2,1,0:T(8,128)(2,1)S(1)}, u32[]{:S(2)}, u32[]{:S(2)}) collective-permute-start(bf16[1,8,224,128]{3,2,1,0:T(8,128)(2,1)} %collective-permute-done.3), channel_id=1, source_target_pairs={{0,2},{1,3},{2,4},{3,5},{4,6},{5,7},{6,0},{7,1},{8,10},{9,11},{10,... | collective-permute-start | bytes 1376264 | tf_op jit(solution)/shard_map/ppermute | solution.py:651
  57.4 13.9 %collective-permute-start.7 = (bf16[1,8,224,128]{3,2,1,0:T(8,128)(2,1)}, bf16[1,8,224,128]{3,2,1,0:T(8,128)(2,1)S(1)}, u32[]{:S(2)}, u32[]{:S(2)}) collective-permute-start(bf16[1,8,224,128]{3,2,1,0:T(8,128)(2,1)} %collective-permute-done.4), channel_id=1, source_target_pairs={{0,7},{1,6},{2,1},{3,0},{4,3},{5,2},{6,5},{7,4},{8,15},{9,14},{10,... | collective-permute-start | bytes 1376264 | tf_op jit(solution)/shard_map/ppermute | solution.py:651
  65.3 12.1 %all-to-all-start.2 = ((bf16[16,32,256]{2,1,0:T(8,128)(2,1)}), bf16[16,32,256]{2,1,0:T(8,128)(2,1)S(1)}, u32[]{:S(2)}, u32[]{:S(2)}) async-start(bf16[16,32,256]{2,1,0:T(8,128)(2,1)} %bitcast.16), calls=%async_computation.2 | async-start | bytes 524288 | tf_op jit(solution)/shard_map/all_to_all | solution.py:588
  70.4 23.1 %copy-start.1 = (bf16[1,8,224,128]{3,2,1,0:T(8,128)(2,1)}, bf16[1,8,224,128]{3,2,1,0:T(8,128)(2,1)S(1)}, u32[]{:S(2)}) copy-start(bf16[1,8,224,128]{3,2,1,0:T(8,128)(2,1)S(1)} %collective-permute-done.6.refs_0_.refs_4_) | copy-start | bytes 1376260
  71.3 22.3 %copy-start.2 = (bf16[1,8,224,128]{3,2,1,0:T(8,128)(2,1)}, bf16[1,8,224,128]{3,2,1,0:T(8,128)(2,1)S(1)}, u32[]{:S(2)}) copy-start(bf16[1,8,224,128]{3,2,1,0:T(8,128)(2,1)S(1)} %collective-permute-done.7.refs_1_.refs_5_) | copy-start | bytes 1376260
  78.2 22.4 %all-to-all-start.3 = ((bf16[32,56,128]{2,1,0:T(8,128)(2,1)}), bf16[32,56,128]{2,1,0:T(8,128)(2,1)}, u32[]{:S(2)}, u32[]{:S(2)}) async-start(bf16[32,56,128]{2,1,0:T(8,128)(2,1)} %get-tuple-element.36), calls=%async_computation.3 | async-start | bytes 917504 | tf_op jit(solution)/shard_map/all_to_all | solution.py:588
  86.3 3.1 %collective-permute-start.8 = (bf16[1,8,224,128]{3,2,1,0:T(8,128)(2,1)}, bf16[1,8,224,128]{3,2,1,0:T(8,128)(2,1)S(1)}, u32[]{:S(2)}, u32[]{:S(2)}) collective-permute-start(bf16[1,8,224,128]{3,2,1,0:T(8,128)(2,1)} %get-tuple-element.37), channel_id=1, source_target_pairs={{0,1},{1,0},{2,3},{3,2},{4,5},{5,4},{6,7},{7,6},{8,9},{9,8},{10,11... | collective-permute-start | bytes 1376264 | tf_op jit(solution)/shard_map/ppermute | solution.py:651
  87.5 2.1 %collective-permute-start.9 = (bf16[1,8,224,128]{3,2,1,0:T(8,128)(2,1)S(1)}, bf16[1,8,224,128]{3,2,1,0:T(8,128)(2,1)S(1)}, u32[]{:S(2)}, u32[]{:S(2)}) collective-permute-start(bf16[1,8,224,128]{3,2,1,0:T(8,128)(2,1)S(1)} %slice.8), channel_id=1, source_target_pairs={{0,1},{1,0},{2,3},{3,2},{4,5},{5,4},{6,7},{7,6},{8,9},{9,8},{10,11... | collective-permute-start | bytes 1376264 | tf_op jit(solution)/shard_map/ppermute | solution.py:651
  88.9 2.0 %collective-permute-start.10 = (bf16[1,8,224,128]{3,2,1,0:T(8,128)(2,1)S(1)}, bf16[1,8,224,128]{3,2,1,0:T(8,128)(2,1)S(1)}, u32[]{:S(2)}, u32[]{:S(2)}) collective-permute-start(bf16[1,8,224,128]{3,2,1,0:T(8,128)(2,1)S(1)} %slice.9), channel_id=1, source_target_pairs={{0,1},{1,0},{2,3},{3,2},{4,5},{5,4},{6,7},{7,6},{8,9},{9,8},{10,11... | collective-permute-start | bytes 1376264 | tf_op jit(solution)/shard_map/ppermute | solution.py:651
  89.5 1.4 copy-start.7
  89.6 1.3 copy-start.8
  90.9 0.8 copy-start.9
  102.5 4.5 %collective-permute-start.11 = (bf16[4,160,256]{2,1,0:T(8,128)(2,1)S(1)}, bf16[4,160,256]{2,1,0:T(8,128)(2,1)S(1)}, u32[]{:S(2)}, u32[]{:S(2)}) collective-permute-start(bf16[4,160,256]{2,1,0:T(8,128)(2,1)S(1)} %get-tuple-element.39), channel_id=1, source_target_pairs={{0,1},{1,0},{2,3},{3,2},{4,5},{5,4},{6,7},{7,6},{8,9},{9,8},{10,11... | collective-permute-start | bytes 983048 | tf_op jit(solution)/shard_map/ppermute | solution.py:594
  107.8 10.5 %all-to-all-start.4 = ((bf16[4,160,256]{2,1,0:T(8,128)(2,1)}), bf16[4,160,256]{2,1,0:T(8,128)(2,1)S(1)}, u32[]{:S(2)}, u32[]{:S(2)}) async-start(bf16[4,160,256]{2,1,0:T(8,128)(2,1)} %add_cores.1), calls=%async_computation.4 | async-start | bytes 655360 | tf_op jit(solution)/shard_map/all_to_all | solution.py:588
  125.8 3.4 %collective-permute-start.12 = (bf16[4,80,256]{2,1,0:T(8,128)(2,1)S(1)}, bf16[4,80,256]{2,1,0:T(8,128)(2,1)S(1)}, u32[]{:S(2)}, u32[]{:S(2)}) collective-permute-start(bf16[4,80,256]{2,1,0:T(8,128)(2,1)S(1)} %all_to_all.35.same_ref), channel_id=1, source_target_pairs={{0,1},{1,0},{2,3},{3,2},{4,5},{5,4},{6,7},{7,6},{8,9},{9,8},{10,11... | collective-permute-start | bytes 491528 | tf_op jit(solution)/shard_map/ppermute | solution.py:594

commit v6 on v5

--- a/solution.py
+++ b/solution.py
@@ -630,11 +630,15 @@
     y_rank = lax.axis_index("y").astype(i32).reshape(1)
     each = w_out.shape[0] // ring
     w_turned = w_out.transpose(0, 2, 1)
-    out_pieces = []
-    for k in range(1, ring):
-        piece = lax.dynamic_slice_in_dim(w_turned, (y_rank[0] + k) % ring * each, each, 0)
-        pairs = [(j, (j + k) % ring) for j in range(ring)]
-        out_pieces.append(lax.ppermute(piece, "y", pairs))
+    out_pieces = [
+        lax.dynamic_slice_in_dim(w_turned, (y_rank[0] + k) % ring * each, each, 0)
+        for k in range(1, ring)
+    ]
+    incoming, _ = lax.optimization_barrier((incoming, out_pieces))
+    out_pieces = [
+        lax.ppermute(piece, "y", [(j, (j + k) % ring) for j in range(ring)])
+        for k, piece in enumerate(out_pieces, 1)
+    ]
 
     ctx_lengths, _ = lax.optimization_barrier((ctx_lengths, arrays[0]))
     tokens = jnp.pad(step_latents.transpose(1, 0, 2), ((0, 0), (0, 16 - steps), (0, 0)))

time: 152 us -> 152 us (level)
    ppermute x9, waiting for transfers between devices: 9.97 us -> 14 us  [along_x(): lax.ppermute(piece, 'tp', [(j, partner(j, tp, k, sign)) for j in range(tp)])]
    all_to_all x5, waiting for transfers between devices: 20.2 us -> 16.3 us  [exchange(): lax.all_to_all(x, axis, split_axis=0, concat_axis=0, tiled=True, axis_ind...]
  transfers between devices with their start and end apart: 18 -> 18, of which waited for: 11 -> 12; matrix products, arithmetic and copies ran while one was open for 1% -> 1% of each run, Pallas kernels for 15% -> 15%
where the time goes in v6:
time: 152 us; the launch traced here: 151 us
  starting transfers between devices  55.9 us (37%)
  waiting for transfers between devices  33.9 us (22%)
  Pallas kernels  31.6 us (21%)
  blocking collectives  26.7 us (18%)
  local copies, waits for them, and re-layouts  2.97 us (2%)
    all_to_all x5, starting transfers between devices, exchange(): lax.all_to_all(x, axis, split_axis=0, concat_axis=0, tiled=True, axis_ind...  34.5 us
    all_to_all x2, blocking collectives, exchange(): lax.all_to_all(x, axis, split_axis=0, concat_axis=0, tiled=True, axis_ind...  26.7 us
    all_to_all x5, waiting for transfers between devices, exchange(): lax.all_to_all(x, axis, split_axis=0, concat_axis=0, tiled=True, axis_ind...  16.3 us
    ppermute x9, waiting for transfers between devices, along_x(): lax.ppermute(piece, 'tp', [(j, partner(j, tp, k, sign)) for j in range(tp)])  14 us
    ppermute x9, starting transfers between devices, along_x(): lax.ppermute(piece, 'tp', [(j, partner(j, tp, k, sign)) for j in range(tp)])  11.5 us
    ppermute x3, starting transfers between devices, swap_cores(): lax.ppermute(x, 'tp', [(j, j ^ 1) for j in range(lax.axis_size('tp'))])  8.63 us
    pallas_call x1, Pallas kernels, reshard(): call(functools.partial(reshard_kernel, tp, width), tuple((pltpu.HBM((size...  7.13 us
    pallas_call x1, Pallas kernels, attend_cache(): call(cache_kernel, (pltpu.HBM((per_owner, rows, LAT), f32), pltpu.HBM((pe...  5.99 us
  transfers between devices with their start and end apart: 18, of which 12 were waited for; matrix products, arithmetic and copies ran while one was open for 1% of the time, Pallas kernels for 15%

profile of v6, /device:TPU:1, one launch (start us, length us, event | category | flops | bytes accessed | tf_op | source)
XLA Modules:
  0.0 151.3 jit_solution(12040901850615271798)
XLA Ops:
  0.0 2.6 %route.1 = bf16[256,576]{1,0:T(8,128)(2,1)} custom-call(s32[1]{0:T(128)} %bitcast.rank_ref, s32[1,128]{1,0:T(1,128)} %bitcast.39, s32[4,32]{1,0:T(4,128)} %bitcast.38, bf16[576,512]{1,0:T(8,128)(2,1)} %bitcast.33), custom_call_target="tpu_custom_call" | custom-call | flops 150994944 | bytes 884736 | tf_op jit(solution)/shard_map/route/pallas_call | solution.py:107
  2.6 12.2 %all-to-all-start = ((bf16[32,8,576]{2,1,0:T(8,128)(2,1)}), bf16[32,8,576]{2,1,0:T(8,128)(2,1)S(1)}, u32[]{:S(2)}, u32[]{:S(2)}) async-start(bf16[32,8,576]{2,1,0:T(8,128)(2,1)} %bitcast.5), calls=%async_computation | async-start | bytes 655360 | tf_op jit(solution)/shard_map/all_to_all | solution.py:588
  14.8 0.0 copy-start.12
  14.8 0.0 copy-start.11
  14.8 0.0 copy-start.3
  14.8 0.0 copy-start.4
  14.8 7.1 %reshard.1 = (bf16[1,8,224,128]{3,2,1,0:T(8,128)(2,1)}, bf16[1,8,224,128]{3,2,1,0:T(8,128)(2,1)}, bf16[2,8,224,128]{3,2,1,0:T(8,128)(2,1)}, bf16[2,8,224,128]{3,...) custom-call(s32[1]{0:T(128)} %bitcast.rank_ref, f32[1,7168]{1,0:T(1,128)} %bitcast.36, ...), custom_call_target="tpu_custom_call" | custom-call | flops 792723456 | bytes 7225344 | tf_op jit(solution)/shard_map/reshard/pallas_call | solution.py:176
  22.0 1.3 collective-permute-start.1
  23.2 1.5 collective-permute-start.2
  24.7 0.8 dynamic-slice_bitcast_fusion
  25.5 1.9 %all-to-all-done = bf16[32,8,576]{2,1,0:T(8,128)(2,1)S(1)} async-done(((bf16[32,8,576]{2,1,0:T(8,128)(2,1)}), bf16[32,8,576]{2,1,0:T(8,128)(2,1)S(1)}, u32[]{:S(2)}, u32[]{:S(2)}) %all-to-all-start) | async-done | bytes 294944 | tf_op jit(solution)/shard_map/all_to_all | solution.py:588
  27.4 2.4 %collective-permute-start = (bf16[256,576]{1,0:T(8,128)(2,1)S(1)}, bf16[256,576]{1,0:T(8,128)(2,1)S(1)}, u32[]{:S(2)}, u32[]{:S(2)}) collective-permute-start(bf16[256,576]{1,0:T(8,128)(2,1)S(1)} %bitcast.26), channel_id=1, source_target_pairs={{0,1},{1,0},{2,3},{3,2},{4,5},{5,4},{6,7},{7,6},{8,9},{9,8},{10,11... | collective-permute-start | bytes 884744 | tf_op jit(solution)/shard_map/ppermute | solution.py:594
  29.7 0.0 copy-done.12
  29.7 0.2 dynamic-slice_reduce_fusion.len_ref
  30.0 0.0 copy-start
  30.0 6.0 %attend_cache.1 = (f32[4,32,512]{2,1,0:T(8,128)}, f32[4,32,128]{2,1,0:T(8,128)}) custom-call(s32[4]{0:T(128)S(1)} %copy-done.4, bf16[2,4,16,576]{3,2,1,0:T(8,128)(2,1)S(1)} %copy-done.3, bf16[4,576,1024]{2,1,0:T(8,128)(2,1)} %bitcast.29, bf16[4,16,576]{2,1,0:T(8,128)(2,1)S(1)} %pad.4.tok_ref), custom_call_target="tpu_custom_call" | custom-call | flops 285212672 | bytes 4718592 | tf_op jit(solution)/shard_map/attend_cache/pallas_call | solution.py:261
  36.0 0.0 collective-permute-done.other_ref
  36.0 3.0 %attend_new.1 = bf16[16,2,8,1024]{3,2,1,0:T(8,128)(2,1)} custom-call(s32[1]{0:T(128)} %bitcast.rank_ref, s32[4]{0:T(128)S(1)} %dynamic-slice_reduce_fusion.len_ref, bf16[2,4,16,576]{3,2,1,0:T(8,128)(2,1)S(1)} %copy-done.3, bf16[256,576]{1,0:T(8,128)(2,1)S(1)} %bitcast.27, bf16[256,576]{1,0:T(8,128)(2,1)S(1)} %collective-permute-done.other_ref, ...), custom_call_target="tpu_custom_call" | custom-call | flops 150994944 | bytes 2097152 | tf_op jit(solution)/shard_map/attend_new/pallas_call | solution.py:324
  39.0 6.9 %all-to-all-start.1 = ((bf16[32,8,1024]{2,1,0:T(8,128)(2,1)}), bf16[32,8,1024]{2,1,0:T(8,128)(2,1)S(1)}, u32[]{:S(2)}, u32[]{:S(2)}) async-start(bf16[32,8,1024]{2,1,0:T(8,128)(2,1)} %bitcast.13), calls=%async_computation.1 | async-start | bytes 1048576 | tf_op jit(solution)/shard_map/all_to_all | solution.py:588
  46.0 0.0 collective-permute-done.1.refs_2_
  46.0 0.0 collective-permute-done.2.refs_4_.refs_6_
  46.0 0.1 collective-permute-start.3
  46.1 2.7 %collective-permute-start.4 = (bf16[1,8,224,128]{3,2,1,0:T(8,128)(2,1)S(1)}, bf16[1,8,224,128]{3,2,1,0:T(8,128)(2,1)}, u32[]{:S(2)}, u32[]{:S(2)}) collective-permute-start(bf16[1,8,224,128]{3,2,1,0:T(8,128)(2,1)S(1)} %copy-done.13), channel_id=1, source_target_pairs={{0,6},{1,7},{2,0},{3,1},{4,2},{5,3},{6,4},{7,5},{8,14},{9,15},{10,... | collective-permute-start | bytes 1376264 | tf_op jit(solution)/shard_map/ppermute | solution.py:655
  48.8 1.2 collective-permute-start.5
  50.0 9.2 %collective-permute-done.3 = bf16[1,8,224,128]{3,2,1,0:T(8,128)(2,1)} collective-permute-done((bf16[1,8,224,128]{3,2,1,0:T(8,128)(2,1)S(1)}, bf16[1,8,224,128]{3,2,1,0:T(8,128)(2,1)}, u32[]{:S(2)}, u32[]{:S(2)}) %collective-permute-start.3) | collective-permute-done | bytes 458784 | tf_op jit(solution)/shard_map/ppermute | solution.py:655
  59.2 0.0 collective-permute-start.6
  59.2 0.0 collective-permute-done.4
  59.2 3.9 %collective-permute-start.7 = (bf16[1,8,224,128]{3,2,1,0:T(8,128)(2,1)}, bf16[1,8,224,128]{3,2,1,0:T(8,128)(2,1)S(1)}, u32[]{:S(2)}, u32[]{:S(2)}) collective-permute-start(bf16[1,8,224,128]{3,2,1,0:T(8,128)(2,1)} %collective-permute-done.4), channel_id=1, source_target_pairs={{0,7},{1,6},{2,1},{3,0},{4,3},{5,2},{6,5},{7,4},{8,15},{9,14},{10,... | collective-permute-start | bytes 1376264 | tf_op jit(solution)/shard_map/ppermute | solution.py:655
  63.2 1.1 own_heads.1.own_ref
  64.3 0.0 all-to-all-done.1
  64.3 1.3 collective-permute-done.5.refs_0_
  65.6 1.2 project.1
  66.8 4.1 %all-to-all-start.2 = ((bf16[16,32,256]{2,1,0:T(8,128)(2,1)}), bf16[16,32,256]{2,1,0:T(8,128)(2,1)S(1)}, u32[]{:S(2)}, u32[]{:S(2)}) async-start(bf16[16,32,256]{2,1,0:T(8,128)(2,1)} %bitcast.16), calls=%async_computation.2 | async-start | bytes 524288 | tf_op jit(solution)/shard_map/all_to_all | solution.py:588
  70.9 0.3 turn_hidden.1.hidden_ref
  71.2 0.4 collective-permute-done.6.refs_0_.refs_4_
  71.6 2.9 %collective-permute-done.7.refs_1_.refs_5_ = bf16[1,8,224,128]{3,2,1,0:T(8,128)(2,1)S(1)} collective-permute-done((bf16[1,8,224,128]{3,2,1,0:T(8,128)(2,1)}, bf16[1,8,224,128]{3,2,1,0:T(8,128)(2,1)S(1)}, u32[]{:S(2)}, u32[]{:S(2)}) %collective-permute-start.7) | collective-permute-done | bytes 458784 | tf_op jit(solution)/shard_map/ppermute | solution.py:655
  74.5 3.6 %all-to-all-done.2.part_ref = bf16[16,32,256]{2,1,0:T(8,128)(2,1)S(1)} async-done(((bf16[16,32,256]{2,1,0:T(8,128)(2,1)}), bf16[16,32,256]{2,1,0:T(8,128)(2,1)S(1)}, u32[]{:S(2)}, u32[]{:S(2)}) %all-to-all-start.2) | async-done | bytes 262176 | tf_op jit(solution)/shard_map/all_to_all | solution.py:588
  78.1 0.8 make_mixed.1
  79.0 7.8 %all-to-all-start.3 = ((bf16[32,56,128]{2,1,0:T(8,128)(2,1)}), bf16[32,56,128]{2,1,0:T(8,128)(2,1)}, u32[]{:S(2)}, u32[]{:S(2)}) async-start(bf16[32,56,128]{2,1,0:T(8,128)(2,1)} %get-tuple-element.38), calls=%async_computation.3 | async-start | bytes 917504 | tf_op jit(solution)/shard_map/all_to_all | solution.py:588
  86.7 1.2 collective-permute-start.8
  88.0 0.3 collective-permute-start.9
  88.3 1.0 slice.9
  89.3 0.6 collective-permute-start.10
  89.9 0.0 collective-permute-done.8.refs_1_
  89.9 0.2 collective-permute-done.9.refs_3_
  90.1 1.3 collective-permute-done.10.refs_5_.refs_7_
  91.3 0.8 copy-done.9
  92.1 1.9 %collect.2.refs_0_ = bf16[6,144,1024]{2,1,0:T(8,128)(2,1)S(1)} custom-call(bf16[1,8,224,128]{3,2,1,0:T(8,128)(2,1)} %get-tuple-element.26.refs_0_, bf16[1,8,224,128]{3,2,1,0:T(8,128)(2,1)} %copy-done.7, bf16[2,8,224,128]{3,2,1,0:T(8,128)(2,1)} %copy-done.5, bf16[1,8,224,128]{3,2,1,0:T(8,128)(2,1)} %copy-done.8, ...), custom_call_target="tpu_custom_call" | custom-call | bytes 3538944 | tf_op jit(solution)/shard_map/collect/pallas_call | solution.py:467
  94.0 0.2 collect.3.refs_1_
  94.2 6.9 %all-to-all-done.3.x_ref = bf16[32,56,128]{2,1,0:T(8,128)(2,1)} async-done(((bf16[32,56,128]{2,1,0:T(8,128)(2,1)}), bf16[32,56,128]{2,1,0:T(8,128)(2,1)}, u32[]{:S(2)}, u32[]{:S(2)}) %all-to-all-start.3) | async-done | bytes 458784 | tf_op jit(solution)/shard_map/all_to_all | solution.py:588
  101.1 1.8 %gate_up.1 = (bf16[4,160,256]{2,1,0:T(8,128)(2,1)S(1)}, bf16[4,160,256]{2,1,0:T(8,128)(2,1)S(1)}) custom-call(s32[1]{0:T(128)} %bitcast.rank_ref, bf16[32,56,128]{2,1,0:T(8,128)(2,1)} %all-to-all-done.3.x_ref, bf16[6,144,1024]{2,1,0:T(8,128)(2,1)S(1)} %collect.2.refs_0_, bf16[2,144,1024]{2,1,0:T(8,128)(2,1)S(1)} %collect.3.refs_1_), custom_call_target="tpu_custom_call" | custom-call | flops 603979776 | bytes 2818048 | tf_op jit(solution)/shard_map/gate_up/pallas_call | solution.py:487
  102.9 3.3 %collective-permute-start.11 = (bf16[4,160,256]{2,1,0:T(8,128)(2,1)S(1)}, bf16[4,160,256]{2,1,0:T(8,128)(2,1)S(1)}, u32[]{:S(2)}, u32[]{:S(2)}) collective-permute-start(bf16[4,160,256]{2,1,0:T(8,128)(2,1)S(1)} %get-tuple-element.41), channel_id=1, source_target_pairs={{0,1},{1,0},{2,3},{3,2},{4,5},{5,4},{6,7},{7,6},{8,9},{9,8},{10,11... | collective-permute-start | bytes 983048 | tf_op jit(solution)/shard_map/ppermute | solution.py:594
  106.2 1.3 collective-permute-done.11.b_ref
  107.5 0.8 add_cores.1
  108.3 3.6 %all-to-all-start.4 = ((bf16[4,160,256]{2,1,0:T(8,128)(2,1)}), bf16[4,160,256]{2,1,0:T(8,128)(2,1)S(1)}, u32[]{:S(2)}, u32[]{:S(2)}) async-start(bf16[4,160,256]{2,1,0:T(8,128)(2,1)} %add_cores.1), calls=%async_computation.4 | async-start | bytes 655360 | tf_op jit(solution)/shard_map/all_to_all | solution.py:588
  111.9 2.5 %turn.1.w_ref = bf16[1024,640]{1,0:T(8,128)(2,1)S(1)} custom-call(bf16[1,8,224,128]{3,2,1,0:T(8,128)(2,1)} %get-tuple-element.26.refs_0_, bf16[1,8,224,128]{3,2,1,0:T(8,128)(2,1)} %copy-done.7, bf16[2,8,224,128]{3,2,1,0:T(8,128)(2,1)} %copy-done.5, bf16[1,8,224,128]{3,2,1,0:T(8,128)(2,1)} %copy-done.8, bf16[1,8,224,128]{3,2,1,0:T(8,128)(2,1)} %copy-done.1, ...), custom_call_target="tpu_custom_call" | custom-call | flops 167772160 | bytes 2621440 | tf_op jit(solution)/shard_map/turn/pallas_call | solution.py:213
  114.5 4.0 %all-to-all-done.4.part_ref = bf16[4,160,256]{2,1,0:T(8,128)(2,1)S(1)} async-done(((bf16[4,160,256]{2,1,0:T(8,128)(2,1)}), bf16[4,160,256]{2,1,0:T(8,128)(2,1)S(1)}, u32[]{:S(2)}, u32[]{:S(2)}) %all-to-all-start.4) | async-done | bytes 327712 | tf_op jit(solution)/shard_map/all_to_all | solution.py:588
  118.4 0.1 activate.1
  118.5 7.4 %all_to_all.35.same_ref = bf16[4,80,256]{2,1,0:T(8,128)(2,1)S(1)} all-to-all(bf16[4,80,256]{2,1,0:T(8,128)(2,1)S(1)} %activate.1), channel_id=1, replica_groups={{0,2,4,6},{1,3,5,7},{8,10,12,14},{9,11,13,15},{16,18,20,22},{17,19,21,2..., dimensions={0} | all-to-all | bytes 327680 | tf_op jit(solution)/shard_map/all_to_all | solution.py:588
  125.9 3.0 %collective-permute-start.12 = (bf16[4,80,256]{2,1,0:T(8,128)(2,1)S(1)}, bf16[4,80,256]{2,1,0:T(8,128)(2,1)S(1)}, u32[]{:S(2)}, u32[]{:S(2)}) collective-permute-start(bf16[4,80,256]{2,1,0:T(8,128)(2,1)S(1)} %all_to_all.35.same_ref), channel_id=1, source_target_pairs={{0,1},{1,0},{2,3},{3,2},{4,5},{5,4},{6,7},{7,6},{8,9},{9,8},{10,11... | collective-permute-start | bytes 491528 | tf_op jit(solution)/shard_map/ppermute | solution.py:594
  128.8 1.0 collective-permute-done.12.other_ref
  129.9 1.2 down.1
  131.1 19.4 %all_to_all.36.part_ref = bf16[32,56,128]{2,1,0:T(8,128)(2,1)S(1)} all-to-all(bf16[32,56,128]{2,1,0:T(8,128)(2,1)S(1)} %down.1), channel_id=1, replica_groups=mesh['z'=16,'y'=2,'tp'=8] {'z','y'}, dimensions={0} | all-to-all | bytes 917504 | tf_op jit(solution)/shard_map/all_to_all | solution.py:588
  150.4 0.9 finish.1
  (28 shorter events, 0.1 us)
Async XLA Ops:
  2.6 22.1 %copy-start.6 = (bf16[16,128,224]{1,2,0:T(8,128)(2,1)S(1)}, bf16[16,128,224]{1,2,0:T(8,128)(2,1)}, u32[]{:S(2)}) copy-start(bf16[16,128,224]{1,2,0:T(8,128)(2,1)} %param.22) | copy-start | bytes 2752516
  2.6 24.7 %all-to-all-start = ((bf16[32,8,576]{2,1,0:T(8,128)(2,1)}), bf16[32,8,576]{2,1,0:T(8,128)(2,1)S(1)}, u32[]{:S(2)}, u32[]{:S(2)}) async-start(bf16[32,8,576]{2,1,0:T(8,128)(2,1)} %bitcast.5), calls=%async_computation | async-start | bytes 655360 | tf_op jit(solution)/shard_map/all_to_all | solution.py:588
  14.8 14.9 %copy-start.12 = (s32[32,4]{0,1:T(4,128)S(1)}, s32[32,4]{0,1:T(4,128)}, u32[]{:S(2)}) copy-start(s32[32,4]{0,1:T(4,128)} %param.16) | copy-start | bytes 1540
  14.8 15.1 %copy-start.11 = (bf16[2,4,576]{2,1,0:T(4,128)(2,1)S(1)}, bf16[2,4,576]{2,1,0:T(4,128)(2,1)}, u32[]{:S(2)}) copy-start(bf16[2,4,576]{2,1,0:T(4,128)(2,1)} %param.20) | copy-start | bytes 27652
  14.8 15.2 %copy-start.3 = (bf16[2,4,16,576]{3,2,1,0:T(8,128)(2,1)S(1)}, bf16[2,4,16,576]{3,2,1,0:T(8,128)(2,1)}, u32[]{:S(2)}) copy-start(bf16[2,4,16,576]{3,2,1,0:T(8,128)(2,1)} %q_ref.3) | copy-start | bytes 442372
  14.8 15.1 %copy-start.4 = (s32[4]{0:T(128)S(1)}, s32[4]{0:T(128)}, u32[]{:S(2)}) copy-start(s32[4]{0:T(128)} %ctx_ref) | copy-start | bytes 52
  22.0 24.0 %collective-permute-start.1 = (bf16[2,8,224,128]{3,2,1,0:T(8,128)(2,1)}, bf16[2,8,224,128]{3,2,1,0:T(8,128)(2,1)S(1)}, u32[]{:S(2)}, u32[]{:S(2)}) collective-permute-start(bf16[2,8,224,128]{3,2,1,0:T(8,128)(2,1)} %get-tuple-element.30), channel_id=1, source_target_pairs={{0,2},{1,3},{2,4},{3,5},{4,6},{5,7},{6,0},{7,1},{8,10},{9,11},{10,... | collective-permute-start | bytes 2752520 | tf_op jit(solution)/shard_map/ppermute | solution.py:655
  23.2 22.7 %collective-permute-start.2 = (bf16[2,8,224,128]{3,2,1,0:T(8,128)(2,1)}, bf16[2,8,224,128]{3,2,1,0:T(8,128)(2,1)}, u32[]{:S(2)}, u32[]{:S(2)}) collective-permute-start(bf16[2,8,224,128]{3,2,1,0:T(8,128)(2,1)} %get-tuple-element.31), channel_id=1, source_target_pairs={{0,6},{1,7},{2,0},{3,1},{4,2},{5,3},{6,4},{7,5},{8,14},{9,15},{10,... | collective-permute-start | bytes 2752520 | tf_op jit(solution)/shard_map/ppermute | solution.py:655
  27.4 8.6 %collective-permute-start = (bf16[256,576]{1,0:T(8,128)(2,1)S(1)}, bf16[256,576]{1,0:T(8,128)(2,1)S(1)}, u32[]{:S(2)}, u32[]{:S(2)}) collective-permute-start(bf16[256,576]{1,0:T(8,128)(2,1)S(1)} %bitcast.26), channel_id=1, source_target_pairs={{0,1},{1,0},{2,3},{3,2},{4,5},{5,4},{6,7},{7,6},{8,9},{9,8},{10,11... | collective-permute-start | bytes 884744 | tf_op jit(solution)/shard_map/ppermute | solution.py:594
  30.0 6.0 %copy-start = (bf16[16,512,128]{2,1,0:T(8,128)(2,1)S(1)}, bf16[16,512,128]{2,1,0:T(8,128)(2,1)}, u32[]{:S(2)}) copy-start(bf16[16,512,128]{2,1,0:T(8,128)(2,1)} %uv_ref.1) | copy-start | bytes 6291460
  36.0 10.0 %copy-start.14 = (bf16[1,8,224,128]{3,2,1,0:T(8,128)(2,1)S(1)}, bf16[1,8,224,128]{3,2,1,0:T(8,128)(2,1)}, u32[]{:S(2)}) copy-start(bf16[1,8,224,128]{3,2,1,0:T(8,128)(2,1)} %get-tuple-element.34) | copy-start | bytes 1376260
  36.0 10.1 %copy-start.13 = (bf16[1,8,224,128]{3,2,1,0:T(8,128)(2,1)S(1)}, bf16[1,8,224,128]{3,2,1,0:T(8,128)(2,1)}, u32[]{:S(2)}) copy-start(bf16[1,8,224,128]{3,2,1,0:T(8,128)(2,1)} %get-tuple-element.35) | copy-start | bytes 1376260
  39.0 31.8 %copy-start.10 = (bf16[2,128,28]{1,0,2:T(2,128)(2,1)S(1)}, bf16[2,128,28]{1,0,2:T(2,128)(2,1)}, u32[]{:S(2)}) copy-start(bf16[2,128,28]{1,0,2:T(2,128)(2,1)} %param.23) | copy-start | bytes 43012
  39.0 25.3 %all-to-all-start.1 = ((bf16[32,8,1024]{2,1,0:T(8,128)(2,1)}), bf16[32,8,1024]{2,1,0:T(8,128)(2,1)S(1)}, u32[]{:S(2)}, u32[]{:S(2)}) async-start(bf16[32,8,1024]{2,1,0:T(8,128)(2,1)} %bitcast.13), calls=%async_computation.1 | async-start | bytes 1048576 | tf_op jit(solution)/shard_map/all_to_all | solution.py:588
  46.0 42.0 %copy-start.5 = (bf16[2,8,224,128]{3,2,1,0:T(8,128)(2,1)}, bf16[2,8,224,128]{3,2,1,0:T(8,128)(2,1)S(1)}, u32[]{:S(2)}) copy-start(bf16[2,8,224,128]{3,2,1,0:T(8,128)(2,1)S(1)} %collective-permute-done.1.refs_2_) | copy-start | bytes 2752516
  46.0 13.2 %collective-permute-start.3 = (bf16[1,8,224,128]{3,2,1,0:T(8,128)(2,1)S(1)}, bf16[1,8,224,128]{3,2,1,0:T(8,128)(2,1)}, u32[]{:S(2)}, u32[]{:S(2)}) collective-permute-start(bf16[1,8,224,128]{3,2,1,0:T(8,128)(2,1)S(1)} %copy-done.14), channel_id=1, source_target_pairs={{0,2},{1,3},{2,4},{3,5},{4,6},{5,7},{6,0},{7,1},{8,10},{9,11},{10,... | collective-permute-start | bytes 1376264 | tf_op jit(solution)/shard_map/ppermute | solution.py:655
  46.1 13.1 %collective-permute-start.4 = (bf16[1,8,224,128]{3,2,1,0:T(8,128)(2,1)S(1)}, bf16[1,8,224,128]{3,2,1,0:T(8,128)(2,1)}, u32[]{:S(2)}, u32[]{:S(2)}) collective-permute-start(bf16[1,8,224,128]{3,2,1,0:T(8,128)(2,1)S(1)} %copy-done.13), channel_id=1, source_target_pairs={{0,6},{1,7},{2,0},{3,1},{4,2},{5,3},{6,4},{7,5},{8,14},{9,15},{10,... | collective-permute-start | bytes 1376264 | tf_op jit(solution)/shard_map/ppermute | solution.py:655
  48.8 16.8 %collective-permute-start.5 = (bf16[8,224,128]{2,1,0:T(8,128)(2,1)}, bf16[8,224,128]{2,1,0:T(8,128)(2,1)S(1)}, u32[]{:S(2)}, u32[]{:S(2)}) collective-permute-start(bf16[8,224,128]{2,1,0:T(8,128)(2,1)} %dynamic-slice_bitcast_fusion), channel_id=1, source_target_pairs={{0,8},{8,0},{1,9},{9,1},{2,10},{10,2},{3,11},{11,3},{4,12},{12,4},... | collective-permute-start | bytes 1376264 | tf_op jit(solution)/shard_map/ppermute | solution.py:639
  59.2 12.3 %collective-permute-start.6 = (bf16[1,8,224,128]{3,2,1,0:T(8,128)(2,1)}, bf16[1,8,224,128]{3,2,1,0:T(8,128)(2,1)S(1)}, u32[]{:S(2)}, u32[]{:S(2)}) collective-permute-start(bf16[1,8,224,128]{3,2,1,0:T(8,128)(2,1)} %collective-permute-done.3), channel_id=1, source_target_pairs={{0,2},{1,3},{2,4},{3,5},{4,6},{5,7},{6,0},{7,1},{8,10},{9,11},{10,... | collective-permute-start | bytes 1376264 | tf_op jit(solution)/shard_map/ppermute | solution.py:655
  59.2 15.3 %collective-permute-start.7 = (bf16[1,8,224,128]{3,2,1,0:T(8,128)(2,1)}, bf16[1,8,224,128]{3,2,1,0:T(8,128)(2,1)S(1)}, u32[]{:S(2)}, u32[]{:S(2)}) collective-permute-start(bf16[1,8,224,128]{3,2,1,0:T(8,128)(2,1)} %collective-permute-done.4), channel_id=1, source_target_pairs={{0,7},{1,6},{2,1},{3,0},{4,3},{5,2},{6,5},{7,4},{8,15},{9,14},{10,... | collective-permute-start | bytes 1376264 | tf_op jit(solution)/shard_map/ppermute | solution.py:655
  66.8 11.3 %all-to-all-start.2 = ((bf16[16,32,256]{2,1,0:T(8,128)(2,1)}), bf16[16,32,256]{2,1,0:T(8,128)(2,1)S(1)}, u32[]{:S(2)}, u32[]{:S(2)}) async-start(bf16[16,32,256]{2,1,0:T(8,128)(2,1)} %bitcast.16), calls=%async_computation.2 | async-start | bytes 524288 | tf_op jit(solution)/shard_map/all_to_all | solution.py:588
  71.6 22.5 %copy-start.1 = (bf16[1,8,224,128]{3,2,1,0:T(8,128)(2,1)}, bf16[1,8,224,128]{3,2,1,0:T(8,128)(2,1)S(1)}, u32[]{:S(2)}) copy-start(bf16[1,8,224,128]{3,2,1,0:T(8,128)(2,1)S(1)} %collective-permute-done.6.refs_0_.refs_4_) | copy-start | bytes 1376260
  74.5 19.5 %copy-start.2 = (bf16[1,8,224,128]{3,2,1,0:T(8,128)(2,1)}, bf16[1,8,224,128]{3,2,1,0:T(8,128)(2,1)S(1)}, u32[]{:S(2)}) copy-start(bf16[1,8,224,128]{3,2,1,0:T(8,128)(2,1)S(1)} %collective-permute-done.7.refs_1_.refs_5_) | copy-start | bytes 1376260
  79.0 22.1 %all-to-all-start.3 = ((bf16[32,56,128]{2,1,0:T(8,128)(2,1)}), bf16[32,56,128]{2,1,0:T(8,128)(2,1)}, u32[]{:S(2)}, u32[]{:S(2)}) async-start(bf16[32,56,128]{2,1,0:T(8,128)(2,1)} %get-tuple-element.38), calls=%async_computation.3 | async-start | bytes 917504 | tf_op jit(solution)/shard_map/all_to_all | solution.py:588
  86.7 3.1 %collective-permute-start.8 = (bf16[1,8,224,128]{3,2,1,0:T(8,128)(2,1)}, bf16[1,8,224,128]{3,2,1,0:T(8,128)(2,1)S(1)}, u32[]{:S(2)}, u32[]{:S(2)}) collective-permute-start(bf16[1,8,224,128]{3,2,1,0:T(8,128)(2,1)} %get-tuple-element.39), channel_id=1, source_target_pairs={{0,1},{1,0},{2,3},{3,2},{4,5},{5,4},{6,7},{7,6},{8,9},{9,8},{10,11... | collective-permute-start | bytes 1376264 | tf_op jit(solution)/shard_map/ppermute | solution.py:655
  88.0 2.1 %collective-permute-start.9 = (bf16[1,8,224,128]{3,2,1,0:T(8,128)(2,1)S(1)}, bf16[1,8,224,128]{3,2,1,0:T(8,128)(2,1)S(1)}, u32[]{:S(2)}, u32[]{:S(2)}) collective-permute-start(bf16[1,8,224,128]{3,2,1,0:T(8,128)(2,1)S(1)} %slice.8), channel_id=1, source_target_pairs={{0,1},{1,0},{2,3},{3,2},{4,5},{5,4},{6,7},{7,6},{8,9},{9,8},{10,11... | collective-permute-start | bytes 1376264 | tf_op jit(solution)/shard_map/ppermute | solution.py:655
  89.3 2.0 %collective-permute-start.10 = (bf16[1,8,224,128]{3,2,1,0:T(8,128)(2,1)S(1)}, bf16[1,8,224,128]{3,2,1,0:T(8,128)(2,1)S(1)}, u32[]{:S(2)}, u32[]{:S(2)}) collective-permute-start(bf16[1,8,224,128]{3,2,1,0:T(8,128)(2,1)S(1)} %slice.9), channel_id=1, source_target_pairs={{0,1},{1,0},{2,3},{3,2},{4,5},{5,4},{6,7},{7,6},{8,9},{9,8},{10,11... | collective-permute-start | bytes 1376264 | tf_op jit(solution)/shard_map/ppermute | solution.py:655
  89.9 1.4 copy-start.7
  90.1 1.3 copy-start.8
  91.3 0.8 copy-start.9
  102.9 4.5 %collective-permute-start.11 = (bf16[4,160,256]{2,1,0:T(8,128)(2,1)S(1)}, bf16[4,160,256]{2,1,0:T(8,128)(2,1)S(1)}, u32[]{:S(2)}, u32[]{:S(2)}) collective-permute-start(bf16[4,160,256]{2,1,0:T(8,128)(2,1)S(1)} %get-tuple-element.41), channel_id=1, source_target_pairs={{0,1},{1,0},{2,3},{3,2},{4,5},{5,4},{6,7},{7,6},{8,9},{9,8},{10,11... | collective-permute-start | bytes 983048 | tf_op jit(solution)/shard_map/ppermute | solution.py:594
  108.3 10.1 %all-to-all-start.4 = ((bf16[4,160,256]{2,1,0:T(8,128)(2,1)}), bf16[4,160,256]{2,1,0:T(8,128)(2,1)S(1)}, u32[]{:S(2)}, u32[]{:S(2)}) async-start(bf16[4,160,256]{2,1,0:T(8,128)(2,1)} %add_cores.1), calls=%async_computation.4 | async-start | bytes 655360 | tf_op jit(solution)/shard_map/all_to_all | solution.py:588
  125.9 4.0 %collective-permute-start.12 = (bf16[4,80,256]{2,1,0:T(8,128)(2,1)S(1)}, bf16[4,80,256]{2,1,0:T(8,128)(2,1)S(1)}, u32[]{:S(2)}, u32[]{:S(2)}) collective-permute-start(bf16[4,80,256]{2,1,0:T(8,128)(2,1)S(1)} %all_to_all.35.same_ref), channel_id=1, source_target_pairs={{0,1},{1,0},{2,3},{3,2},{4,5},{5,4},{6,7},{7,6},{8,9},{9,8},{10,11... | collective-permute-start | bytes 491528 | tf_op jit(solution)/shard_map/ppermute | solution.py:594
